TPU v7x, 512 devices: a whole 4x4x16 slice. The times are simulated.
512 devices in a mesh: dp: 8 (over y, core), expert: 64 (over z, x).
Axes of the slice: x: 4, y: 4, z: 16, core: 2. Of those that a mesh axis runs over, the one named last changes fastest.
Arguments:
- tokens: bfloat16 [65536, 2048], P(('dp', 'expert')), may hold values from -6 to 6
- hidden_grad: bfloat16 [65536, 1536], P(('dp', 'expert')), may hold values from -6 to 6
- gate_weight: bfloat16 [64, 1536, 2048], P('expert', 'dp'), may hold values from -0.125 to 0.125
- up_weight: bfloat16 [64, 1536, 2048], P('expert', 'dp'), may hold values from -0.125 to 0.125
- replica_offset: int32 [64], P('expert'), may hold values from 1 to 2, as said below
- block_expert: int32 [1024], P(('dp', 'expert')), may hold values from 0 to 63, as said below
- block_rows: int32 [1024], P(('dp', 'expert')), may hold values from 16 to 64, as said below
Outputs:
- input_grad: bfloat16 [65536, 2048], P(('dp', 'expert'))
- gate_grad: bfloat16 [64, 1536, 2048], P('expert', 'dp')
- up_grad: bfloat16 [64, 1536, 2048], P('expert', 'dp')
Inputs may be any that keep to these rules, and one draw needn't show every extreme that they name: Host h holds a copy of expert (h - replica_offset[h]) mod 64. `block_expert`: each block's expert is either its host's own expert (the host's index on the expert axis) or the expert that the host holds a copy of. `block_rows`: every device has at least one block with all 64 rows live.
All inputs are finite; a program needn't handle non-finite values.
Results may differ from a plain program's by a relative error of at most 0.017.
Values may be sent and summed in bfloat16 or wider, within the bound.
No kernel may reach another device: no remote copies, remote signals or barrier semaphores. Data moves between devices by JAX's collectives and lax.ppermute only.
A program may use at most 64 MiB of HBM per device.

v0:
```python
import jax
import jax.numpy as jnp
from jax import lax
from jax.sharding import PartitionSpec as P

REACH = 2


def from_behind(value, axis, steps):
    count = lax.axis_size(axis)
    pairs = [(source, (source + steps) % count) for source in range(count)]
    return lax.ppermute(value, axis, pairs)


def return_partials(copy_part, offset):
    summed = jnp.zeros(copy_part.shape, jnp.float32)
    for hop_index in range(1, REACH + 1):
        masked_part = jnp.where(offset == hop_index, copy_part, jnp.zeros_like(copy_part))
        incoming = from_behind(masked_part, "expert", -hop_index)
        summed = summed + incoming.astype(jnp.float32)
    return summed


def local(tokens, hidden_grad, gate_weight, up_weight, replica_offset, block_expert, block_rows):
    home_id = lax.axis_index("expert")
    gathered, experts, lengths = (
        lax.all_gather(tokens, "dp", axis=0, tiled=True),
        lax.all_gather(block_expert, "dp", axis=0, tiled=True),
        lax.all_gather(block_rows, "dp", axis=0, tiled=True),
    )
    cotangents = lax.all_to_all(hidden_grad, "dp", split_axis=1, concat_axis=0, tiled=True)
    shard_width = gate_weight.shape[1]
    model_width = gate_weight.shape[2]
    w_home = jnp.concatenate([gate_weight[0], up_weight[0]], axis=0)
    offset = replica_offset[0]
    w_copy = jnp.zeros_like(w_home)
    for hop_index in range(1, REACH + 1):
        fetched = from_behind((gate_weight[0], up_weight[0]), "expert", hop_index)
        w_copy = jnp.where(offset == hop_index, jnp.concatenate(fetched, axis=0), w_copy)
    nblocks = experts.shape[0]
    block_len = gathered.shape[0] // nblocks
    x_blocks = gathered.reshape(nblocks, block_len, model_width)
    dh_blocks = cotangents.reshape(nblocks, block_len, shard_width)
    along_width = (((1,), (1,)), ((), ()))

    def one_block(block_item):
        x_blk, dh_blk, e_blk, n_blk = block_item
        weights = jnp.where(e_blk == home_id, w_home, w_copy)
        projected = lax.dot_general(x_blk, weights, along_width, preferred_element_type=jnp.float32)
        gate_val = projected[:, :shard_width]
        up_val = projected[:, shard_width:]
        sig_val = jax.nn.sigmoid(gate_val)
        live_rows = (jnp.arange(block_len, dtype=jnp.int32) < n_blk).astype(jnp.float32)
        cotan = dh_blk.astype(jnp.float32) * live_rows[:, None]
        dgate = cotan * up_val * sig_val * (1.0 + gate_val * (1.0 - sig_val))
        dup = cotan * gate_val * sig_val
        dgu = jnp.concatenate([dgate, dup], axis=1).astype(jnp.bfloat16)
        partial_dx = jnp.dot(dgu, weights, preferred_element_type=jnp.float32)
        return (dgu, partial_dx.astype(jnp.bfloat16))

    dgu_all, partials = lax.map(one_block, (x_blocks, dh_blocks, experts, lengths))
    rounded = lax.optimization_barrier(partials.reshape(-1, model_width))
    input_grad = lax.psum_scatter(
        rounded.astype(jnp.float32).astype(jnp.bfloat16), "dp", scatter_dimension=0, tiled=True
    )
    flat_terms = dgu_all.reshape(-1, 2 * shard_width)
    on_home = jnp.repeat(experts == home_id, block_len)[:, None]
    zeros_bf = jnp.zeros_like(flat_terms)
    home_terms = jnp.where(on_home, flat_terms, zeros_bf)
    copy_terms = jnp.where(on_home, zeros_bf, flat_terms)
    contract = (((0,), (0,)), ((), ()))
    both_parts = lax.dot_general(
        jnp.concatenate([home_terms, copy_terms], axis=1),
        gathered,
        contract,
        preferred_element_type=jnp.float32,
    )
    copy_part = both_parts[2 * shard_width :].astype(jnp.bfloat16)
    summed = both_parts[: 2 * shard_width] + return_partials(copy_part, offset)
    gate_grad = summed[:shard_width].astype(jnp.bfloat16)[None]
    up_grad = summed[shard_width:].astype(jnp.bfloat16)[None]
    return (input_grad, gate_grad, up_grad)


def solution(mesh):
    placed = (
        P(("dp", "expert"), None),
        P(("dp", "expert"), None),
        P("expert", "dp", None),
        P("expert", "dp", None),
        P("expert"),
        P(("dp", "expert")),
        P(("dp", "expert")),
    )
    return jax.shard_map(
        local,
        mesh=mesh,
        in_specs=placed,
        out_specs=(P(("dp", "expert"), None), P("expert", "dp", None), P("expert", "dp", None)),
        check_vma=False,
    )
```

profile of v0, /device:TPU:28, one launch (start us, length us, event | category | flops | bytes accessed | tf_op | source)
XLA Modules:
  0.0 322.5 jit_solution(12334415862563654267)
XLA Ops:
  7.9 3.8 %collective-permute-start = (bf16[192,2048]{1,0:T(8,128)(2,1)}, bf16[192,2048]{1,0:T(8,128)(2,1)S(1)}, u32[]{:S(2)}, u32[]{:S(2)}) collective-permute-start(bf16[192,2048]{1,0:T(8,128)(2,1)} %bitcast.52), channel_id=1, source_target_pairs={{0,2},{1,3},{2,4},{3,5},{4,6},{5,7},{6,8},{7,9},{8,10},{9,11},{10,... | collective-permute-start | bytes 2359304 | tf_op jit(solution)/shard_map/ppermute | solution.py:12
  11.7 4.9 %collective-permute-start.1 = (bf16[192,2048]{1,0:T(8,128)(2,1)}, bf16[192,2048]{1,0:T(8,128)(2,1)S(1)}, u32[]{:S(2)}, u32[]{:S(2)}) collective-permute-start(bf16[192,2048]{1,0:T(8,128)(2,1)} %bitcast.55), channel_id=1, source_target_pairs={{0,2},{1,3},{2,4},{3,5},{4,6},{5,7},{6,8},{7,9},{8,10},{9,11},{10,... | collective-permute-start | bytes 2359304 | tf_op jit(solution)/shard_map/ppermute | solution.py:12
  16.6 3.1 collective-permute-start.2
  19.8 3.7 %collective-permute-start.3 = (bf16[192,2048]{1,0:T(8,128)(2,1)}, bf16[192,2048]{1,0:T(8,128)(2,1)}, u32[]{:S(2)}, u32[]{:S(2)}) collective-permute-start(bf16[192,2048]{1,0:T(8,128)(2,1)} %bitcast.56), channel_id=1, source_target_pairs={{0,1},{1,2},{2,3},{3,4},{4,5},{5,6},{6,7},{7,8},{8,9},{9,10},{10,1... | collective-permute-start | bytes 2359304 | tf_op jit(solution)/shard_map/ppermute | solution.py:12
  23.5 1.9 copy.12
  25.4 4.7 %all-to-all-start = ((bf16[128,8,192]{0,2,1:T(8,128)(2,1)}), bf16[128,8,192]{0,2,1:T(8,128)(2,1)S(1)}, u32[]{:S(2)}, u32[]{:S(2)}) async-start(bf16[128,8,192]{0,2,1:T(8,128)(2,1)} %bitcast.7), calls=%async_computation | async-start | bytes 786432 | tf_op jit(solution)/shard_map/all_to_all | solution.py:31
  33.2 8.5 %all-reduce.2 = (s32[16]{0:T(128)S(1)}, s32[16]{0:T(128)S(1)}) all-reduce(s32[16]{0:T(128)S(1)} %dynamic-update-slice, s32[16]{0:T(128)S(1)} %dynamic-update-slice.1), channel_id=1, replica_groups=mesh['dp'=8,'expert'=64] {'dp'}, use_global_device_ids=true, to_apply=%add | all-reduce | flops 32 | bytes 256
  44.2 4.6 %collective-permute-done.1 = bf16[192,2048]{1,0:T(8,128)(2,1)S(1)} collective-permute-done((bf16[192,2048]{1,0:T(8,128)(2,1)}, bf16[192,2048]{1,0:T(8,128)(2,1)S(1)}, u32[]{:S(2)}, u32[]{:S(2)}) %collective-permute-start.1) | collective-permute-done | bytes 786464 | tf_op jit(solution)/shard_map/ppermute | solution.py:12
  48.9 21.1 %collective-permute-done.2 = bf16[192,2048]{1,0:T(8,128)(2,1)} collective-permute-done((bf16[192,2048]{1,0:T(8,128)(2,1)}, bf16[192,2048]{1,0:T(8,128)(2,1)}, u32[]{:S(2)}, u32[]{:S(2)}) %collective-permute-start.2) | collective-permute-done | bytes 786464 | tf_op jit(solution)/shard_map/ppermute | solution.py:12
  70.0 16.8 %collective-permute-done.3 = bf16[192,2048]{1,0:T(8,128)(2,1)} collective-permute-done((bf16[192,2048]{1,0:T(8,128)(2,1)}, bf16[192,2048]{1,0:T(8,128)(2,1)}, u32[]{:S(2)}, u32[]{:S(2)}) %collective-permute-start.3) | collective-permute-done | bytes 786464 | tf_op jit(solution)/shard_map/ppermute | solution.py:12
  86.7 2.4 maximum_select_fusion
  89.1 108.3 %while.12 = (s32[]{:T(128)}, bf16[16,64,384]{2,1,0:T(8,128)(2,1)}, bf16[16,64,2048]{2,1,0:T(8,128)(2,1)}, bf16[16,64,192]{2,1,0:T(8,128)(2,1)}, s32[16]{0:T(128)...) while((s32[]{:T(128)}, bf16[16,64,384]{2,1,0:T(8,128)(2,1)}, ...), condition=%wide.region_1.2_spmd, body=%wide.region_0.1_spmd.sunk | while | flops 203411584 | bytes 7235736 | solution.py:61
  90.4 1.5 fusion.30
  97.2 1.5 fusion.30
  103.9 1.5 fusion.30
  110.7 1.5 fusion.30
  117.4 1.5 fusion.30
  124.2 1.5 fusion.30
  131.0 1.5 fusion.30
  137.8 1.5 fusion.30
  144.5 1.5 fusion.30
  151.3 1.5 fusion.30
  158.1 1.5 fusion.30
  171.6 1.5 fusion.30
  178.3 1.5 fusion.30
  185.1 1.5 fusion.30
  191.9 1.5 fusion.30
  199.0 5.4 %fusion.17 = f32[768,2048]{1,0:T(8,128)S(1)} fusion(bf16[1024,2048]{1,0:T(8,128)(2,1)} %bitcast.59, bf16[1024,384]{1,0:T(8,128)(2,1)S(1)} %get-tuple-element.87, bf16[1024,384]{1,0:T(8,128)(2,1)S(1)} %get-tuple-element.86), kind=kOutput, calls=%fused_computation.29 | convolution fusion | flops 3224371200 | bytes 12058624 | tf_op jit(solution)/shard_map/dot_general | solution.py:72
  204.6 1.9 collective-permute-start.4
  206.6 7.6 %collective-permute-start.5 = (bf16[384,2048]{1,0:T(8,128)(2,1)S(1)}, bf16[384,2048]{1,0:T(8,128)(2,1)S(1)}, u32[]{:S(2)}, u32[]{:S(2)}) collective-permute-start(bf16[384,2048]{1,0:T(8,128)(2,1)S(1)} %get-tuple-element.83), channel_id=1, source_target_pairs={{0,62},{1,63},{2,0},{3,1},{4,2},{5,3},{6,4},{7,5},{8,6},{9,7},{10,... | collective-permute-start | bytes 4718600 | tf_op jit(solution)/shard_map/ppermute | solution.py:12
  214.1 30.1 %collective-permute-done.4 = bf16[384,2048]{1,0:T(8,128)(2,1)S(1)} collective-permute-done((bf16[384,2048]{1,0:T(8,128)(2,1)S(1)}, bf16[384,2048]{1,0:T(8,128)(2,1)S(1)}, u32[]{:S(2)}, u32[]{:S(2)}) %collective-permute-start.4) | collective-permute-done | bytes 1572896 | tf_op jit(solution)/shard_map/ppermute | solution.py:12
  244.2 69.4 %collective-permute-done.5 = bf16[384,2048]{1,0:T(8,128)(2,1)S(1)} collective-permute-done((bf16[384,2048]{1,0:T(8,128)(2,1)S(1)}, bf16[384,2048]{1,0:T(8,128)(2,1)S(1)}, u32[]{:S(2)}, u32[]{:S(2)}) %collective-permute-start.5) | collective-permute-done | bytes 1572896 | tf_op jit(solution)/shard_map/ppermute | solution.py:12
  (129 shorter events, 83.5 us)
Async XLA Ops:
  7.2 25.6 %copy-start.2 = (s32[2]{0:T(128)S(1)}, s32[2]{0:T(128)}, u32[]{:S(2)}) copy-start(s32[2]{0:T(128)} %param.15) | copy-start | bytes 28
  7.2 25.8 %copy-start.3 = (s32[2]{0:T(128)S(1)}, s32[2]{0:T(128)}, u32[]{:S(2)}) copy-start(s32[2]{0:T(128)} %param.14) | copy-start | bytes 28
  7.2 81.9 %all-gather.2.cloned.1.call-start = ((), (), s32[]{:S(2)}) async-start(), calls=%async_computation.2 | async-start | bytes 4718592 | tf_op jit(solution)/shard_map/all_gather | solution.py:27
  7.9 36.3 %collective-permute-start = (bf16[192,2048]{1,0:T(8,128)(2,1)}, bf16[192,2048]{1,0:T(8,128)(2,1)S(1)}, u32[]{:S(2)}, u32[]{:S(2)}) collective-permute-start(bf16[192,2048]{1,0:T(8,128)(2,1)} %bitcast.52), channel_id=1, source_target_pairs={{0,2},{1,3},{2,4},{3,5},{4,6},{5,7},{6,8},{7,9},{8,10},{9,11},{10,... | collective-permute-start | bytes 2359304 | tf_op jit(solution)/shard_map/ppermute | solution.py:12
  11.7 37.2 %collective-permute-start.1 = (bf16[192,2048]{1,0:T(8,128)(2,1)}, bf16[192,2048]{1,0:T(8,128)(2,1)S(1)}, u32[]{:S(2)}, u32[]{:S(2)}) collective-permute-start(bf16[192,2048]{1,0:T(8,128)(2,1)} %bitcast.55), channel_id=1, source_target_pairs={{0,2},{1,3},{2,4},{3,5},{4,6},{5,7},{6,8},{7,9},{8,10},{9,11},{10,... | collective-permute-start | bytes 2359304 | tf_op jit(solution)/shard_map/ppermute | solution.py:12
  16.6 53.3 %collective-permute-start.2 = (bf16[192,2048]{1,0:T(8,128)(2,1)}, bf16[192,2048]{1,0:T(8,128)(2,1)}, u32[]{:S(2)}, u32[]{:S(2)}) collective-permute-start(bf16[192,2048]{1,0:T(8,128)(2,1)} %bitcast.53), channel_id=1, source_target_pairs={{0,1},{1,2},{2,3},{3,4},{4,5},{5,6},{6,7},{7,8},{8,9},{9,10},{10,1... | collective-permute-start | bytes 2359304 | tf_op jit(solution)/shard_map/ppermute | solution.py:12
  19.8 67.0 %collective-permute-start.3 = (bf16[192,2048]{1,0:T(8,128)(2,1)}, bf16[192,2048]{1,0:T(8,128)(2,1)}, u32[]{:S(2)}, u32[]{:S(2)}) collective-permute-start(bf16[192,2048]{1,0:T(8,128)(2,1)} %bitcast.56), channel_id=1, source_target_pairs={{0,1},{1,2},{2,3},{3,4},{4,5},{5,6},{6,7},{7,8},{8,9},{9,10},{10,1... | collective-permute-start | bytes 2359304 | tf_op jit(solution)/shard_map/ppermute | solution.py:12
  25.4 17.8 %all-to-all-start = ((bf16[128,8,192]{0,2,1:T(8,128)(2,1)}), bf16[128,8,192]{0,2,1:T(8,128)(2,1)S(1)}, u32[]{:S(2)}, u32[]{:S(2)}) async-start(bf16[128,8,192]{0,2,1:T(8,128)(2,1)} %bitcast.7), calls=%async_computation | async-start | bytes 786432 | tf_op jit(solution)/shard_map/all_to_all | solution.py:31
  30.1 285.6 %reduce-scatter.2.cloned.1.call-start = ((), (), s32[]{:S(2)}) async-start(), calls=%async_computation.3 | async-start | bytes 4718592 | tf_op jit(solution)/shard_map/reduce_scatter | solution.py:63
  44.2 42.5 %copy-start = (bf16[192,2048]{1,0:T(8,128)(2,1)}, bf16[192,2048]{1,0:T(8,128)(2,1)S(1)}, u32[]{:S(2)}) copy-start(bf16[192,2048]{1,0:T(8,128)(2,1)S(1)} %collective-permute-done) | copy-start | bytes 2359300
  48.9 37.9 %copy-start.1 = (bf16[192,2048]{1,0:T(8,128)(2,1)}, bf16[192,2048]{1,0:T(8,128)(2,1)S(1)}, u32[]{:S(2)}) copy-start(bf16[192,2048]{1,0:T(8,128)(2,1)S(1)} %collective-permute-done.1) | copy-start | bytes 2359300
  204.6 39.6 %collective-permute-start.4 = (bf16[384,2048]{1,0:T(8,128)(2,1)S(1)}, bf16[384,2048]{1,0:T(8,128)(2,1)S(1)}, u32[]{:S(2)}, u32[]{:S(2)}) collective-permute-start(bf16[384,2048]{1,0:T(8,128)(2,1)S(1)} %get-tuple-element.82), channel_id=1, source_target_pairs={{0,63},{1,0},{2,1},{3,2},{4,3},{5,4},{6,5},{7,6},{8,7},{9,8},{10,9... | collective-permute-start | bytes 4718600 | tf_op jit(solution)/shard_map/ppermute | solution.py:12
  206.6 107.1 %collective-permute-start.5 = (bf16[384,2048]{1,0:T(8,128)(2,1)S(1)}, bf16[384,2048]{1,0:T(8,128)(2,1)S(1)}, u32[]{:S(2)}, u32[]{:S(2)}) collective-permute-start(bf16[384,2048]{1,0:T(8,128)(2,1)S(1)} %get-tuple-element.83), channel_id=1, source_target_pairs={{0,62},{1,63},{2,0},{3,1},{4,2},{5,3},{6,4},{7,5},{8,6},{9,7},{10,... | collective-permute-start | bytes 4718600 | tf_op jit(solution)/shard_map/ppermute | solution.py:12
Sparse Core Ops, SparseCore 0:
  10.2 44.8 all-gather.1
  197.6 41.0 reduce-scatter.1
where the time goes:
time: 325 us; the launch traced here: 323 us
  waiting for transfers between devices  143 us (44%)
  matrix products  48.8 us (15%)
  other arithmetic  41.5 us (13%)
  starting transfers between devices  29.8 us (9%)
  local copies, waits for them, and re-layouts  24.9 us (8%)
  between operations  15.5 us (5%)
  loops' own time  10.8 us (3%)
  blocking collectives  8.52 us (3%)
    ppermute x6, waiting for transfers between devices, from_behind(): return lax.ppermute(value, axis, pairs)  142 us
    ppermute x6, starting transfers between devices, from_behind(): return lax.ppermute(value, axis, pairs)  25 us
    dot_general x16, matrix products, one_block(): lax.dot_general(x_blk, weights, along_width, preferred_element_type=jnp.f...  24.4 us
    dot_general x16, matrix products, one_block(): partial_dx = jnp.dot(dgu, weights, preferred_element_type=jnp.float32)  19 us
    dynamic_slice x32, local copies, waits for them, and re-layouts, local(): lax.map(one_block, (x_blocks, dh_blocks, experts, lengths))  18.7 us
    another operation x17, other arithmetic  14.5 us
    dynamic_update_slice x16, other arithmetic, local(): lax.map(one_block, (x_blocks, dh_blocks, experts, lengths))  11.2 us
    another operation x1, loops' own time, local(): lax.map(one_block, (x_blocks, dh_blocks, experts, lengths))  10.8 us
  transfers between devices with their start and end apart: 9, of which 5 were waited for; matrix products, arithmetic and copies ran while one was open for 6% of the time, Pallas kernels for 0%

commit v1 on v0

v1 whole, which is shorter than its diff:
```python
import jax
import jax.numpy as jnp
from jax import lax
from jax.sharding import PartitionSpec as P

CHIPS_X = 4
CORES = 2
FLAG_ROWS = 16


def ring_pairs(count, steps):
    return [(source, (source + steps) % count) for source in range(count)]


def ring_step(count, steps):
    return [(e, e // CHIPS_X * CHIPS_X + (e + steps) % CHIPS_X) for e in range(count)]


def onward(count, steps, total):
    return [(holder, (source + total) % count) for source, holder in ring_step(count, steps)]


def local(tokens, hidden_grad, gate_weight, up_weight, replica_offset, block_expert, block_rows):
    n_exp = lax.axis_size("expert")
    n_dp = lax.axis_size("dp")
    chips_y = n_dp // CORES
    home_id = lax.axis_index("expert")
    core = lax.axis_index("dp") % CORES
    gate_w, up_w = gate_weight[0], up_weight[0]
    shard, width = gate_w.shape
    rows = tokens.shape[0]
    nblk = block_expert.shape[0]
    block_len = rows // nblk
    ahead, behind = ring_pairs(n_exp, 1), ring_pairs(n_exp, -1)
    swap = [(d, d // CORES * CORES + (d + 1) % CORES) for d in range(n_dp)]
    same_core = [[y * CORES + c for y in range(chips_y)] for c in range(CORES)]
    zero = jnp.zeros((), jnp.bfloat16)
    barrier = lax.optimization_barrier

    def exchange_y(parts):
        return lax.all_to_all(
            parts, "dp", split_axis=0, concat_axis=0, axis_index_groups=same_core, tiled=True
        )

    offset = replica_offset[0]
    spread = jnp.broadcast_to(tokens[None], (chips_y, rows, width))
    live = (jnp.arange(block_len, dtype=jnp.int32)[None, :] < block_rows[:, None]).reshape(1, rows)
    flag = jnp.repeat((block_expert == home_id).astype(jnp.bfloat16), block_len).reshape(1, rows)
    cot = jnp.where(live, hidden_grad.T, zero).reshape(n_dp, shard, rows)
    flags = jnp.broadcast_to(flag[None], (n_dp, FLAG_ROWS, rows))
    sent = jnp.concatenate([cot, flags], axis=1)
    w_home = jnp.concatenate([gate_w, up_w], axis=0)
    gate_w, up_w, spread = barrier((gate_w, up_w, spread))
    gate_1 = lax.ppermute(gate_w, "expert", ahead)
    up_held = lax.ppermute(up_w, "expert", ring_step(n_exp, -1))
    sent, replica_offset = barrier((sent, replica_offset))
    offset_next = lax.ppermute(replica_offset, "expert", behind)[0]
    own_rows = exchange_y(spread).reshape(chips_y * rows, width)

    mixed = jnp.where(offset_next == 1, up_w, gate_1)
    mixed, up_held, own_rows = barrier((mixed, up_held, own_rows))
    mixed_1 = lax.ppermute(mixed, "expert", ahead)
    up_2 = lax.ppermute(up_held, "expert", onward(n_exp, -1, 2))
    other_rows = lax.ppermute(own_rows, "dp", swap)
    sent, other_rows = barrier((sent, other_rows))
    got = lax.all_to_all(sent, "dp", split_axis=0, concat_axis=0, tiled=True)
    got = got.reshape(chips_y, CORES, shard + FLAG_ROWS, rows)

    def cotangents(which):
        part = lax.dynamic_index_in_dim(got, which, 1, keepdims=False)
        return jnp.transpose(part, (1, 0, 2)).reshape(shard + FLAG_ROWS, chips_y * rows)

    nt = (((1,), (1,)), ((), ()))
    tn = (((0,), (0,)), ((), ()))

    def project(weights, x):
        return lax.dot_general(weights, x, nt, preferred_element_type=jnp.float32)

    halves = (own_rows, other_rows)
    cots = [cotangents(core), cotangents(1 - core)]
    home_proj = [project(w_home, x) for x in halves]
    mixed_1, up_2, home_proj, cots = barrier((mixed_1, up_2, home_proj, cots))

    w_copy = jnp.concatenate(
        [jnp.where(offset == 1, gate_1, mixed_1), jnp.where(offset == 1, mixed_1, up_2)], axis=0
    )
    home_terms, copy_terms = [], []
    for x, cot, proj in zip(halves, cots, home_proj):
        on_home = cot[shard : shard + 1] > 0.5
        both = jnp.where(on_home, proj, project(w_copy, x))
        cotan = cot[:shard].astype(jnp.float32)
        gate_val, up_val = both[:shard], both[shard:]
        sig_val = jax.nn.sigmoid(gate_val)
        dgate = (cotan * up_val * sig_val * (1.0 + gate_val * (1.0 - sig_val))).astype(jnp.bfloat16)
        dup = (cotan * gate_val * sig_val).astype(jnp.bfloat16)
        terms = jnp.concatenate([dgate, dup], axis=0)
        home_terms.append(jnp.where(on_home, terms, zero))
        copy_terms.append(jnp.where(on_home, zero, terms))

    def weight_part(terms):
        return sum(jnp.dot(t, x, preferred_element_type=jnp.float32) for t, x in zip(terms, halves))

    copy_part = weight_part(copy_terms).astype(jnp.bfloat16)
    copy_g, copy_u = copy_part[:shard], copy_part[shard:]
    first = jnp.where(offset == 1, copy_u, copy_g)
    second = jnp.where(offset == 2, copy_u, zero)
    first, second, home_terms, copy_terms, copy_g = barrier(
        (first, second, home_terms, copy_terms, copy_g)
    )

    ret_1 = lax.ppermute(first, "expert", behind)
    ret_h = lax.ppermute(second, "expert", ring_step(n_exp, 1))
    weights_all = jnp.concatenate([w_home, w_copy], axis=0)

    def rows_part(half):
        terms = jnp.concatenate([home_terms[half], copy_terms[half]], axis=0)
        return lax.dot_general(terms, weights_all, tn, preferred_element_type=jnp.float32)

    dx_oth = rows_part(1).astype(jnp.bfloat16)
    dx_in = lax.ppermute(dx_oth, "dp", swap)
    dx_own, dx_in = barrier((rows_part(0), dx_in))
    dx_pair = (dx_own + dx_in.astype(jnp.float32)).astype(jnp.bfloat16)
    ret_1, ret_h, dx_pair = barrier((ret_1, ret_h, dx_pair))
    dx_parts = exchange_y(dx_pair.reshape(chips_y, rows, width))

    sum_g = jnp.where(offset == 1, copy_g, zero).astype(jnp.float32) + jnp.where(
        offset_next == 2, ret_1, zero
    ).astype(jnp.float32)
    sum_g, ret_h, home_terms = barrier((sum_g.astype(jnp.bfloat16), ret_h, home_terms))
    ret_g = lax.ppermute(sum_g, "expert", behind)
    ret_u = lax.ppermute(ret_h, "expert", onward(n_exp, 1, -2))
    home_part = weight_part(home_terms)
    up_part = home_part[shard:] + jnp.where(offset_next == 1, ret_1, zero).astype(jnp.float32)
    gate_part = home_part[:shard]
    up_part, gate_part, dx_parts, ret_g, ret_u = barrier((up_part, gate_part, dx_parts, ret_g, ret_u))
    input_grad = jnp.sum(dx_parts.astype(jnp.float32), axis=0).astype(jnp.bfloat16)
    gate_grad = (gate_part + ret_g.astype(jnp.float32)).astype(jnp.bfloat16)
    up_grad = (up_part + ret_u.astype(jnp.float32)).astype(jnp.bfloat16)
    return input_grad, gate_grad[None], up_grad[None]


def solution(mesh):
    placed = (
        P(("dp", "expert"), None),
        P(("dp", "expert"), None),
        P("expert", "dp", None),
        P("expert", "dp", None),
        P("expert"),
        P(("dp", "expert")),
        P(("dp", "expert")),
    )
    return jax.shard_map(
        local,
        mesh=mesh,
        in_specs=placed,
        out_specs=(P(("dp", "expert"), None), P("expert", "dp", None), P("expert", "dp", None)),
        check_vma=False,
    )
```

time: 325 us -> 156 us (0.48)
  the two profiles are of different devices: /device:TPU:28 before, /device:TPU:1 now
where the time goes in v1:
time: 156 us; the launch traced here: 155 us
  starting transfers between devices  55.2 us (35%)
  waiting for transfers between devices  48.4 us (31%)
  matrix products  21.9 us (14%)
  other arithmetic  20 us (13%)
  local copies, waits for them, and re-layouts  6.44 us (4%)
  between operations  2.88 us (2%)
    ppermute x1, waiting for transfers between devices, local(): ret_1 = lax.ppermute(first, 'expert', behind)  11 us
    ppermute x1, starting transfers between devices, local(): offset_next = lax.ppermute(replica_offset, 'expert', behind)[0]  10.7 us
    dot_general x4, matrix products, project(): return lax.dot_general(weights, x, nt, preferred_element_type=jnp.float32)  10.5 us
    all_to_all x2, starting transfers between devices, exchange_y(): lax.all_to_all(parts, 'dp', split_axis=0, concat_axis=0, axis_index_group...  9.78 us
    ppermute x1, waiting for transfers between devices, local(): ret_g = lax.ppermute(sum_g, 'expert', behind)  9.43 us
    ppermute x1, waiting for transfers between devices, local(): mixed_1 = lax.ppermute(mixed, 'expert', ahead)  7.57 us
    dot_general x4, matrix products, weight_part(): jnp.dot(t, x, preferred_element_type=jnp.float32)  7.46 us
    ppermute x1, waiting for transfers between devices, local(): gate_1 = lax.ppermute(gate_w, 'expert', ahead)  6.26 us
  transfers between devices with their start and end apart: 14, of which 10 were waited for; matrix products, arithmetic and copies ran while one was open for 15% of the time, Pallas kernels for 0%

profile of v1, /device:TPU:1, one launch (start us, length us, event | category | flops | bytes accessed | tf_op | source)
XLA Modules:
  0.0 154.7 jit_solution(10292120188029984994)
XLA Ops:
  0.6 2.6 %broadcast_in_dim.91 = bf16[4,128,2048]{2,1,0:T(8,128)(2,1)} broadcast(bf16[128,2048]{1,0:T(8,128)(2,1)} %param.7), dimensions={1,2} | broadcast | bytes 2621440 | tf_op jit(solution)/shard_map/broadcast_in_dim | solution.py:46
  3.3 5.1 %all-to-all-start = ((bf16[4,128,2048]{2,1,0:T(8,128)(2,1)}), bf16[4,128,2048]{2,1,0:T(8,128)(2,1)S(1)}, u32[]{:S(2)}, u32[]{:S(2)}) async-start(bf16[4,128,2048]{2,1,0:T(8,128)(2,1)} %broadcast_in_dim.91), calls=%async_computation | async-start | bytes 4194304 | tf_op jit(solution)/shard_map/all_to_all | solution.py:41
  8.4 3.1 %collective-permute-start.1 = (bf16[192,2048]{1,0:T(8,128)(2,1)}, bf16[192,2048]{1,0:T(8,128)(2,1)S(1)}, u32[]{:S(2)}, u32[]{:S(2)}) collective-permute-start(bf16[192,2048]{1,0:T(8,128)(2,1)} %bitcast.56), channel_id=1, source_target_pairs={{0,1},{1,2},{2,3},{3,4},{4,5},{5,6},{6,7},{7,8},{8,9},{9,10},{10,1... | collective-permute-start | bytes 2359304 | tf_op jit(solution)/shard_map/ppermute | solution.py:54
  11.5 4.7 %collective-permute-start.2 = (bf16[192,2048]{1,0:T(8,128)(2,1)}, bf16[192,2048]{1,0:T(8,128)(2,1)}, u32[]{:S(2)}, u32[]{:S(2)}) collective-permute-start(bf16[192,2048]{1,0:T(8,128)(2,1)} %bitcast.50), channel_id=1, source_target_pairs={{0,3},{1,0},{2,1},{3,2},{4,7},{5,4},{6,5},{7,6},{8,11},{9,8},{10,9... | collective-permute-start | bytes 2359304 | tf_op jit(solution)/shard_map/ppermute | solution.py:55
  20.4 10.7 %collective-permute-start = (s32[1]{0:T(128)}, s32[1]{0:T(128)}, u32[]{:S(2)}, u32[]{:S(2)}) collective-permute-start(s32[1]{0:T(128)} %param.11), channel_id=1, source_target_pairs={{0,63},{1,0},{2,1},{3,2},{4,3},{5,4},{6,5},{7,6},{8,7},{9,8},{10,9... | collective-permute-start | bytes 20 | tf_op jit(solution)/shard_map/ppermute | solution.py:57
  32.6 6.3 %collective-permute-done.1 = bf16[192,2048]{1,0:T(8,128)(2,1)S(1)} collective-permute-done((bf16[192,2048]{1,0:T(8,128)(2,1)}, bf16[192,2048]{1,0:T(8,128)(2,1)S(1)}, u32[]{:S(2)}, u32[]{:S(2)}) %collective-permute-start.1) | collective-permute-done | bytes 786464 | tf_op jit(solution)/shard_map/ppermute | solution.py:54
  38.9 2.1 %broadcast_select_fusion.1 = bf16[192,2048]{1,0:T(8,128)(2,1)} fusion(bf16[192,2048]{1,0:T(8,128)(2,1)} %bitcast.51, bf16[192,2048]{1,0:T(8,128)(2,1)S(1)} %collective-permute-done.1, pred[]{:T(512)} %bitcast.3), kind=kLoop, calls=%fused_computation.25 | loop fusion | flops 393216 | bytes 2359297 | tf_op jit(solution)/shard_map/jit(_where)/select_n | solution.py:60
  41.0 3.4 %collective-permute-start.5 = (bf16[512,2048]{1,0:T(8,128)(2,1)S(1)}, bf16[512,2048]{1,0:T(8,128)(2,1)}, u32[]{:S(2)}, u32[]{:S(2)}) collective-permute-start(bf16[512,2048]{1,0:T(8,128)(2,1)S(1)} %bitcast.42), channel_id=1, source_target_pairs={{0,64},{64,0},{128,192},{192,128},{256,320},{320,256},{384,448},{4... | collective-permute-start | bytes 6291464 | tf_op jit(solution)/shard_map/ppermute | solution.py:64
  45.1 1.9 %collective-permute-start.3 = (bf16[192,2048]{1,0:T(8,128)(2,1)}, bf16[192,2048]{1,0:T(8,128)(2,1)}, u32[]{:S(2)}, u32[]{:S(2)}) collective-permute-start(bf16[192,2048]{1,0:T(8,128)(2,1)} %broadcast_select_fusion.1), channel_id=1, source_target_pairs={{0,1},{1,2},{2,3},{3,4},{4,5},{5,6},{6,7},{7,8},{8,9},{9,10},{10,1... | collective-permute-start | bytes 2359304 | tf_op jit(solution)/shard_map/ppermute | solution.py:62
  47.0 1.9 %collective-permute-start.4 = (bf16[192,2048]{1,0:T(8,128)(2,1)}, bf16[192,2048]{1,0:T(8,128)(2,1)}, u32[]{:S(2)}, u32[]{:S(2)}) collective-permute-start(bf16[192,2048]{1,0:T(8,128)(2,1)} %collective-permute-done.2), channel_id=1, source_target_pairs={{3,2},{0,3},{1,4},{2,5},{7,6},{4,7},{5,8},{6,9},{11,10},{8,11},{9,... | collective-permute-start | bytes 2359304 | tf_op jit(solution)/shard_map/ppermute | solution.py:63
  49.0 4.6 %all-to-all-start.1 = ((bf16[8,208,128]{2,1,0:T(8,128)(2,1)}), bf16[8,208,128]{2,1,0:T(8,128)(2,1)S(1)}, u32[]{:S(2)}, u32[]{:S(2)}) async-start(bf16[8,208,128]{2,1,0:T(8,128)(2,1)} %pad_maximum_fusion.9), calls=%async_computation.1 | async-start | bytes 851968 | tf_op jit(solution)/shard_map/all_to_all | solution.py:66
  53.6 3.4 %fusion.3 = f32[384,512]{1,0:T(8,128)} fusion(bf16[512,2048]{1,0:T(8,128)(2,1)S(1)} %bitcast.43, bf16[192,2048]{1,0:T(8,128)(2,1)} %bitcast.52, bf16[192,2048]{1,0:T(8,128)(2,1)} %bitcast.57), kind=kOutput, calls=%fused_computation.14 | convolution fusion | flops 808452096 | bytes 4456448 | tf_op jit(solution)/shard_map/dot_general | solution.py:77
  57.0 3.5 %fusion.2 = f32[384,512]{1,0:T(8,128)} fusion(bf16[512,2048]{1,0:T(8,128)(2,1)} %collective-permute-done.5, bf16[192,2048]{1,0:T(8,128)(2,1)S(1)} %bitcast.53, bf16[192,2048]{1,0:T(8,128)(2,1)S(1)} %bitcast.58), kind=kOutput, calls=%fused_computation.13 | convolution fusion | flops 808452096 | bytes 4456448 | tf_op jit(solution)/shard_map/dot_general | solution.py:77
  62.2 7.6 %collective-permute-done.3 = bf16[192,2048]{1,0:T(8,128)(2,1)} collective-permute-done((bf16[192,2048]{1,0:T(8,128)(2,1)}, bf16[192,2048]{1,0:T(8,128)(2,1)}, u32[]{:S(2)}, u32[]{:S(2)}) %collective-permute-start.3) | collective-permute-done | bytes 786464 | tf_op jit(solution)/shard_map/ppermute | solution.py:62
  73.0 2.6 %fusion = f32[384,512]{1,0:T(8,128)S(1)} fusion(bf16[512,2048]{1,0:T(8,128)(2,1)} %collective-permute-done.5, bf16[192,2048]{1,0:T(8,128)(2,1)S(1)} %get-tuple-element.87, bf16[192,2048]{1,0:T(8,128)(2,1)S(1)} %get-tuple-element.86), kind=kOutput, calls=%fused_computation.11 | convolution fusion | flops 808452096 | bytes 4456448 | tf_op jit(solution)/shard_map/dot_general | solution.py:77
  78.3 2.8 %fusion.31 = f32[384,2048]{1,0:T(8,128)S(1)} fusion(bf16[384,512]{1,0:T(8,128)(2,1)S(1)} %get-tuple-element.62, bf16[512,2048]{1,0:T(8,128)(2,1)} %collective-permute-done.5), kind=kOutput, calls=%fused_computation.71 | convolution fusion | flops 805306368 | bytes 5636096 | tf_op jit(solution)/shard_map/dot_general | solution.py:101
  83.9 2.0 %convolution_convert_fusion = bf16[512,2048]{1,0:T(8,128)(2,1)S(1)} fusion(bf16[384,512]{1,0:T(8,128)(2,1)S(1)} %get-tuple-element.62, bf16[384,512]{1,0:T(8,128)(2,1)S(1)} %get-tuple-element.68, bf16[192,2048]{1,0:T(8,128)(2,1)S(1)} %get-tuple-element.87, bf16[192,2048]{1,0:T(8,128)(2,1)S(1)} %get-tuple-element.86, bf16[192,2048]{1,0:T(8,128)(2,1)S(1)} %bitcast.54, ...), kind=kOutput, calls=%fused_computation.4 | convolution fusion | flops 1625817088 | bytes 6029312 | tf_op jit(solution)/shard_map/dot_general | solution.py:117
  85.9 2.7 %collective-permute-start.8 = (bf16[512,2048]{1,0:T(8,128)(2,1)S(1)}, bf16[512,2048]{1,0:T(8,128)(2,1)S(1)}, u32[]{:S(2)}, u32[]{:S(2)}) collective-permute-start(bf16[512,2048]{1,0:T(8,128)(2,1)S(1)} %convolution_convert_fusion), channel_id=1, source_target_pairs={{0,64},{64,0},{128,192},{192,128},{256,320},{320,256},{384,448},{4... | collective-permute-start | bytes 6291464 | tf_op jit(solution)/shard_map/ppermute | solution.py:120
  89.3 4.8 %collective-permute-start.6 = (bf16[192,2048]{1,0:T(8,128)(2,1)S(1)}, bf16[192,2048]{1,0:T(8,128)(2,1)S(1)}, u32[]{:S(2)}, u32[]{:S(2)}) collective-permute-start(bf16[192,2048]{1,0:T(8,128)(2,1)S(1)} %get-tuple-element.57), channel_id=1, source_target_pairs={{0,63},{1,0},{2,1},{3,2},{4,3},{5,4},{6,5},{7,6},{8,7},{9,8},{10,9... | collective-permute-start | bytes 2359304 | tf_op jit(solution)/shard_map/ppermute | solution.py:111
  94.1 1.9 %collective-permute-start.7 = (bf16[192,2048]{1,0:T(8,128)(2,1)S(1)}, bf16[192,2048]{1,0:T(8,128)(2,1)S(1)}, u32[]{:S(2)}, u32[]{:S(2)}) collective-permute-start(bf16[192,2048]{1,0:T(8,128)(2,1)S(1)} %get-tuple-element.58), channel_id=1, source_target_pairs={{0,1},{1,2},{2,3},{3,0},{4,5},{5,6},{6,7},{7,4},{8,9},{9,10},{10,1... | collective-permute-start | bytes 2359304 | tf_op jit(solution)/shard_map/ppermute | solution.py:112
  97.9 2.1 %add_convert_fusion = bf16[512,2048]{1,0:T(8,128)(2,1)} fusion(f32[512,2048]{1,0:T(8,128)S(1)} %fusion.6, bf16[512,2048]{1,0:T(8,128)(2,1)S(1)} %collective-permute-done.8), kind=kLoop, calls=%fused_computation | loop fusion | flops 3145728 | bytes 8388608 | tf_op jit(solution)/shard_map/convert_element_type | solution.py:122
  100.0 11.0 %collective-permute-done.6 = bf16[192,2048]{1,0:T(8,128)(2,1)S(1)} collective-permute-done((bf16[192,2048]{1,0:T(8,128)(2,1)S(1)}, bf16[192,2048]{1,0:T(8,128)(2,1)S(1)}, u32[]{:S(2)}, u32[]{:S(2)}) %collective-permute-start.6) | collective-permute-done | bytes 786464 | tf_op jit(solution)/shard_map/ppermute | solution.py:111
  111.0 5.0 %collective-permute-done.7 = bf16[192,2048]{1,0:T(8,128)(2,1)S(1)} collective-permute-done((bf16[192,2048]{1,0:T(8,128)(2,1)S(1)}, bf16[192,2048]{1,0:T(8,128)(2,1)S(1)}, u32[]{:S(2)}, u32[]{:S(2)}) %collective-permute-start.7) | collective-permute-done | bytes 786464 | tf_op jit(solution)/shard_map/ppermute | solution.py:112
  116.9 4.6 %all-to-all-start.2 = ((bf16[4,128,2048]{2,1,0:T(8,128)(2,1)}), bf16[4,128,2048]{2,1,0:T(8,128)(2,1)}, u32[]{:S(2)}, u32[]{:S(2)}) async-start(bf16[4,128,2048]{2,1,0:T(8,128)(2,1)} %bitcast.47), calls=%async_computation.2 | async-start | bytes 4194304 | tf_op jit(solution)/shard_map/all_to_all | solution.py:41
  121.9 2.8 %collective-permute-start.9 = (bf16[192,2048]{1,0:T(8,128)(2,1)S(1)}, bf16[192,2048]{1,0:T(8,128)(2,1)}, u32[]{:S(2)}, u32[]{:S(2)}) collective-permute-start(bf16[192,2048]{1,0:T(8,128)(2,1)S(1)} %add_convert_fusion.4), channel_id=1, source_target_pairs={{0,63},{1,0},{2,1},{3,2},{4,3},{5,4},{6,5},{7,6},{8,7},{9,8},{10,9... | collective-permute-start | bytes 2359304 | tf_op jit(solution)/shard_map/ppermute | solution.py:130
  124.7 2.6 %collective-permute-start.10 = (bf16[192,2048]{1,0:T(8,128)(2,1)S(1)}, bf16[192,2048]{1,0:T(8,128)(2,1)}, u32[]{:S(2)}, u32[]{:S(2)}) collective-permute-start(bf16[192,2048]{1,0:T(8,128)(2,1)S(1)} %copy-done.9), channel_id=1, source_target_pairs={{1,62},{2,63},{3,0},{0,1},{5,2},{6,3},{7,4},{4,5},{9,6},{10,7},{11... | collective-permute-start | bytes 2359304 | tf_op jit(solution)/shard_map/ppermute | solution.py:131
  127.4 2.6 %fusion.32 = f32[384,2048]{1,0:T(8,128)S(1)} fusion(bf16[384,512]{1,0:T(8,128)(2,1)S(1)} %copy-done.1, bf16[512,2048]{1,0:T(8,128)(2,1)} %collective-permute-done.5), kind=kOutput, calls=%fused_computation.72 | convolution fusion | flops 805306368 | bytes 5636096 | tf_op jit(solution)/shard_map/dot_general | solution.py:101
  132.5 9.4 %collective-permute-done.9 = bf16[192,2048]{1,0:T(8,128)(2,1)} collective-permute-done((bf16[192,2048]{1,0:T(8,128)(2,1)S(1)}, bf16[192,2048]{1,0:T(8,128)(2,1)}, u32[]{:S(2)}, u32[]{:S(2)}) %collective-permute-start.9) | collective-permute-done | bytes 786464 | tf_op jit(solution)/shard_map/ppermute | solution.py:130
  142.0 3.6 %collective-permute-done.10 = bf16[192,2048]{1,0:T(8,128)(2,1)} collective-permute-done((bf16[192,2048]{1,0:T(8,128)(2,1)S(1)}, bf16[192,2048]{1,0:T(8,128)(2,1)}, u32[]{:S(2)}, u32[]{:S(2)}) %collective-permute-start.10) | collective-permute-done | bytes 786464 | tf_op jit(solution)/shard_map/ppermute | solution.py:131
  147.0 2.9 %reduce_sum.12 = bf16[128,2048]{1,0:T(8,128)(2,1)} reduce(bf16[4,128,2048]{2,1,0:T(8,128)(2,1)} %all-to-all-done.2, bf16[]{:T(256)} %constant.34.clone.1), dimensions={0}, to_apply=%region_0.1 | reduce | flops 786432 | bytes 2621442 | tf_op jit(solution)/shard_map/reduce_sum | solution.py:136
  149.9 2.7 %fusion.4 = bf16[1,192,2048]{2,1,0:T(8,128)(2,1)} fusion(f32[192,2048]{1,0:T(8,128)} %get-tuple-element.73, bf16[192,2048]{1,0:T(8,128)(2,1)} %collective-permute-done.9), kind=kLoop, calls=%fused_computation.15 | loop fusion | flops 1179648 | bytes 3145728 | tf_op jit(solution)/shard_map/broadcast_in_dim | solution.py:139
  152.5 2.2 %fusion.5 = bf16[1,192,2048]{2,1,0:T(8,128)(2,1)} fusion(f32[192,2048]{1,0:T(8,128)S(1)} %get-tuple-element.75, bf16[192,2048]{1,0:T(8,128)(2,1)} %collective-permute-done.10), kind=kLoop, calls=%fused_computation.16 | loop fusion | flops 1179648 | bytes 3145728 | tf_op jit(solution)/shard_map/broadcast_in_dim | solution.py:139
  (59 shorter events, 22.3 us)
Async XLA Ops:
  3.3 13.0 %copy-start.10 = (s32[2]{0:T(128)S(1)}, s32[2]{0:T(128)}, u32[]{:S(2)}) copy-start(s32[2]{0:T(128)} %param.13) | copy-start | bytes 28
  3.3 15.2 %copy-start.11 = (s32[2]{0:T(128)S(1)}, s32[2]{0:T(128)}, u32[]{:S(2)}) copy-start(s32[2]{0:T(128)} %param.12) | copy-start | bytes 28
  3.3 37.7 %all-to-all-start = ((bf16[4,128,2048]{2,1,0:T(8,128)(2,1)}), bf16[4,128,2048]{2,1,0:T(8,128)(2,1)S(1)}, u32[]{:S(2)}, u32[]{:S(2)}) async-start(bf16[4,128,2048]{2,1,0:T(8,128)(2,1)} %broadcast_in_dim.91), calls=%async_computation | async-start | bytes 4194304 | tf_op jit(solution)/shard_map/all_to_all | solution.py:41
  8.4 30.5 %collective-permute-start.1 = (bf16[192,2048]{1,0:T(8,128)(2,1)}, bf16[192,2048]{1,0:T(8,128)(2,1)S(1)}, u32[]{:S(2)}, u32[]{:S(2)}) collective-permute-start(bf16[192,2048]{1,0:T(8,128)(2,1)} %bitcast.56), channel_id=1, source_target_pairs={{0,1},{1,2},{2,3},{3,4},{4,5},{5,6},{6,7},{7,8},{8,9},{9,10},{10,1... | collective-permute-start | bytes 2359304 | tf_op jit(solution)/shard_map/ppermute | solution.py:54
  11.5 29.4 %collective-permute-start.2 = (bf16[192,2048]{1,0:T(8,128)(2,1)}, bf16[192,2048]{1,0:T(8,128)(2,1)}, u32[]{:S(2)}, u32[]{:S(2)}) collective-permute-start(bf16[192,2048]{1,0:T(8,128)(2,1)} %bitcast.50), channel_id=1, source_target_pairs={{0,3},{1,0},{2,1},{3,2},{4,7},{5,4},{6,5},{7,6},{8,11},{9,8},{10,9... | collective-permute-start | bytes 2359304 | tf_op jit(solution)/shard_map/ppermute | solution.py:55
  20.4 11.6 %collective-permute-start = (s32[1]{0:T(128)}, s32[1]{0:T(128)}, u32[]{:S(2)}, u32[]{:S(2)}) collective-permute-start(s32[1]{0:T(128)} %param.11), channel_id=1, source_target_pairs={{0,63},{1,0},{2,1},{3,2},{4,3},{5,4},{6,5},{7,6},{8,7},{9,8},{10,9... | collective-permute-start | bytes 20 | tf_op jit(solution)/shard_map/ppermute | solution.py:57
  41.0 8.0 %collective-permute-start.5 = (bf16[512,2048]{1,0:T(8,128)(2,1)S(1)}, bf16[512,2048]{1,0:T(8,128)(2,1)}, u32[]{:S(2)}, u32[]{:S(2)}) collective-permute-start(bf16[512,2048]{1,0:T(8,128)(2,1)S(1)} %bitcast.42), channel_id=1, source_target_pairs={{0,64},{64,0},{128,192},{192,128},{256,320},{320,256},{384,448},{4... | collective-permute-start | bytes 6291464 | tf_op jit(solution)/shard_map/ppermute | solution.py:64
  45.1 24.7 %collective-permute-start.3 = (bf16[192,2048]{1,0:T(8,128)(2,1)}, bf16[192,2048]{1,0:T(8,128)(2,1)}, u32[]{:S(2)}, u32[]{:S(2)}) collective-permute-start(bf16[192,2048]{1,0:T(8,128)(2,1)} %broadcast_select_fusion.1), channel_id=1, source_target_pairs={{0,1},{1,2},{2,3},{3,4},{4,5},{5,6},{6,7},{7,8},{8,9},{9,10},{10,1... | collective-permute-start | bytes 2359304 | tf_op jit(solution)/shard_map/ppermute | solution.py:62
  47.0 24.4 %collective-permute-start.4 = (bf16[192,2048]{1,0:T(8,128)(2,1)}, bf16[192,2048]{1,0:T(8,128)(2,1)}, u32[]{:S(2)}, u32[]{:S(2)}) collective-permute-start(bf16[192,2048]{1,0:T(8,128)(2,1)} %collective-permute-done.2), channel_id=1, source_target_pairs={{3,2},{0,3},{1,4},{2,5},{7,6},{4,7},{5,8},{6,9},{11,10},{8,11},{9,... | collective-permute-start | bytes 2359304 | tf_op jit(solution)/shard_map/ppermute | solution.py:63
  49.0 13.2 %all-to-all-start.1 = ((bf16[8,208,128]{2,1,0:T(8,128)(2,1)}), bf16[8,208,128]{2,1,0:T(8,128)(2,1)S(1)}, u32[]{:S(2)}, u32[]{:S(2)}) async-start(bf16[8,208,128]{2,1,0:T(8,128)(2,1)} %pad_maximum_fusion.9), calls=%async_computation.1 | async-start | bytes 851968 | tf_op jit(solution)/shard_map/all_to_all | solution.py:66
  53.6 3.4 %copy-start.2 = (bf16[1,192,2048]{2,1,0:T(8,128)(2,1)S(1)}, bf16[1,192,2048]{2,1,0:T(8,128)(2,1)}, u32[]{:S(2)}) copy-start(bf16[1,192,2048]{2,1,0:T(8,128)(2,1)} %param.10) | copy-start | bytes 2359300
  53.6 3.4 %copy-start.6 = (bf16[1,192,2048]{2,1,0:T(8,128)(2,1)S(1)}, bf16[1,192,2048]{2,1,0:T(8,128)(2,1)}, u32[]{:S(2)}) copy-start(bf16[1,192,2048]{2,1,0:T(8,128)(2,1)} %param.9) | copy-start | bytes 2359300
  75.6 1.1 copy-start.5
  76.6 1.2 copy-start.4
  78.2 5.0 %copy-start = (bf16[384,512]{1,0:T(8,128)(2,1)}, bf16[384,512]{1,0:T(8,128)(2,1)S(1)}, u32[]{:S(2)}) copy-start(bf16[384,512]{1,0:T(8,128)(2,1)S(1)} %get-tuple-element.68) | copy-start | bytes 1179652
  82.2 1.2 copy-start.3
  82.2 1.6 %copy-start.7 = (bf16[1,192,2048]{2,1,0:T(8,128)(2,1)S(1)}, bf16[1,192,2048]{2,1,0:T(8,128)(2,1)}, u32[]{:S(2)}) copy-start(bf16[1,192,2048]{2,1,0:T(8,128)(2,1)} %param.9) | copy-start | bytes 2359300
  85.9 12.0 %collective-permute-start.8 = (bf16[512,2048]{1,0:T(8,128)(2,1)S(1)}, bf16[512,2048]{1,0:T(8,128)(2,1)S(1)}, u32[]{:S(2)}, u32[]{:S(2)}) collective-permute-start(bf16[512,2048]{1,0:T(8,128)(2,1)S(1)} %convolution_convert_fusion), channel_id=1, source_target_pairs={{0,64},{64,0},{128,192},{192,128},{256,320},{320,256},{384,448},{4... | collective-permute-start | bytes 6291464 | tf_op jit(solution)/shard_map/ppermute | solution.py:120
  89.3 21.8 %collective-permute-start.6 = (bf16[192,2048]{1,0:T(8,128)(2,1)S(1)}, bf16[192,2048]{1,0:T(8,128)(2,1)S(1)}, u32[]{:S(2)}, u32[]{:S(2)}) collective-permute-start(bf16[192,2048]{1,0:T(8,128)(2,1)S(1)} %get-tuple-element.57), channel_id=1, source_target_pairs={{0,63},{1,0},{2,1},{3,2},{4,3},{5,4},{6,5},{7,6},{8,7},{9,8},{10,9... | collective-permute-start | bytes 2359304 | tf_op jit(solution)/shard_map/ppermute | solution.py:111
  94.1 21.9 %collective-permute-start.7 = (bf16[192,2048]{1,0:T(8,128)(2,1)S(1)}, bf16[192,2048]{1,0:T(8,128)(2,1)S(1)}, u32[]{:S(2)}, u32[]{:S(2)}) collective-permute-start(bf16[192,2048]{1,0:T(8,128)(2,1)S(1)} %get-tuple-element.58), channel_id=1, source_target_pairs={{0,1},{1,2},{2,3},{3,0},{4,5},{5,6},{6,7},{7,4},{8,9},{9,10},{10,1... | collective-permute-start | bytes 2359304 | tf_op jit(solution)/shard_map/ppermute | solution.py:112
  116.0 0.9 copy-start.8
  116.9 30.0 %all-to-all-start.2 = ((bf16[4,128,2048]{2,1,0:T(8,128)(2,1)}), bf16[4,128,2048]{2,1,0:T(8,128)(2,1)}, u32[]{:S(2)}, u32[]{:S(2)}) async-start(bf16[4,128,2048]{2,1,0:T(8,128)(2,1)} %bitcast.47), calls=%async_computation.2 | async-start | bytes 4194304 | tf_op jit(solution)/shard_map/all_to_all | solution.py:41
  121.6 3.1 %copy-start.9 = (bf16[192,2048]{1,0:T(8,128)(2,1)S(1)}, bf16[192,2048]{1,0:T(8,128)(2,1)}, u32[]{:S(2)}) copy-start(bf16[192,2048]{1,0:T(8,128)(2,1)} %copy-done.8) | copy-start | bytes 2359300
  121.6 5.8 %copy-start.1 = (bf16[384,512]{1,0:T(8,128)(2,1)S(1)}, bf16[384,512]{1,0:T(8,128)(2,1)}, u32[]{:S(2)}) copy-start(bf16[384,512]{1,0:T(8,128)(2,1)} %copy-done) | copy-start | bytes 1179652
  121.9 20.1 %collective-permute-start.9 = (bf16[192,2048]{1,0:T(8,128)(2,1)S(1)}, bf16[192,2048]{1,0:T(8,128)(2,1)}, u32[]{:S(2)}, u32[]{:S(2)}) collective-permute-start(bf16[192,2048]{1,0:T(8,128)(2,1)S(1)} %add_convert_fusion.4), channel_id=1, source_target_pairs={{0,63},{1,0},{2,1},{3,2},{4,3},{5,4},{6,5},{7,6},{8,7},{9,8},{10,9... | collective-permute-start | bytes 2359304 | tf_op jit(solution)/shard_map/ppermute | solution.py:130
  124.7 20.9 %collective-permute-start.10 = (bf16[192,2048]{1,0:T(8,128)(2,1)S(1)}, bf16[192,2048]{1,0:T(8,128)(2,1)}, u32[]{:S(2)}, u32[]{:S(2)}) collective-permute-start(bf16[192,2048]{1,0:T(8,128)(2,1)S(1)} %copy-done.9), channel_id=1, source_target_pairs={{1,62},{2,63},{3,0},{0,1},{5,2},{6,3},{7,4},{4,5},{9,6},{10,7},{11... | collective-permute-start | bytes 2359304 | tf_op jit(solution)/shard_map/ppermute | solution.py:131

commit v2 on v1

--- a/solution.py
+++ b/solution.py
@@ -59,8 +59,8 @@
 
     mixed = jnp.where(offset_next == 1, up_w, gate_1)
     mixed, up_held, own_rows = barrier((mixed, up_held, own_rows))
+    up_2 = lax.ppermute(up_held, "expert", onward(n_exp, -1, 2))
     mixed_1 = lax.ppermute(mixed, "expert", ahead)
-    up_2 = lax.ppermute(up_held, "expert", onward(n_exp, -1, 2))
     other_rows = lax.ppermute(own_rows, "dp", swap)
     sent, other_rows = barrier((sent, other_rows))
     got = lax.all_to_all(sent, "dp", split_axis=0, concat_axis=0, tiled=True)
@@ -70,72 +70,69 @@
         part = lax.dynamic_index_in_dim(got, which, 1, keepdims=False)
         return jnp.transpose(part, (1, 0, 2)).reshape(shard + FLAG_ROWS, chips_y * rows)
 
+    cots = jnp.concatenate([cotangents(core), cotangents(1 - core)], axis=1)
+    all_rows = jnp.concatenate([own_rows, other_rows], axis=0)
     nt = (((1,), (1,)), ((), ()))
     tn = (((0,), (0,)), ((), ()))
 
     def project(weights, x):
         return lax.dot_general(weights, x, nt, preferred_element_type=jnp.float32)
 
-    halves = (own_rows, other_rows)
-    cots = [cotangents(core), cotangents(1 - core)]
-    home_proj = [project(w_home, x) for x in halves]
-    mixed_1, up_2, home_proj, cots = barrier((mixed_1, up_2, home_proj, cots))
+    home_proj = project(w_home, all_rows)
+    mixed_1, home_proj, cots = barrier((mixed_1, home_proj, cots))
 
-    w_copy = jnp.concatenate(
-        [jnp.where(offset == 1, gate_1, mixed_1), jnp.where(offset == 1, mixed_1, up_2)], axis=0
-    )
-    home_terms, copy_terms = [], []
-    for x, cot, proj in zip(halves, cots, home_proj):
-        on_home = cot[shard : shard + 1] > 0.5
-        both = jnp.where(on_home, proj, project(w_copy, x))
-        cotan = cot[:shard].astype(jnp.float32)
-        gate_val, up_val = both[:shard], both[shard:]
-        sig_val = jax.nn.sigmoid(gate_val)
-        dgate = (cotan * up_val * sig_val * (1.0 + gate_val * (1.0 - sig_val))).astype(jnp.bfloat16)
-        dup = (cotan * gate_val * sig_val).astype(jnp.bfloat16)
-        terms = jnp.concatenate([dgate, dup], axis=0)
-        home_terms.append(jnp.where(on_home, terms, zero))
-        copy_terms.append(jnp.where(on_home, zero, terms))
-
-    def weight_part(terms):
-        return sum(jnp.dot(t, x, preferred_element_type=jnp.float32) for t, x in zip(terms, halves))
-
-    copy_part = weight_part(copy_terms).astype(jnp.bfloat16)
+    on_home = cots[shard : shard + 1] > 0.5
+    gate_c = jnp.where(offset == 1, gate_1, mixed_1)
+    gate_val = jnp.where(on_home, home_proj[:shard], project(gate_c, all_rows))
+    gate_val, up_2 = barrier((gate_val, up_2))
+    up_c = jnp.where(offset == 1, mixed_1, up_2)
+    up_val = jnp.where(on_home, home_proj[shard:], project(up_c, all_rows))
+    cotan = cots[:shard].astype(jnp.float32)
+    sig_val = jax.nn.sigmoid(gate_val)
+    dgate = (cotan * up_val * sig_val * (1.0 + gate_val * (1.0 - sig_val))).astype(jnp.bfloat16)
+    dup = (cotan * gate_val * sig_val).astype(jnp.bfloat16)
+    terms = jnp.concatenate([dgate, dup], axis=0)
+    home_terms = jnp.where(on_home, terms, zero)
+    copy_terms = jnp.where(on_home, zero, terms)
+    copy_part = jnp.dot(copy_terms, all_rows, preferred_element_type=jnp.float32).astype(jnp.bfloat16)
     copy_g, copy_u = copy_part[:shard], copy_part[shard:]
     first = jnp.where(offset == 1, copy_u, copy_g)
     second = jnp.where(offset == 2, copy_u, zero)
-    first, second, home_terms, copy_terms, copy_g = barrier(
-        (first, second, home_terms, copy_terms, copy_g)
+    kept = jnp.where(offset == 1, copy_g, zero)
+    first, second, kept, home_terms, copy_terms = barrier(
+        (first, second, kept, home_terms, copy_terms)
     )
 
     ret_1 = lax.ppermute(first, "expert", behind)
     ret_h = lax.ppermute(second, "expert", ring_step(n_exp, 1))
-    weights_all = jnp.concatenate([w_home, w_copy], axis=0)
+    weights_all = jnp.concatenate([w_home, gate_c, up_c], axis=0)
+    both_terms = jnp.concatenate([home_terms, copy_terms], axis=0)
+    half = chips_y * rows
 
-    def rows_part(half):
-        terms = jnp.concatenate([home_terms[half], copy_terms[half]], axis=0)
+    def rows_part(terms):
         return lax.dot_general(terms, weights_all, tn, preferred_element_type=jnp.float32)
 
-    dx_oth = rows_part(1).astype(jnp.bfloat16)
+    dx_oth = rows_part(both_terms[:, half:]).astype(jnp.bfloat16)
     dx_in = lax.ppermute(dx_oth, "dp", swap)
-    dx_own, dx_in = barrier((rows_part(0), dx_in))
+    dx_own, dx_in = barrier((rows_part(both_terms[:, :half]), dx_in))
     dx_pair = (dx_own + dx_in.astype(jnp.float32)).astype(jnp.bfloat16)
-    ret_1, ret_h, dx_pair = barrier((ret_1, ret_h, dx_pair))
+    dx_pair, home_terms = barrier((dx_pair, home_terms))
     dx_parts = exchange_y(dx_pair.reshape(chips_y, rows, width))
 
-    sum_g = jnp.where(offset == 1, copy_g, zero).astype(jnp.float32) + jnp.where(
-        offset_next == 2, ret_1, zero
-    ).astype(jnp.float32)
-    sum_g, ret_h, home_terms = barrier((sum_g.astype(jnp.bfloat16), ret_h, home_terms))
+    home_part = jnp.dot(home_terms, all_rows, preferred_element_type=jnp.float32)
+    ret_1, ret_h, home_part = barrier((ret_1, ret_h, home_part))
+    sum_g = kept.astype(jnp.float32) + jnp.where(offset_next == 2, ret_1, zero).astype(jnp.float32)
+    sum_g, ret_h, home_part = barrier((sum_g.astype(jnp.bfloat16), ret_h, home_part))
     ret_g = lax.ppermute(sum_g, "expert", behind)
     ret_u = lax.ppermute(ret_h, "expert", onward(n_exp, 1, -2))
-    home_part = weight_part(home_terms)
-    up_part = home_part[shard:] + jnp.where(offset_next == 1, ret_1, zero).astype(jnp.float32)
-    gate_part = home_part[:shard]
-    up_part, gate_part, dx_parts, ret_g, ret_u = barrier((up_part, gate_part, dx_parts, ret_g, ret_u))
     input_grad = jnp.sum(dx_parts.astype(jnp.float32), axis=0).astype(jnp.bfloat16)
-    gate_grad = (gate_part + ret_g.astype(jnp.float32)).astype(jnp.bfloat16)
-    up_grad = (up_part + ret_u.astype(jnp.float32)).astype(jnp.bfloat16)
+    home_part, ret_1, input_grad, ret_g, ret_u = barrier((home_part, ret_1, input_grad, ret_g, ret_u))
+    gate_grad = (home_part[:shard] + ret_g.astype(jnp.float32)).astype(jnp.bfloat16)
+    up_grad = (
+        home_part[shard:]
+        + jnp.where(offset_next == 1, ret_1, zero).astype(jnp.float32)
+        + ret_u.astype(jnp.float32)
+    ).astype(jnp.bfloat16)
     return input_grad, gate_grad[None], up_grad[None]
 
 

time: 156 us -> 143 us (0.917)
  waiting for transfers between devices: 48.4 us -> 37.5 us
  local copies, waits for them, and re-layouts: 6.44 us -> 9.57 us
  matrix products: 21.9 us -> 19.3 us
  other arithmetic: 20 us -> 18.1 us
  starting transfers between devices: 55.2 us -> 53.5 us
    ppermute x1, waiting for transfers between devices: 11 us -> 1.51 us  [local(): ret_1 = lax.ppermute(first, 'expert', behind)]
    all_to_all x2, waiting for transfers between devices: 1.41 us -> 7.36 us  [exchange_y(): lax.all_to_all(parts, 'dp', split_axis=0, concat_axis=0, axis_index_group...]
    ppermute x1, waiting for transfers between devices: 9.43 us -> 6.16 us  [local(): ret_g = lax.ppermute(sum_g, 'expert', behind)]
    concatenate x0 -> x2, local copies, waits for them, and re-layouts: none -> 3.2 us  [the longest x1 3.15 us: local(): all_rows = jnp.concatenate([own_rows, other_rows], axis=0)]
    dot_general x4 -> x3, matrix products: 10.5 us -> 7.57 us  [project(): return lax.dot_general(weights, x, nt, preferred_element_type=jnp.float32)]
    slice x2 -> x0, other arithmetic: 2.56 us -> none  [the longest x1 1.53 us: local(): gate_part = home_part[:shard]]
    select_n x5 -> x4, other arithmetic: 2.01 us -> 4.14 us  [the longest x1 1.44 us: local(): kept = jnp.where(offset == 1, copy_g, zero)]
    ppermute x1, waiting for transfers between devices: 1.67 us -> 0.01 us  [local(): up_2 = lax.ppermute(up_held, 'expert', onward(n_exp, -1, 2))]
  transfers between devices with their start and end apart: 14 -> 14, of which waited for: 10 -> 9; matrix products, arithmetic and copies ran while one was open for 15% -> 22% of each run, Pallas kernels for 0% -> 0%
where the time goes in v2:
time: 143 us; the launch traced here: 141 us
  starting transfers between devices  53.5 us (37%)
  waiting for transfers between devices  37.5 us (26%)
  matrix products  19.3 us (13%)
  other arithmetic  18.1 us (13%)
  local copies, waits for them, and re-layouts  9.57 us (7%)
  between operations  2.7 us (2%)
    ppermute x1, starting transfers between devices, local(): offset_next = lax.ppermute(replica_offset, 'expert', behind)[0]  10.7 us
    all_to_all x2, starting transfers between devices, exchange_y(): lax.all_to_all(parts, 'dp', split_axis=0, concat_axis=0, axis_index_group...  9.38 us
    dot_general x3, matrix products, project(): return lax.dot_general(weights, x, nt, preferred_element_type=jnp.float32)  7.57 us
    all_to_all x2, waiting for transfers between devices, exchange_y(): lax.all_to_all(parts, 'dp', split_axis=0, concat_axis=0, axis_index_group...  7.36 us
    ppermute x1, waiting for transfers between devices, local(): gate_1 = lax.ppermute(gate_w, 'expert', ahead)  6.31 us
    ppermute x1, waiting for transfers between devices, local(): ret_g = lax.ppermute(sum_g, 'expert', behind)  6.16 us
    ppermute x1, waiting for transfers between devices, local(): mixed_1 = lax.ppermute(mixed, 'expert', ahead)  6.06 us
    dot_general x1, matrix products, local(): jnp.dot(home_terms, all_rows, preferred_element_type=jnp.float32)  5.97 us
  transfers between devices with their start and end apart: 14, of which 9 were waited for; matrix products, arithmetic and copies ran while one was open for 22% of the time, Pallas kernels for 0%

profile of v2, /device:TPU:1, one launch (start us, length us, event | category | flops | bytes accessed | tf_op | source)
XLA Modules:
  0.0 140.6 jit_solution(3522425930515956106)
XLA Ops:
  0.6 2.6 %broadcast_in_dim.81 = bf16[4,128,2048]{2,1,0:T(8,128)(2,1)} broadcast(bf16[128,2048]{1,0:T(8,128)(2,1)} %param.7), dimensions={1,2} | broadcast | bytes 2621440 | tf_op jit(solution)/shard_map/broadcast_in_dim | solution.py:46
  3.3 5.1 %all-to-all-start = ((bf16[4,128,2048]{2,1,0:T(8,128)(2,1)}), bf16[4,128,2048]{2,1,0:T(8,128)(2,1)S(1)}, u32[]{:S(2)}, u32[]{:S(2)}) async-start(bf16[4,128,2048]{2,1,0:T(8,128)(2,1)} %broadcast_in_dim.81), calls=%async_computation | async-start | bytes 4194304 | tf_op jit(solution)/shard_map/all_to_all | solution.py:41
  8.4 3.1 %collective-permute-start.1 = (bf16[192,2048]{1,0:T(8,128)(2,1)}, bf16[192,2048]{1,0:T(8,128)(2,1)S(1)}, u32[]{:S(2)}, u32[]{:S(2)}) collective-permute-start(bf16[192,2048]{1,0:T(8,128)(2,1)} %bitcast.49), channel_id=1, source_target_pairs={{0,1},{1,2},{2,3},{3,4},{4,5},{5,6},{6,7},{7,8},{8,9},{9,10},{10,1... | collective-permute-start | bytes 2359304 | tf_op jit(solution)/shard_map/ppermute | solution.py:54
  11.5 4.7 %collective-permute-start.2 = (bf16[192,2048]{1,0:T(8,128)(2,1)}, bf16[192,2048]{1,0:T(8,128)(2,1)}, u32[]{:S(2)}, u32[]{:S(2)}) collective-permute-start(bf16[192,2048]{1,0:T(8,128)(2,1)} %bitcast.44), channel_id=1, source_target_pairs={{0,3},{1,0},{2,1},{3,2},{4,7},{5,4},{6,5},{7,6},{8,11},{9,8},{10,9... | collective-permute-start | bytes 2359304 | tf_op jit(solution)/shard_map/ppermute | solution.py:55
  18.6 1.8 %pad_maximum_fusion.4 = bf16[8,208,128]{2,1,0:T(8,128)(2,1)} fusion(bf16[8,16,128]{2,1,0:T(8,128)(2,1)S(1)} %broadcast_in_dim.80, bf16[8,192,128]{2,1,0:T(8,128)(2,1)} %bitcast.43), kind=kLoop, calls=%fused_computation.34 | loop fusion | flops 851968 | bytes 851968 | tf_op jit(solution)/shard_map/concatenate | solution.py:51
  20.4 10.7 %collective-permute-start = (s32[1]{0:T(128)}, s32[1]{0:T(128)}, u32[]{:S(2)}, u32[]{:S(2)}) collective-permute-start(s32[1]{0:T(128)} %param.11), channel_id=1, source_target_pairs={{0,63},{1,0},{2,1},{3,2},{4,3},{5,4},{6,5},{7,6},{8,7},{9,8},{10,9... | collective-permute-start | bytes 20 | tf_op jit(solution)/shard_map/ppermute | solution.py:57
  32.6 6.3 %collective-permute-done.1 = bf16[192,2048]{1,0:T(8,128)(2,1)S(1)} collective-permute-done((bf16[192,2048]{1,0:T(8,128)(2,1)}, bf16[192,2048]{1,0:T(8,128)(2,1)S(1)}, u32[]{:S(2)}, u32[]{:S(2)}) %collective-permute-start.1) | collective-permute-done | bytes 786464 | tf_op jit(solution)/shard_map/ppermute | solution.py:54
  38.9 2.1 %broadcast_select_fusion.3 = bf16[192,2048]{1,0:T(8,128)(2,1)} fusion(bf16[192,2048]{1,0:T(8,128)(2,1)} %bitcast.45, bf16[192,2048]{1,0:T(8,128)(2,1)S(1)} %collective-permute-done.1, pred[]{:T(512)} %bitcast.3), kind=kLoop, calls=%fused_computation.29 | loop fusion | flops 393216 | bytes 2359297 | tf_op jit(solution)/shard_map/jit(_where)/select_n | solution.py:60
  41.0 3.4 %collective-permute-start.4 = (bf16[512,2048]{1,0:T(8,128)(2,1)S(1)}, bf16[512,2048]{1,0:T(8,128)(2,1)}, u32[]{:S(2)}, u32[]{:S(2)}) collective-permute-start(bf16[512,2048]{1,0:T(8,128)(2,1)S(1)} %bitcast.39), channel_id=1, source_target_pairs={{0,64},{64,0},{128,192},{192,128},{256,320},{320,256},{384,448},{4... | collective-permute-start | bytes 6291464 | tf_op jit(solution)/shard_map/ppermute | solution.py:64
  45.1 1.9 %collective-permute-start.3 = (bf16[192,2048]{1,0:T(8,128)(2,1)}, bf16[192,2048]{1,0:T(8,128)(2,1)}, u32[]{:S(2)}, u32[]{:S(2)}) collective-permute-start(bf16[192,2048]{1,0:T(8,128)(2,1)} %broadcast_select_fusion.3), channel_id=1, source_target_pairs={{0,1},{1,2},{2,3},{3,4},{4,5},{5,6},{6,7},{7,8},{8,9},{9,10},{10,1... | collective-permute-start | bytes 2359304 | tf_op jit(solution)/shard_map/ppermute | solution.py:63
  47.0 1.9 %collective-permute-start.5 = (bf16[192,2048]{1,0:T(8,128)(2,1)}, bf16[192,2048]{1,0:T(8,128)(2,1)}, u32[]{:S(2)}, u32[]{:S(2)}) collective-permute-start(bf16[192,2048]{1,0:T(8,128)(2,1)} %collective-permute-done.2), channel_id=1, source_target_pairs={{3,2},{0,3},{1,4},{2,5},{7,6},{4,7},{5,8},{6,9},{11,10},{8,11},{9,... | collective-permute-start | bytes 2359304 | tf_op jit(solution)/shard_map/ppermute | solution.py:62
  50.5 4.6 %all-to-all-start.1 = ((bf16[8,208,128]{2,1,0:T(8,128)(2,1)}), bf16[8,208,128]{2,1,0:T(8,128)(2,1)S(1)}, u32[]{:S(2)}, u32[]{:S(2)}) async-start(bf16[8,208,128]{2,1,0:T(8,128)(2,1)} %pad_maximum_fusion.4), calls=%async_computation.1 | async-start | bytes 851968 | tf_op jit(solution)/shard_map/all_to_all | solution.py:66
  55.1 3.1 %constant_dynamic-update-slice_fusion = bf16[1024,2048]{1,0:T(8,128)(2,1)} fusion(bf16[1024,2048]{1,0:T(8,128)(2,1)} %constant_dynamic-update-slice_fusion.1, bf16[512,2048]{1,0:T(8,128)(2,1)} %collective-permute-done.4), kind=kLoop, calls=%fused_computation.42 | loop fusion | bytes 4194304 | tf_op jit(solution)/shard_map/concatenate | solution.py:74
  58.2 4.5 %fusion = f32[384,1024]{1,0:T(8,128)S(1)} fusion(bf16[1024,2048]{1,0:T(8,128)(2,1)} %constant_dynamic-update-slice_fusion, bf16[192,2048]{1,0:T(8,128)(2,1)} %bitcast.46, bf16[192,2048]{1,0:T(8,128)(2,1)} %bitcast.50), kind=kOutput, calls=%fused_computation.4 | convolution fusion | flops 1613758464 | bytes 7340032 | tf_op jit(solution)/shard_map/dot_general | solution.py:79
  63.8 6.1 %collective-permute-done.3 = bf16[192,2048]{1,0:T(8,128)(2,1)} collective-permute-done((bf16[192,2048]{1,0:T(8,128)(2,1)}, bf16[192,2048]{1,0:T(8,128)(2,1)}, u32[]{:S(2)}, u32[]{:S(2)}) %collective-permute-start.3) | collective-permute-done | bytes 786464 | tf_op jit(solution)/shard_map/ppermute | solution.py:63
  71.1 1.5 %slice_select_fusion = f32[192,1024]{1,0:T(8,128)S(1)} fusion(f32[384,1024]{1,0:T(8,128)S(1)} %fusion, pred[1024]{0:T(1024)(128)(4,1)S(1)} %compare_reduce_fusion, bf16[192,2048]{1,0:T(8,128)(2,1)S(1)} %broadcast_select_fusion.7, bf16[1024,2048]{1,0:T(8,128)(2,1)S(1)} %copy-done), kind=kOutput, calls=%fused_computation.25 | convolution fusion | flops 805502976 | bytes 6554624 | tf_op jit(solution)/shard_map/dot_general | solution.py:79
  76.1 1.8 %convolution_convert_fusion.1 = bf16[384,2048]{1,0:T(8,128)(2,1)S(1)} fusion(bf16[384,1024]{1,0:T(8,128)(2,1)S(1)} %get-tuple-element.57, bf16[1024,2048]{1,0:T(8,128)(2,1)S(1)} %copy-done), kind=kOutput, calls=%fused_computation.3 | convolution fusion | flops 1611399168 | bytes 6553600 | tf_op jit(solution)/shard_map/dot_general | solution.py:97
  80.2 2.1 %convolution_convert_fusion = bf16[512,2048]{1,0:T(8,128)(2,1)S(1)} fusion(bf16[768,1024]{1,0:T(8,128)(2,1)S(1)} %constant_dynamic-update-slice_fusion.2, bf16[192,2048]{1,0:T(8,128)(2,1)S(1)} %broadcast_select_fusion.6, bf16[192,2048]{1,0:T(8,128)(2,1)S(1)} %broadcast_select_fusion.7, bf16[192,2048]{1,0:T(8,128)(2,1)S(1)} %bitcast.47, ...), kind=kOutput, calls=%fused_computation.2 | convolution fusion | flops 1624244224 | bytes 6029312 | tf_op jit(solution)/shard_map/dot_general | solution.py:113
  82.2 2.7 %collective-permute-start.8 = (bf16[512,2048]{1,0:T(8,128)(2,1)S(1)}, bf16[512,2048]{1,0:T(8,128)(2,1)S(1)}, u32[]{:S(2)}, u32[]{:S(2)}) collective-permute-start(bf16[512,2048]{1,0:T(8,128)(2,1)S(1)} %convolution_convert_fusion), channel_id=1, source_target_pairs={{0,64},{64,0},{128,192},{192,128},{256,320},{320,256},{384,448},{4... | collective-permute-start | bytes 6291464 | tf_op jit(solution)/shard_map/ppermute | solution.py:116
  85.5 3.7 %collective-permute-start.6 = (bf16[192,2048]{1,0:T(8,128)(2,1)}, bf16[192,2048]{1,0:T(8,128)(2,1)S(1)}, u32[]{:S(2)}, u32[]{:S(2)}) collective-permute-start(bf16[192,2048]{1,0:T(8,128)(2,1)} %get-tuple-element.54), channel_id=1, source_target_pairs={{0,63},{1,0},{2,1},{3,2},{4,3},{5,4},{6,5},{7,6},{8,7},{9,8},{10,9... | collective-permute-start | bytes 2359304 | tf_op jit(solution)/shard_map/ppermute | solution.py:106
  89.2 1.9 %collective-permute-start.7 = (bf16[192,2048]{1,0:T(8,128)(2,1)}, bf16[192,2048]{1,0:T(8,128)(2,1)}, u32[]{:S(2)}, u32[]{:S(2)}) collective-permute-start(bf16[192,2048]{1,0:T(8,128)(2,1)} %get-tuple-element.55), channel_id=1, source_target_pairs={{0,1},{1,2},{2,3},{3,0},{4,5},{5,6},{6,7},{7,4},{8,9},{9,10},{10,1... | collective-permute-start | bytes 2359304 | tf_op jit(solution)/shard_map/ppermute | solution.py:107
  91.1 1.9 %fusion.12 = f32[512,2048]{1,0:T(8,128)S(1)} fusion(bf16[768,1024]{1,0:T(8,128)(2,1)S(1)} %constant_dynamic-update-slice_fusion.2, bf16[192,2048]{1,0:T(8,128)(2,1)S(1)} %broadcast_select_fusion.6, bf16[192,2048]{1,0:T(8,128)(2,1)S(1)} %broadcast_select_fusion.7, bf16[192,2048]{1,0:T(8,128)(2,1)S(1)} %bitcast.48, bf16[192,2048]{1,0:T(8,128)(2,1)S(1)} %bitcast.52), kind=kOutput, calls=%fused_computation.21 | convolution fusion | flops 1623195648 | bytes 8126464 | tf_op jit(solution)/shard_map/dot_general | solution.py:113
  93.0 2.1 %add_convert_fusion = bf16[512,2048]{1,0:T(8,128)(2,1)} fusion(f32[512,2048]{1,0:T(8,128)S(1)} %fusion.12, bf16[512,2048]{1,0:T(8,128)(2,1)S(1)} %collective-permute-done.8), kind=kLoop, calls=%fused_computation | loop fusion | flops 3145728 | bytes 8388608 | tf_op jit(solution)/shard_map/convert_element_type | solution.py:118
  95.2 4.2 %all-to-all-start.2 = ((bf16[4,128,2048]{2,1,0:T(8,128)(2,1)}), bf16[4,128,2048]{2,1,0:T(8,128)(2,1)S(1)}, u32[]{:S(2)}, u32[]{:S(2)}) async-start(bf16[4,128,2048]{2,1,0:T(8,128)(2,1)} %bitcast.41), calls=%async_computation.2 | async-start | bytes 4194304 | tf_op jit(solution)/shard_map/all_to_all | solution.py:41
  99.4 6.0 %fusion.18 = f32[384,2048]{1,0:T(8,128)} fusion(bf16[384,1024]{1,0:T(8,128)(2,1)} %copy-done.2, bf16[1024,2048]{1,0:T(8,128)(2,1)} %constant_dynamic-update-slice_fusion), kind=kOutput, calls=%fused_computation.52 | convolution fusion | flops 1610612736 | bytes 8126464 | tf_op jit(solution)/shard_map/dot_general | solution.py:122
  106.9 4.6 %collective-permute-done.7 = bf16[192,2048]{1,0:T(8,128)(2,1)} collective-permute-done((bf16[192,2048]{1,0:T(8,128)(2,1)}, bf16[192,2048]{1,0:T(8,128)(2,1)}, u32[]{:S(2)}, u32[]{:S(2)}) %collective-permute-start.7) | collective-permute-done | bytes 786464 | tf_op jit(solution)/shard_map/ppermute | solution.py:107
  112.6 2.8 %collective-permute-start.9 = (bf16[192,2048]{1,0:T(8,128)(2,1)}, bf16[192,2048]{1,0:T(8,128)(2,1)}, u32[]{:S(2)}, u32[]{:S(2)}) collective-permute-start(bf16[192,2048]{1,0:T(8,128)(2,1)} %add_convert_fusion.3), channel_id=1, source_target_pairs={{0,63},{1,0},{2,1},{3,2},{4,3},{5,4},{6,5},{7,6},{8,7},{9,8},{10,9... | collective-permute-start | bytes 2359304 | tf_op jit(solution)/shard_map/ppermute | solution.py:126
  115.4 2.5 %collective-permute-start.10 = (bf16[192,2048]{1,0:T(8,128)(2,1)}, bf16[192,2048]{1,0:T(8,128)(2,1)}, u32[]{:S(2)}, u32[]{:S(2)}) collective-permute-start(bf16[192,2048]{1,0:T(8,128)(2,1)} %collective-permute-done.7), channel_id=1, source_target_pairs={{1,62},{2,63},{3,0},{0,1},{5,2},{6,3},{7,4},{4,5},{9,6},{10,7},{11... | collective-permute-start | bytes 2359304 | tf_op jit(solution)/shard_map/ppermute | solution.py:127
  117.9 7.4 %all-to-all-done.2 = bf16[4,128,2048]{2,1,0:T(8,128)(2,1)S(1)} async-done(((bf16[4,128,2048]{2,1,0:T(8,128)(2,1)}), bf16[4,128,2048]{2,1,0:T(8,128)(2,1)S(1)}, u32[]{:S(2)}, u32[]{:S(2)}) %all-to-all-start.2) | async-done | bytes 2097184 | tf_op jit(solution)/shard_map/all_to_all | solution.py:41
  126.6 6.2 %collective-permute-done.9 = bf16[192,2048]{1,0:T(8,128)(2,1)} collective-permute-done((bf16[192,2048]{1,0:T(8,128)(2,1)}, bf16[192,2048]{1,0:T(8,128)(2,1)}, u32[]{:S(2)}, u32[]{:S(2)}) %collective-permute-start.9) | collective-permute-done | bytes 786464 | tf_op jit(solution)/shard_map/ppermute | solution.py:126
  132.7 3.8 %collective-permute-done.10 = bf16[192,2048]{1,0:T(8,128)(2,1)} collective-permute-done((bf16[192,2048]{1,0:T(8,128)(2,1)}, bf16[192,2048]{1,0:T(8,128)(2,1)}, u32[]{:S(2)}, u32[]{:S(2)}) %collective-permute-start.10) | collective-permute-done | bytes 786464 | tf_op jit(solution)/shard_map/ppermute | solution.py:127
  136.5 4.1 %fusion.10 = (bf16[1,192,2048]{2,1,0:T(8,128)(2,1)}, bf16[1,192,2048]{2,1,0:T(8,128)(2,1)}) fusion(bf16[192,2048]{1,0:T(8,128)(2,1)} %collective-permute-done.10, f32[384,2048]{1,0:T(8,128)} %fusion.18, bf16[192,2048]{1,0:T(8,128)(2,1)S(1)} %collective-permute-done.6, pred[]{:T(512)} %bitcast.3, bf16[192,2048]{1,0:T(8,128)(2,1)} %collective-permute-done.9), kind=kLoop, calls=%fused_computation.19 | loop fusion | flops 3538944 | bytes 7077889 | tf_op jit(solution)/shard_map/broadcast_in_dim | solution.py:136
  (45 shorter events, 16.5 us)
Async XLA Ops:
  0.6 15.7 %copy-start.5 = (s32[2]{0:T(128)S(1)}, s32[2]{0:T(128)}, u32[]{:S(2)}) copy-start(s32[2]{0:T(128)} %param.13) | copy-start | bytes 28
  3.3 15.2 %copy-start.6 = (s32[2]{0:T(128)S(1)}, s32[2]{0:T(128)}, u32[]{:S(2)}) copy-start(s32[2]{0:T(128)} %param.12) | copy-start | bytes 28
  3.3 37.7 %all-to-all-start = ((bf16[4,128,2048]{2,1,0:T(8,128)(2,1)}), bf16[4,128,2048]{2,1,0:T(8,128)(2,1)S(1)}, u32[]{:S(2)}, u32[]{:S(2)}) async-start(bf16[4,128,2048]{2,1,0:T(8,128)(2,1)} %broadcast_in_dim.81), calls=%async_computation | async-start | bytes 4194304 | tf_op jit(solution)/shard_map/all_to_all | solution.py:41
  8.4 30.5 %collective-permute-start.1 = (bf16[192,2048]{1,0:T(8,128)(2,1)}, bf16[192,2048]{1,0:T(8,128)(2,1)S(1)}, u32[]{:S(2)}, u32[]{:S(2)}) collective-permute-start(bf16[192,2048]{1,0:T(8,128)(2,1)} %bitcast.49), channel_id=1, source_target_pairs={{0,1},{1,2},{2,3},{3,4},{4,5},{5,6},{6,7},{7,8},{8,9},{9,10},{10,1... | collective-permute-start | bytes 2359304 | tf_op jit(solution)/shard_map/ppermute | solution.py:54
  11.5 29.4 %collective-permute-start.2 = (bf16[192,2048]{1,0:T(8,128)(2,1)}, bf16[192,2048]{1,0:T(8,128)(2,1)}, u32[]{:S(2)}, u32[]{:S(2)}) collective-permute-start(bf16[192,2048]{1,0:T(8,128)(2,1)} %bitcast.44), channel_id=1, source_target_pairs={{0,3},{1,0},{2,1},{3,2},{4,7},{5,4},{6,5},{7,6},{8,11},{9,8},{10,9... | collective-permute-start | bytes 2359304 | tf_op jit(solution)/shard_map/ppermute | solution.py:55
  20.4 11.6 %collective-permute-start = (s32[1]{0:T(128)}, s32[1]{0:T(128)}, u32[]{:S(2)}, u32[]{:S(2)}) collective-permute-start(s32[1]{0:T(128)} %param.11), channel_id=1, source_target_pairs={{0,63},{1,0},{2,1},{3,2},{4,3},{5,4},{6,5},{7,6},{8,7},{9,8},{10,9... | collective-permute-start | bytes 20 | tf_op jit(solution)/shard_map/ppermute | solution.py:57
  41.0 9.5 %collective-permute-start.4 = (bf16[512,2048]{1,0:T(8,128)(2,1)S(1)}, bf16[512,2048]{1,0:T(8,128)(2,1)}, u32[]{:S(2)}, u32[]{:S(2)}) collective-permute-start(bf16[512,2048]{1,0:T(8,128)(2,1)S(1)} %bitcast.39), channel_id=1, source_target_pairs={{0,64},{64,0},{128,192},{192,128},{256,320},{320,256},{384,448},{4... | collective-permute-start | bytes 6291464 | tf_op jit(solution)/shard_map/ppermute | solution.py:64
  45.1 24.7 %collective-permute-start.3 = (bf16[192,2048]{1,0:T(8,128)(2,1)}, bf16[192,2048]{1,0:T(8,128)(2,1)}, u32[]{:S(2)}, u32[]{:S(2)}) collective-permute-start(bf16[192,2048]{1,0:T(8,128)(2,1)} %broadcast_select_fusion.3), channel_id=1, source_target_pairs={{0,1},{1,2},{2,3},{3,4},{4,5},{5,6},{6,7},{7,8},{8,9},{9,10},{10,1... | collective-permute-start | bytes 2359304 | tf_op jit(solution)/shard_map/ppermute | solution.py:63
  47.0 25.6 %collective-permute-start.5 = (bf16[192,2048]{1,0:T(8,128)(2,1)}, bf16[192,2048]{1,0:T(8,128)(2,1)}, u32[]{:S(2)}, u32[]{:S(2)}) collective-permute-start(bf16[192,2048]{1,0:T(8,128)(2,1)} %collective-permute-done.2), channel_id=1, source_target_pairs={{3,2},{0,3},{1,4},{2,5},{7,6},{4,7},{5,8},{6,9},{11,10},{8,11},{9,... | collective-permute-start | bytes 2359304 | tf_op jit(solution)/shard_map/ppermute | solution.py:62
  50.5 13.2 %all-to-all-start.1 = ((bf16[8,208,128]{2,1,0:T(8,128)(2,1)}), bf16[8,208,128]{2,1,0:T(8,128)(2,1)S(1)}, u32[]{:S(2)}, u32[]{:S(2)}) async-start(bf16[8,208,128]{2,1,0:T(8,128)(2,1)} %pad_maximum_fusion.4), calls=%async_computation.1 | async-start | bytes 851968 | tf_op jit(solution)/shard_map/all_to_all | solution.py:66
  63.6 7.4 %copy-start = (bf16[1024,2048]{1,0:T(8,128)(2,1)S(1)}, bf16[1024,2048]{1,0:T(8,128)(2,1)}, u32[]{:S(2)}) copy-start(bf16[1024,2048]{1,0:T(8,128)(2,1)} %constant_dynamic-update-slice_fusion) | copy-start | bytes 12582916
  76.1 3.3 %copy-start.2 = (bf16[384,1024]{1,0:T(8,128)(2,1)}, bf16[384,1024]{1,0:T(8,128)(2,1)S(1)}, u32[]{:S(2)}) copy-start(bf16[384,1024]{1,0:T(8,128)(2,1)S(1)} %get-tuple-element.60) | copy-start | bytes 2359300
  77.9 1.6 %copy-start.3 = (bf16[1,192,2048]{2,1,0:T(8,128)(2,1)S(1)}, bf16[1,192,2048]{2,1,0:T(8,128)(2,1)}, u32[]{:S(2)}) copy-start(bf16[1,192,2048]{2,1,0:T(8,128)(2,1)} %param.10) | copy-start | bytes 2359300
  77.9 2.2 %copy-start.4 = (bf16[1,192,2048]{2,1,0:T(8,128)(2,1)S(1)}, bf16[1,192,2048]{2,1,0:T(8,128)(2,1)}, u32[]{:S(2)}) copy-start(bf16[1,192,2048]{2,1,0:T(8,128)(2,1)} %param.9) | copy-start | bytes 2359300
  82.2 10.8 %collective-permute-start.8 = (bf16[512,2048]{1,0:T(8,128)(2,1)S(1)}, bf16[512,2048]{1,0:T(8,128)(2,1)S(1)}, u32[]{:S(2)}, u32[]{:S(2)}) collective-permute-start(bf16[512,2048]{1,0:T(8,128)(2,1)S(1)} %convolution_convert_fusion), channel_id=1, source_target_pairs={{0,64},{64,0},{128,192},{192,128},{256,320},{320,256},{384,448},{4... | collective-permute-start | bytes 6291464 | tf_op jit(solution)/shard_map/ppermute | solution.py:116
  85.5 21.4 %collective-permute-start.6 = (bf16[192,2048]{1,0:T(8,128)(2,1)}, bf16[192,2048]{1,0:T(8,128)(2,1)S(1)}, u32[]{:S(2)}, u32[]{:S(2)}) collective-permute-start(bf16[192,2048]{1,0:T(8,128)(2,1)} %get-tuple-element.54), channel_id=1, source_target_pairs={{0,63},{1,0},{2,1},{3,2},{4,3},{5,4},{6,5},{7,6},{8,7},{9,8},{10,9... | collective-permute-start | bytes 2359304 | tf_op jit(solution)/shard_map/ppermute | solution.py:106
  89.2 22.3 %collective-permute-start.7 = (bf16[192,2048]{1,0:T(8,128)(2,1)}, bf16[192,2048]{1,0:T(8,128)(2,1)}, u32[]{:S(2)}, u32[]{:S(2)}) collective-permute-start(bf16[192,2048]{1,0:T(8,128)(2,1)} %get-tuple-element.55), channel_id=1, source_target_pairs={{0,1},{1,2},{2,3},{3,0},{4,5},{5,6},{6,7},{7,4},{8,9},{9,10},{10,1... | collective-permute-start | bytes 2359304 | tf_op jit(solution)/shard_map/ppermute | solution.py:107
  95.2 30.1 %all-to-all-start.2 = ((bf16[4,128,2048]{2,1,0:T(8,128)(2,1)}), bf16[4,128,2048]{2,1,0:T(8,128)(2,1)S(1)}, u32[]{:S(2)}, u32[]{:S(2)}) async-start(bf16[4,128,2048]{2,1,0:T(8,128)(2,1)} %bitcast.41), calls=%async_computation.2 | async-start | bytes 4194304 | tf_op jit(solution)/shard_map/all_to_all | solution.py:41
  99.4 12.0 %copy-start.1 = (bf16[192,2048]{1,0:T(8,128)(2,1)S(1)}, bf16[192,2048]{1,0:T(8,128)(2,1)}, u32[]{:S(2)}) copy-start(bf16[192,2048]{1,0:T(8,128)(2,1)} %get-tuple-element.53) | copy-start | bytes 2359300
  112.6 20.1 %collective-permute-start.9 = (bf16[192,2048]{1,0:T(8,128)(2,1)}, bf16[192,2048]{1,0:T(8,128)(2,1)}, u32[]{:S(2)}, u32[]{:S(2)}) collective-permute-start(bf16[192,2048]{1,0:T(8,128)(2,1)} %add_convert_fusion.3), channel_id=1, source_target_pairs={{0,63},{1,0},{2,1},{3,2},{4,3},{5,4},{6,5},{7,6},{8,7},{9,8},{10,9... | collective-permute-start | bytes 2359304 | tf_op jit(solution)/shard_map/ppermute | solution.py:126
  115.4 21.1 %collective-permute-start.10 = (bf16[192,2048]{1,0:T(8,128)(2,1)}, bf16[192,2048]{1,0:T(8,128)(2,1)}, u32[]{:S(2)}, u32[]{:S(2)}) collective-permute-start(bf16[192,2048]{1,0:T(8,128)(2,1)} %collective-permute-done.7), channel_id=1, source_target_pairs={{1,62},{2,63},{3,0},{0,1},{5,2},{6,3},{7,4},{4,5},{9,6},{10,7},{11... | collective-permute-start | bytes 2359304 | tf_op jit(solution)/shard_map/ppermute | solution.py:127

commit v3 on v2

--- a/solution.py
+++ b/solution.py
@@ -25,7 +25,8 @@
     n_dp = lax.axis_size("dp")
     chips_y = n_dp // CORES
     home_id = lax.axis_index("expert")
-    core = lax.axis_index("dp") % CORES
+    place = lax.axis_index("dp")
+    core = place % CORES
     gate_w, up_w = gate_weight[0], up_weight[0]
     shard, width = gate_w.shape
     rows = tokens.shape[0]
@@ -49,21 +50,33 @@
     cot = jnp.where(live, hidden_grad.T, zero).reshape(n_dp, shard, rows)
     flags = jnp.broadcast_to(flag[None], (n_dp, FLAG_ROWS, rows))
     sent = jnp.concatenate([cot, flags], axis=1)
-    w_home = jnp.concatenate([gate_w, up_w], axis=0)
-    gate_w, up_w, spread = barrier((gate_w, up_w, spread))
     gate_1 = lax.ppermute(gate_w, "expert", ahead)
     up_held = lax.ppermute(up_w, "expert", ring_step(n_exp, -1))
     sent, replica_offset = barrier((sent, replica_offset))
     offset_next = lax.ppermute(replica_offset, "expert", behind)[0]
     own_rows = exchange_y(spread).reshape(chips_y * rows, width)
 
+    gate_1, up_held, gate_w, up_w = barrier((gate_1, up_held, gate_w, up_w))
     mixed = jnp.where(offset_next == 1, up_w, gate_1)
-    mixed, up_held, own_rows = barrier((mixed, up_held, own_rows))
+    w_home = jnp.concatenate([gate_w, up_w], axis=0)
+    own_rows, w_home, _ = barrier((own_rows, w_home, mixed))
     up_2 = lax.ppermute(up_held, "expert", onward(n_exp, -1, 2))
     mixed_1 = lax.ppermute(mixed, "expert", ahead)
-    other_rows = lax.ppermute(own_rows, "dp", swap)
-    sent, other_rows = barrier((sent, other_rows))
+    sent, own_rows = barrier((sent, own_rows))
+    other_rows = lax.cond(
+        place < n_dp, lambda v: lax.ppermute(v, "dp", swap), jnp.zeros_like, own_rows
+    )
     got = lax.all_to_all(sent, "dp", split_axis=0, concat_axis=0, tiled=True)
+    nt = (((1,), (1,)), ((), ()))
+    tn = (((0,), (0,)), ((), ()))
+
+    def project(weights, x):
+        return lax.dot_general(weights, x, nt, preferred_element_type=jnp.float32)
+
+    gate_c = jnp.where(offset == 1, gate_1, mixed_1)
+    gate_c, mixed_1, got, other_rows, own_rows = barrier(
+        (gate_c, mixed_1, got, other_rows, own_rows)
+    )
     got = got.reshape(chips_y, CORES, shard + FLAG_ROWS, rows)
 
     def cotangents(which):
@@ -72,21 +85,13 @@
 
     cots = jnp.concatenate([cotangents(core), cotangents(1 - core)], axis=1)
     all_rows = jnp.concatenate([own_rows, other_rows], axis=0)
-    nt = (((1,), (1,)), ((), ()))
-    tn = (((0,), (0,)), ((), ()))
-
-    def project(weights, x):
-        return lax.dot_general(weights, x, nt, preferred_element_type=jnp.float32)
-
-    home_proj = project(w_home, all_rows)
-    mixed_1, home_proj, cots = barrier((mixed_1, home_proj, cots))
-
+    up_2, all_rows = barrier((up_2, all_rows))
+    up_c = jnp.where(offset == 1, mixed_1, up_2)
+    weights_all = jnp.concatenate([gate_w, up_w, gate_c, up_c], axis=0)
+    proj = project(weights_all, all_rows)
     on_home = cots[shard : shard + 1] > 0.5
-    gate_c = jnp.where(offset == 1, gate_1, mixed_1)
-    gate_val = jnp.where(on_home, home_proj[:shard], project(gate_c, all_rows))
-    gate_val, up_2 = barrier((gate_val, up_2))
-    up_c = jnp.where(offset == 1, mixed_1, up_2)
-    up_val = jnp.where(on_home, home_proj[shard:], project(up_c, all_rows))
+    both = jnp.where(on_home, proj[: 2 * shard], proj[2 * shard :])
+    gate_val, up_val = both[:shard], both[shard:]
     cotan = cots[:shard].astype(jnp.float32)
     sig_val = jax.nn.sigmoid(gate_val)
     dgate = (cotan * up_val * sig_val * (1.0 + gate_val * (1.0 - sig_val))).astype(jnp.bfloat16)
@@ -105,7 +110,6 @@
 
     ret_1 = lax.ppermute(first, "expert", behind)
     ret_h = lax.ppermute(second, "expert", ring_step(n_exp, 1))
-    weights_all = jnp.concatenate([w_home, gate_c, up_c], axis=0)
     both_terms = jnp.concatenate([home_terms, copy_terms], axis=0)
     half = chips_y * rows
 
@@ -119,7 +123,7 @@
     dx_pair, home_terms = barrier((dx_pair, home_terms))
     dx_parts = exchange_y(dx_pair.reshape(chips_y, rows, width))
 
-    home_part = jnp.dot(home_terms, all_rows, preferred_element_type=jnp.float32)
+    home_part = jnp.dot(home_terms, all_rows, preferred_element_type=jnp.float32).astype(jnp.bfloat16)
     ret_1, ret_h, home_part = barrier((ret_1, ret_h, home_part))
     sum_g = kept.astype(jnp.float32) + jnp.where(offset_next == 2, ret_1, zero).astype(jnp.float32)
     sum_g, ret_h, home_part = barrier((sum_g.astype(jnp.bfloat16), ret_h, home_part))
@@ -127,9 +131,9 @@
     ret_u = lax.ppermute(ret_h, "expert", onward(n_exp, 1, -2))
     input_grad = jnp.sum(dx_parts.astype(jnp.float32), axis=0).astype(jnp.bfloat16)
     home_part, ret_1, input_grad, ret_g, ret_u = barrier((home_part, ret_1, input_grad, ret_g, ret_u))
-    gate_grad = (home_part[:shard] + ret_g.astype(jnp.float32)).astype(jnp.bfloat16)
+    gate_grad = (home_part[:shard].astype(jnp.float32) + ret_g.astype(jnp.float32)).astype(jnp.bfloat16)
     up_grad = (
-        home_part[shard:]
+        home_part[shard:].astype(jnp.float32)
         + jnp.where(offset_next == 1, ret_1, zero).astype(jnp.float32)
         + ret_u.astype(jnp.float32)
     ).astype(jnp.bfloat16)

time: 143 us -> 137 us (0.958)
  local copies, waits for them, and re-layouts: 9.57 us -> 4.31 us
  matrix products: 19.3 us -> 14.5 us
  starting transfers between devices: 53.5 us -> 57.4 us
  other arithmetic: 18.1 us -> 21.4 us
  waiting for transfers between devices: 37.5 us -> 35 us
    ppermute x1, waiting for transfers between devices: 6.31 us -> 0.01 us  [local(): gate_1 = lax.ppermute(gate_w, 'expert', ahead)]
    ppermute x1, waiting for transfers between devices: 0.01 us -> 4.14 us  [local(): lax.ppermute(v, 'dp', swap)]
    dot_general x3 -> x1, matrix products: 7.57 us -> 3.44 us  [project(): return lax.dot_general(weights, x, nt, preferred_element_type=jnp.float32)]
    ppermute x1, waiting for transfers between devices: 6.06 us -> 2.71 us  [local(): mixed_1 = lax.ppermute(mixed, 'expert', ahead)]
    concatenate x1, local copies, waits for them, and re-layouts: 3.15 us -> 0.02 us  [local(): cots = jnp.concatenate([cotangents(core), cotangents(1 - core)], axis=1)]
    ppermute x1, starting transfers between devices: 2.72 us -> 5.36 us  [local(): dx_in = lax.ppermute(dx_oth, 'dp', swap)]
    concatenate x1, other arithmetic: 0.04 us -> 2.32 us  [local(): all_rows = jnp.concatenate([own_rows, other_rows], axis=0)]
    unnamed x18, local copies, waits for them, and re-layouts: 3.43 us -> 1.34 us
  transfers between devices with their start and end apart: 14 -> 14, of which waited for: 9 -> 9; matrix products, arithmetic and copies ran while one was open for 22% -> 19% of each run, Pallas kernels for 0% -> 0%
where the time goes in v3:
time: 137 us; the launch traced here: 136 us
  starting transfers between devices  57.4 us (42%)
  waiting for transfers between devices  35 us (26%)
  other arithmetic  21.4 us (16%)
  matrix products  14.5 us (11%)
  local copies, waits for them, and re-layouts  4.31 us (3%)
  between operations  2.9 us (2%)
    ppermute x1, starting transfers between devices, local(): offset_next = lax.ppermute(replica_offset, 'expert', behind)[0]  10.7 us
    all_to_all x2, waiting for transfers between devices, exchange_y(): lax.all_to_all(parts, 'dp', split_axis=0, concat_axis=0, axis_index_group...  8.45 us
    all_to_all x2, starting transfers between devices, exchange_y(): lax.all_to_all(parts, 'dp', split_axis=0, concat_axis=0, axis_index_group...  8.1 us
    ppermute x1, waiting for transfers between devices, local(): ret_g = lax.ppermute(sum_g, 'expert', behind)  8.05 us
    all_to_all x1, starting transfers between devices, local(): got = lax.all_to_all(sent, 'dp', split_axis=0, concat_axis=0, tiled=True)  5.81 us
    ppermute x1, starting transfers between devices, local(): ret_1 = lax.ppermute(first, 'expert', behind)  5.64 us
    dot_general x1, matrix products, local(): jnp.dot(home_terms, all_rows, preferred_element_type=jnp.float32)  5.37 us
    ppermute x1, starting transfers between devices, local(): dx_in = lax.ppermute(dx_oth, 'dp', swap)  5.36 us
  transfers between devices with their start and end apart: 14, of which 9 were waited for; matrix products, arithmetic and copies ran while one was open for 19% of the time, Pallas kernels for 0%

profile of v3, /device:TPU:1, one launch (start us, length us, event | category | flops | bytes accessed | tf_op | source)
XLA Modules:
  0.0 135.6 jit_solution(5960448873787872055)
XLA Ops:
  0.6 4.0 %collective-permute-start.1 = (bf16[192,2048]{1,0:T(8,128)(2,1)}, bf16[192,2048]{1,0:T(8,128)(2,1)S(1)}, u32[]{:S(2)}, u32[]{:S(2)}) collective-permute-start(bf16[192,2048]{1,0:T(8,128)(2,1)} %bitcast.45), channel_id=1, source_target_pairs={{0,1},{1,2},{2,3},{3,4},{4,5},{5,6},{6,7},{7,8},{8,9},{9,10},{10,1... | collective-permute-start | bytes 2359304 | tf_op jit(solution)/shard_map/ppermute | solution.py:53
  4.6 4.7 %collective-permute-start.2 = (bf16[192,2048]{1,0:T(8,128)(2,1)}, bf16[192,2048]{1,0:T(8,128)(2,1)}, u32[]{:S(2)}, u32[]{:S(2)}) collective-permute-start(bf16[192,2048]{1,0:T(8,128)(2,1)} %bitcast.40), channel_id=1, source_target_pairs={{0,3},{1,0},{2,1},{3,2},{4,7},{5,4},{6,5},{7,6},{8,11},{9,8},{10,9... | collective-permute-start | bytes 2359304 | tf_op jit(solution)/shard_map/ppermute | solution.py:54
  9.3 2.6 %broadcast_in_dim.76 = bf16[4,128,2048]{2,1,0:T(8,128)(2,1)} broadcast(bf16[128,2048]{1,0:T(8,128)(2,1)} %param.9), dimensions={1,2} | broadcast | bytes 2621440 | tf_op jit(solution)/shard_map/broadcast_in_dim | solution.py:47
  12.0 4.3 %all-to-all-start = ((bf16[4,128,2048]{2,1,0:T(8,128)(2,1)}), bf16[4,128,2048]{2,1,0:T(8,128)(2,1)S(1)}, u32[]{:S(2)}, u32[]{:S(2)}) async-start(bf16[4,128,2048]{2,1,0:T(8,128)(2,1)} %broadcast_in_dim.76), calls=%async_computation | async-start | bytes 4194304 | tf_op jit(solution)/shard_map/all_to_all | solution.py:42
  20.4 10.7 %collective-permute-start.3 = (s32[1]{0:T(128)}, s32[1]{0:T(128)}, u32[]{:S(2)}, u32[]{:S(2)}) collective-permute-start(s32[1]{0:T(128)} %param.13), channel_id=1, source_target_pairs={{0,63},{1,0},{2,1},{3,2},{4,3},{5,4},{6,5},{7,6},{8,7},{9,8},{10,9... | collective-permute-start | bytes 20 | tf_op jit(solution)/shard_map/ppermute | solution.py:56
  33.6 1.9 %collective-permute-start.4 = (bf16[192,2048]{1,0:T(8,128)(2,1)}, bf16[192,2048]{1,0:T(8,128)(2,1)}, u32[]{:S(2)}, u32[]{:S(2)}) collective-permute-start(bf16[192,2048]{1,0:T(8,128)(2,1)} %broadcast_select_fusion.3), channel_id=1, source_target_pairs={{0,1},{1,2},{2,3},{3,4},{4,5},{5,6},{6,7},{7,8},{8,9},{9,10},{10,1... | collective-permute-start | bytes 2359304 | tf_op jit(solution)/shard_map/ppermute | solution.py:64
  36.2 1.9 %collective-permute-start.5 = (bf16[192,2048]{1,0:T(8,128)(2,1)}, bf16[192,2048]{1,0:T(8,128)(2,1)}, u32[]{:S(2)}, u32[]{:S(2)}) collective-permute-start(bf16[192,2048]{1,0:T(8,128)(2,1)} %collective-permute-done.2), channel_id=1, source_target_pairs={{3,2},{0,3},{1,4},{2,5},{7,6},{4,7},{5,8},{6,9},{11,10},{8,11},{9,... | collective-permute-start | bytes 2359304 | tf_op jit(solution)/shard_map/ppermute | solution.py:63
  38.2 3.0 %all-to-all-done = bf16[4,128,2048]{2,1,0:T(8,128)(2,1)S(1)} async-done(((bf16[4,128,2048]{2,1,0:T(8,128)(2,1)}), bf16[4,128,2048]{2,1,0:T(8,128)(2,1)S(1)}, u32[]{:S(2)}, u32[]{:S(2)}) %all-to-all-start) | async-done | bytes 2097184 | tf_op jit(solution)/shard_map/all_to_all | solution.py:42
  41.1 5.8 %all-to-all-start.1 = ((bf16[8,208,128]{2,1,0:T(8,128)(2,1)}), bf16[8,208,128]{2,1,0:T(8,128)(2,1)S(1)}, u32[]{:S(2)}, u32[]{:S(2)}) async-start(bf16[8,208,128]{2,1,0:T(8,128)(2,1)} %pad_maximum_fusion.3), calls=%async_computation.1 | async-start | bytes 851968 | tf_op jit(solution)/shard_map/all_to_all | solution.py:69
  46.9 6.2 %conditional.1 = (bf16[512,2048]{1,0:T(8,128)(2,1)}) conditional(s32[]{:T(128)} %convert_element_type.63, () %tuple.31, bf16[512,2048]{1,0:T(8,128)(2,1)S(1)} %bitcast.35), branch_computations={%region_0.1_spmd, %region_1.2_spmd} | conditional | bytes 8388656 | solution.py:66
  46.9 2.0 %collective-permute-start = (bf16[512,2048]{1,0:T(8,128)(2,1)S(1)}, bf16[512,2048]{1,0:T(8,128)(2,1)}, u32[]{:S(2)}, u32[]{:S(2)}) collective-permute-start(bf16[512,2048]{1,0:T(8,128)(2,1)S(1)} %param.1), channel_id=1, source_target_pairs={{0,64},{64,0},{128,192},{192,128},{256,320},{320,256},{384,448},{4... | collective-permute-start | bytes 6291464 | tf_op jit(solution)/shard_map/cond/branch_1_fun/ppermute | solution.py:67
  49.0 4.1 %collective-permute-done = bf16[512,2048]{1,0:T(8,128)(2,1)} collective-permute-done((bf16[512,2048]{1,0:T(8,128)(2,1)S(1)}, bf16[512,2048]{1,0:T(8,128)(2,1)}, u32[]{:S(2)}, u32[]{:S(2)}) %collective-permute-start) | collective-permute-done | bytes 2097184 | tf_op jit(solution)/shard_map/cond/branch_1_fun/ppermute | solution.py:67
  53.1 2.7 %collective-permute-done.4 = bf16[192,2048]{1,0:T(8,128)(2,1)} collective-permute-done((bf16[192,2048]{1,0:T(8,128)(2,1)}, bf16[192,2048]{1,0:T(8,128)(2,1)}, u32[]{:S(2)}, u32[]{:S(2)}) %collective-permute-start.4) | collective-permute-done | bytes 786464 | tf_op jit(solution)/shard_map/ppermute | solution.py:64
  55.8 2.1 %broadcast_select_fusion.7 = bf16[192,2048]{1,0:T(8,128)(2,1)} fusion(bf16[192,2048]{1,0:T(8,128)(2,1)S(1)} %collective-permute-done.1, bf16[192,2048]{1,0:T(8,128)(2,1)} %collective-permute-done.4, pred[]{:T(512)} %bitcast), kind=kLoop, calls=%fused_computation.31 | loop fusion | flops 393216 | bytes 2359297 | tf_op jit(solution)/shard_map/jit(_where)/select_n | solution.py:76
  58.1 2.3 %pad_maximum_fusion = bf16[1024,2048]{1,0:T(8,128)(2,1)S(1)} fusion(bf16[512,2048]{1,0:T(8,128)(2,1)} %get-tuple-element.90, bf16[512,2048]{1,0:T(8,128)(2,1)S(1)} %bitcast.36), kind=kLoop, calls=%fused_computation | loop fusion | flops 8388608 | bytes 8388608 | tf_op jit(solution)/shard_map/concatenate | solution.py:87
  62.3 3.4 %fusion.10 = f32[768,1024]{1,0:T(8,128)S(1)} fusion(bf16[1024,2048]{1,0:T(8,128)(2,1)S(1)} %pad_maximum_fusion, bf16[192,2048]{1,0:T(8,128)(2,1)S(1)} %broadcast_select_fusion.6, bf16[192,2048]{1,0:T(8,128)(2,1)S(1)} %copy-done.3, bf16[192,2048]{1,0:T(8,128)(2,1)S(1)} %bitcast.42, bf16[192,2048]{1,0:T(8,128)(2,1)S(1)} %bitcast.46), kind=kOutput, calls=%fused_computation.43 | convolution fusion | flops 3233808384 | bytes 10485760 | tf_op jit(solution)/shard_map/dot_general | solution.py:74
  70.0 2.0 %convolution_convert_fusion = bf16[512,2048]{1,0:T(8,128)(2,1)S(1)} fusion(bf16[768,1024]{1,0:T(8,128)(2,1)S(1)} %constant_dynamic-update-slice_fusion, bf16[192,2048]{1,0:T(8,128)(2,1)S(1)} %broadcast_select_fusion.6, bf16[192,2048]{1,0:T(8,128)(2,1)S(1)} %copy-done.3, bf16[192,2048]{1,0:T(8,128)(2,1)S(1)} %bitcast.43, bf16[192,2048]{1,0:T(8,128)(2,1)S(1)} %bitcast.47), kind=kOutput, calls=%fused_computation.3 | convolution fusion | flops 1624244224 | bytes 6029312 | tf_op jit(solution)/shard_map/dot_general | solution.py:117
  72.0 5.4 %collective-permute-start.8 = (bf16[512,2048]{1,0:T(8,128)(2,1)S(1)}, bf16[512,2048]{1,0:T(8,128)(2,1)S(1)}, u32[]{:S(2)}, u32[]{:S(2)}) collective-permute-start(bf16[512,2048]{1,0:T(8,128)(2,1)S(1)} %convolution_convert_fusion), channel_id=1, source_target_pairs={{0,64},{64,0},{128,192},{192,128},{256,320},{320,256},{384,448},{4... | collective-permute-start | bytes 6291464 | tf_op jit(solution)/shard_map/ppermute | solution.py:120
  78.0 5.6 %collective-permute-start.6 = (bf16[192,2048]{1,0:T(8,128)(2,1)}, bf16[192,2048]{1,0:T(8,128)(2,1)}, u32[]{:S(2)}, u32[]{:S(2)}) collective-permute-start(bf16[192,2048]{1,0:T(8,128)(2,1)} %get-tuple-element.60), channel_id=1, source_target_pairs={{0,63},{1,0},{2,1},{3,2},{4,3},{5,4},{6,5},{7,6},{8,7},{9,8},{10,9... | collective-permute-start | bytes 2359304 | tf_op jit(solution)/shard_map/ppermute | solution.py:111
  83.7 1.9 %collective-permute-start.7 = (bf16[192,2048]{1,0:T(8,128)(2,1)}, bf16[192,2048]{1,0:T(8,128)(2,1)}, u32[]{:S(2)}, u32[]{:S(2)}) collective-permute-start(bf16[192,2048]{1,0:T(8,128)(2,1)} %get-tuple-element.61), channel_id=1, source_target_pairs={{0,1},{1,2},{2,3},{3,0},{4,5},{5,6},{6,7},{7,4},{8,9},{9,10},{10,1... | collective-permute-start | bytes 2359304 | tf_op jit(solution)/shard_map/ppermute | solution.py:112
  87.5 2.1 %add_convert_fusion = bf16[512,2048]{1,0:T(8,128)(2,1)} fusion(f32[512,2048]{1,0:T(8,128)S(1)} %fusion.8, bf16[512,2048]{1,0:T(8,128)(2,1)S(1)} %collective-permute-done.8), kind=kLoop, calls=%fused_computation.1 | loop fusion | flops 3145728 | bytes 8388608 | tf_op jit(solution)/shard_map/convert_element_type | solution.py:122
  89.6 3.8 %all-to-all-start.2 = ((bf16[4,128,2048]{2,1,0:T(8,128)(2,1)}), bf16[4,128,2048]{2,1,0:T(8,128)(2,1)S(1)}, u32[]{:S(2)}, u32[]{:S(2)}) async-start(bf16[4,128,2048]{2,1,0:T(8,128)(2,1)} %bitcast.37), calls=%async_computation.2 | async-start | bytes 4194304 | tf_op jit(solution)/shard_map/all_to_all | solution.py:42
  93.4 5.4 %convolution_convert_fusion.1 = bf16[384,2048]{1,0:T(8,128)(2,1)} fusion(bf16[384,1024]{1,0:T(8,128)(2,1)} %copy-done.1, bf16[1024,2048]{1,0:T(8,128)(2,1)} %copy-done), kind=kOutput, calls=%fused_computation.4 | convolution fusion | flops 1611399168 | bytes 6553600 | tf_op jit(solution)/shard_map/dot_general | solution.py:126
  98.8 2.1 %collective-permute-done.6 = bf16[192,2048]{1,0:T(8,128)(2,1)} collective-permute-done((bf16[192,2048]{1,0:T(8,128)(2,1)}, bf16[192,2048]{1,0:T(8,128)(2,1)}, u32[]{:S(2)}, u32[]{:S(2)}) %collective-permute-start.6) | collective-permute-done | bytes 786464 | tf_op jit(solution)/shard_map/ppermute | solution.py:111
  100.9 5.0 %collective-permute-done.7 = bf16[192,2048]{1,0:T(8,128)(2,1)} collective-permute-done((bf16[192,2048]{1,0:T(8,128)(2,1)}, bf16[192,2048]{1,0:T(8,128)(2,1)}, u32[]{:S(2)}, u32[]{:S(2)}) %collective-permute-start.7) | collective-permute-done | bytes 786464 | tf_op jit(solution)/shard_map/ppermute | solution.py:112
  105.9 2.3 %add_convert_fusion.3 = bf16[192,2048]{1,0:T(8,128)(2,1)} fusion(bf16[192,2048]{1,0:T(8,128)(2,1)S(1)} %get-tuple-element.59, bf16[192,2048]{1,0:T(8,128)(2,1)} %collective-permute-done.6, pred[]{:T(512)} %bitcast.13), kind=kLoop, calls=%fused_computation.9 | loop fusion | flops 1966080 | bytes 2359297 | tf_op jit(solution)/shard_map/convert_element_type | solution.py:129
  108.2 2.4 %collective-permute-start.9 = (bf16[192,2048]{1,0:T(8,128)(2,1)}, bf16[192,2048]{1,0:T(8,128)(2,1)S(1)}, u32[]{:S(2)}, u32[]{:S(2)}) collective-permute-start(bf16[192,2048]{1,0:T(8,128)(2,1)} %add_convert_fusion.3), channel_id=1, source_target_pairs={{0,63},{1,0},{2,1},{3,2},{4,3},{5,4},{6,5},{7,6},{8,7},{9,8},{10,9... | collective-permute-start | bytes 2359304 | tf_op jit(solution)/shard_map/ppermute | solution.py:130
  110.7 2.9 %collective-permute-start.10 = (bf16[192,2048]{1,0:T(8,128)(2,1)}, bf16[192,2048]{1,0:T(8,128)(2,1)}, u32[]{:S(2)}, u32[]{:S(2)}) collective-permute-start(bf16[192,2048]{1,0:T(8,128)(2,1)} %collective-permute-done.7), channel_id=1, source_target_pairs={{1,62},{2,63},{3,0},{0,1},{5,2},{6,3},{7,4},{4,5},{9,6},{10,7},{11... | collective-permute-start | bytes 2359304 | tf_op jit(solution)/shard_map/ppermute | solution.py:131
  113.5 5.5 %all-to-all-done.2 = bf16[4,128,2048]{2,1,0:T(8,128)(2,1)S(1)} async-done(((bf16[4,128,2048]{2,1,0:T(8,128)(2,1)}), bf16[4,128,2048]{2,1,0:T(8,128)(2,1)S(1)}, u32[]{:S(2)}, u32[]{:S(2)}) %all-to-all-start.2) | async-done | bytes 2097184 | tf_op jit(solution)/shard_map/all_to_all | solution.py:42
  120.3 8.1 %collective-permute-done.9 = bf16[192,2048]{1,0:T(8,128)(2,1)S(1)} collective-permute-done((bf16[192,2048]{1,0:T(8,128)(2,1)}, bf16[192,2048]{1,0:T(8,128)(2,1)S(1)}, u32[]{:S(2)}, u32[]{:S(2)}) %collective-permute-start.9) | collective-permute-done | bytes 786464 | tf_op jit(solution)/shard_map/ppermute | solution.py:130
  128.4 3.7 %collective-permute-done.10 = bf16[192,2048]{1,0:T(8,128)(2,1)} collective-permute-done((bf16[192,2048]{1,0:T(8,128)(2,1)}, bf16[192,2048]{1,0:T(8,128)(2,1)}, u32[]{:S(2)}, u32[]{:S(2)}) %collective-permute-start.10) | collective-permute-done | bytes 786464 | tf_op jit(solution)/shard_map/ppermute | solution.py:131
  132.0 3.5 %fusion.6 = (bf16[1,192,2048]{2,1,0:T(8,128)(2,1)}, bf16[1,192,2048]{2,1,0:T(8,128)(2,1)}) fusion(bf16[192,2048]{1,0:T(8,128)(2,1)} %collective-permute-done.10, bf16[192,2048]{1,0:T(8,128)(2,1)} %collective-permute-done.6, bf16[384,2048]{1,0:T(8,128)(2,1)} %convolution_convert_fusion.1, pred[]{:T(512)} %bitcast.5, ...), kind=kLoop, calls=%fused_computation.18 | loop fusion | flops 4325376 | bytes 5505025 | tf_op jit(solution)/shard_map/broadcast_in_dim | solution.py:140
  (44 shorter events, 15.3 us)
Async XLA Ops:
  0.6 32.0 %collective-permute-start.1 = (bf16[192,2048]{1,0:T(8,128)(2,1)}, bf16[192,2048]{1,0:T(8,128)(2,1)S(1)}, u32[]{:S(2)}, u32[]{:S(2)}) collective-permute-start(bf16[192,2048]{1,0:T(8,128)(2,1)} %bitcast.45), channel_id=1, source_target_pairs={{0,1},{1,2},{2,3},{3,4},{4,5},{5,6},{6,7},{7,8},{8,9},{9,10},{10,1... | collective-permute-start | bytes 2359304 | tf_op jit(solution)/shard_map/ppermute | solution.py:53
  4.6 11.7 %copy-start.5 = (s32[2]{0:T(128)S(1)}, s32[2]{0:T(128)}, u32[]{:S(2)}) copy-start(s32[2]{0:T(128)} %param.15) | copy-start | bytes 28
  4.6 28.1 %collective-permute-start.2 = (bf16[192,2048]{1,0:T(8,128)(2,1)}, bf16[192,2048]{1,0:T(8,128)(2,1)}, u32[]{:S(2)}, u32[]{:S(2)}) collective-permute-start(bf16[192,2048]{1,0:T(8,128)(2,1)} %bitcast.40), channel_id=1, source_target_pairs={{0,3},{1,0},{2,1},{3,2},{4,7},{5,4},{6,5},{7,6},{8,11},{9,8},{10,9... | collective-permute-start | bytes 2359304 | tf_op jit(solution)/shard_map/ppermute | solution.py:54
  12.0 6.5 %copy-start.6 = (s32[2]{0:T(128)S(1)}, s32[2]{0:T(128)}, u32[]{:S(2)}) copy-start(s32[2]{0:T(128)} %param.14) | copy-start | bytes 28
  12.0 29.2 %all-to-all-start = ((bf16[4,128,2048]{2,1,0:T(8,128)(2,1)}), bf16[4,128,2048]{2,1,0:T(8,128)(2,1)S(1)}, u32[]{:S(2)}, u32[]{:S(2)}) async-start(bf16[4,128,2048]{2,1,0:T(8,128)(2,1)} %broadcast_in_dim.76), calls=%async_computation | async-start | bytes 4194304 | tf_op jit(solution)/shard_map/all_to_all | solution.py:42
  20.4 11.6 %collective-permute-start.3 = (s32[1]{0:T(128)}, s32[1]{0:T(128)}, u32[]{:S(2)}, u32[]{:S(2)}) collective-permute-start(s32[1]{0:T(128)} %param.13), channel_id=1, source_target_pairs={{0,63},{1,0},{2,1},{3,2},{4,3},{5,4},{6,5},{7,6},{8,7},{9,8},{10,9... | collective-permute-start | bytes 20 | tf_op jit(solution)/shard_map/ppermute | solution.py:56
  33.6 22.2 %collective-permute-start.4 = (bf16[192,2048]{1,0:T(8,128)(2,1)}, bf16[192,2048]{1,0:T(8,128)(2,1)}, u32[]{:S(2)}, u32[]{:S(2)}) collective-permute-start(bf16[192,2048]{1,0:T(8,128)(2,1)} %broadcast_select_fusion.3), channel_id=1, source_target_pairs={{0,1},{1,2},{2,3},{3,4},{4,5},{5,6},{6,7},{7,8},{8,9},{9,10},{10,1... | collective-permute-start | bytes 2359304 | tf_op jit(solution)/shard_map/ppermute | solution.py:64
  36.2 24.2 %collective-permute-start.5 = (bf16[192,2048]{1,0:T(8,128)(2,1)}, bf16[192,2048]{1,0:T(8,128)(2,1)}, u32[]{:S(2)}, u32[]{:S(2)}) collective-permute-start(bf16[192,2048]{1,0:T(8,128)(2,1)} %collective-permute-done.2), channel_id=1, source_target_pairs={{3,2},{0,3},{1,4},{2,5},{7,6},{4,7},{5,8},{6,9},{11,10},{8,11},{9,... | collective-permute-start | bytes 2359304 | tf_op jit(solution)/shard_map/ppermute | solution.py:63
  41.1 16.8 %all-to-all-start.1 = ((bf16[8,208,128]{2,1,0:T(8,128)(2,1)}), bf16[8,208,128]{2,1,0:T(8,128)(2,1)S(1)}, u32[]{:S(2)}, u32[]{:S(2)}) async-start(bf16[8,208,128]{2,1,0:T(8,128)(2,1)} %pad_maximum_fusion.3), calls=%async_computation.1 | async-start | bytes 851968 | tf_op jit(solution)/shard_map/all_to_all | solution.py:69
  46.9 6.2 %collective-permute-start = (bf16[512,2048]{1,0:T(8,128)(2,1)S(1)}, bf16[512,2048]{1,0:T(8,128)(2,1)}, u32[]{:S(2)}, u32[]{:S(2)}) collective-permute-start(bf16[512,2048]{1,0:T(8,128)(2,1)S(1)} %param.1), channel_id=1, source_target_pairs={{0,64},{64,0},{128,192},{192,128},{256,320},{320,256},{384,448},{4... | collective-permute-start | bytes 6291464 | tf_op jit(solution)/shard_map/cond/branch_1_fun/ppermute | solution.py:67
  58.0 4.2 %copy-start.2 = (bf16[1,192,2048]{2,1,0:T(8,128)(2,1)S(1)}, bf16[1,192,2048]{2,1,0:T(8,128)(2,1)}, u32[]{:S(2)}) copy-start(bf16[1,192,2048]{2,1,0:T(8,128)(2,1)} %param.12) | copy-start | bytes 2359300
  58.1 4.2 %copy-start.3 = (bf16[192,2048]{1,0:T(8,128)(2,1)S(1)}, bf16[192,2048]{1,0:T(8,128)(2,1)}, u32[]{:S(2)}) copy-start(bf16[192,2048]{1,0:T(8,128)(2,1)} %broadcast_select_fusion.7) | copy-start | bytes 2359300
  58.1 4.2 %copy-start.4 = (bf16[1,192,2048]{2,1,0:T(8,128)(2,1)S(1)}, bf16[1,192,2048]{2,1,0:T(8,128)(2,1)}, u32[]{:S(2)}) copy-start(bf16[1,192,2048]{2,1,0:T(8,128)(2,1)} %param.11) | copy-start | bytes 2359300
  60.4 6.4 %copy-start = (bf16[1024,2048]{1,0:T(8,128)(2,1)}, bf16[1024,2048]{1,0:T(8,128)(2,1)S(1)}, u32[]{:S(2)}) copy-start(bf16[1024,2048]{1,0:T(8,128)(2,1)S(1)} %pad_maximum_fusion) | copy-start | bytes 12582916
  66.7 3.1 %copy-start.1 = (bf16[384,1024]{1,0:T(8,128)(2,1)}, bf16[384,1024]{1,0:T(8,128)(2,1)S(1)}, u32[]{:S(2)}) copy-start(bf16[384,1024]{1,0:T(8,128)(2,1)S(1)} %get-tuple-element.66) | copy-start | bytes 2359300
  72.0 15.5 %collective-permute-start.8 = (bf16[512,2048]{1,0:T(8,128)(2,1)S(1)}, bf16[512,2048]{1,0:T(8,128)(2,1)S(1)}, u32[]{:S(2)}, u32[]{:S(2)}) collective-permute-start(bf16[512,2048]{1,0:T(8,128)(2,1)S(1)} %convolution_convert_fusion), channel_id=1, source_target_pairs={{0,64},{64,0},{128,192},{192,128},{256,320},{320,256},{384,448},{4... | collective-permute-start | bytes 6291464 | tf_op jit(solution)/shard_map/ppermute | solution.py:120
  78.0 22.9 %collective-permute-start.6 = (bf16[192,2048]{1,0:T(8,128)(2,1)}, bf16[192,2048]{1,0:T(8,128)(2,1)}, u32[]{:S(2)}, u32[]{:S(2)}) collective-permute-start(bf16[192,2048]{1,0:T(8,128)(2,1)} %get-tuple-element.60), channel_id=1, source_target_pairs={{0,63},{1,0},{2,1},{3,2},{4,3},{5,4},{6,5},{7,6},{8,7},{9,8},{10,9... | collective-permute-start | bytes 2359304 | tf_op jit(solution)/shard_map/ppermute | solution.py:111
  83.7 22.3 %collective-permute-start.7 = (bf16[192,2048]{1,0:T(8,128)(2,1)}, bf16[192,2048]{1,0:T(8,128)(2,1)}, u32[]{:S(2)}, u32[]{:S(2)}) collective-permute-start(bf16[192,2048]{1,0:T(8,128)(2,1)} %get-tuple-element.61), channel_id=1, source_target_pairs={{0,1},{1,2},{2,3},{3,0},{4,5},{5,6},{6,7},{7,4},{8,9},{9,10},{10,1... | collective-permute-start | bytes 2359304 | tf_op jit(solution)/shard_map/ppermute | solution.py:112
  89.6 29.4 %all-to-all-start.2 = ((bf16[4,128,2048]{2,1,0:T(8,128)(2,1)}), bf16[4,128,2048]{2,1,0:T(8,128)(2,1)S(1)}, u32[]{:S(2)}, u32[]{:S(2)}) async-start(bf16[4,128,2048]{2,1,0:T(8,128)(2,1)} %bitcast.37), calls=%async_computation.2 | async-start | bytes 4194304 | tf_op jit(solution)/shard_map/all_to_all | solution.py:42
  108.2 20.1 %collective-permute-start.9 = (bf16[192,2048]{1,0:T(8,128)(2,1)}, bf16[192,2048]{1,0:T(8,128)(2,1)S(1)}, u32[]{:S(2)}, u32[]{:S(2)}) collective-permute-start(bf16[192,2048]{1,0:T(8,128)(2,1)} %add_convert_fusion.3), channel_id=1, source_target_pairs={{0,63},{1,0},{2,1},{3,2},{4,3},{5,4},{6,5},{7,6},{8,7},{9,8},{10,9... | collective-permute-start | bytes 2359304 | tf_op jit(solution)/shard_map/ppermute | solution.py:130
  110.7 21.4 %collective-permute-start.10 = (bf16[192,2048]{1,0:T(8,128)(2,1)}, bf16[192,2048]{1,0:T(8,128)(2,1)}, u32[]{:S(2)}, u32[]{:S(2)}) collective-permute-start(bf16[192,2048]{1,0:T(8,128)(2,1)} %collective-permute-done.7), channel_id=1, source_target_pairs={{1,62},{2,63},{3,0},{0,1},{5,2},{6,3},{7,4},{4,5},{9,6},{10,7},{11... | collective-permute-start | bytes 2359304 | tf_op jit(solution)/shard_map/ppermute | solution.py:131

commit v4 on v3

--- a/solution.py
+++ b/solution.py
@@ -103,9 +103,8 @@
     copy_g, copy_u = copy_part[:shard], copy_part[shard:]
     first = jnp.where(offset == 1, copy_u, copy_g)
     second = jnp.where(offset == 2, copy_u, zero)
-    kept = jnp.where(offset == 1, copy_g, zero)
-    first, second, kept, home_terms, copy_terms = barrier(
-        (first, second, kept, home_terms, copy_terms)
+    first, second, copy_g, home_terms, copy_terms = barrier(
+        (first, second, copy_g, home_terms, copy_terms)
     )
 
     ret_1 = lax.ppermute(first, "expert", behind)
@@ -124,14 +123,16 @@
     dx_parts = exchange_y(dx_pair.reshape(chips_y, rows, width))
 
     home_part = jnp.dot(home_terms, all_rows, preferred_element_type=jnp.float32).astype(jnp.bfloat16)
-    ret_1, ret_h, home_part = barrier((ret_1, ret_h, home_part))
-    sum_g = kept.astype(jnp.float32) + jnp.where(offset_next == 2, ret_1, zero).astype(jnp.float32)
-    sum_g, ret_h, home_part = barrier((sum_g.astype(jnp.bfloat16), ret_h, home_part))
+    ret_1, home_part = barrier((ret_1, home_part))
+    sum_g = jnp.where(offset == 1, copy_g, zero).astype(jnp.float32) + jnp.where(offset_next == 2, ret_1, zero).astype(jnp.float32)
+    sum_g, home_part = barrier((sum_g.astype(jnp.bfloat16), home_part))
     ret_g = lax.ppermute(sum_g, "expert", behind)
+    ret_h, _ = barrier((ret_h, sum_g))
     ret_u = lax.ppermute(ret_h, "expert", onward(n_exp, 1, -2))
     input_grad = jnp.sum(dx_parts.astype(jnp.float32), axis=0).astype(jnp.bfloat16)
-    home_part, ret_1, input_grad, ret_g, ret_u = barrier((home_part, ret_1, input_grad, ret_g, ret_u))
+    home_part, input_grad, ret_g = barrier((home_part, input_grad, ret_g))
     gate_grad = (home_part[:shard].astype(jnp.float32) + ret_g.astype(jnp.float32)).astype(jnp.bfloat16)
+    gate_grad, home_part, ret_1, ret_u = barrier((gate_grad, home_part, ret_1, ret_u))
     up_grad = (
         home_part[shard:].astype(jnp.float32)
         + jnp.where(offset_next == 1, ret_1, zero).astype(jnp.float32)

time: 137 us -> 135 us (0.985)
  waiting for transfers between devices: 35 us -> 28.6 us
  starting transfers between devices: 57.4 us -> 61.5 us
    ppermute x1, starting transfers between devices: 2.41 us -> 8.56 us  [local(): ret_g = lax.ppermute(sum_g, 'expert', behind)]
    ppermute x1, waiting for transfers between devices: 5.01 us -> 0.01 us  [local(): ret_h = lax.ppermute(second, 'expert', ring_step(n_exp, 1))]
    ppermute x1, waiting for transfers between devices: 8.05 us -> 5.16 us  [local(): ret_g = lax.ppermute(sum_g, 'expert', behind)]
    slice x0 -> x1, other arithmetic: none -> 1.45 us  [local(): copy_g, copy_u = (copy_part[:shard], copy_part[shard:])]
    convert_element_type x1 -> x2, other arithmetic: 2.29 us -> 2.81 us  [the longest x1 2.52 us: local(): (home_part[:shard].astype(jnp.float32) + ret_g.astype(jnp.float32)).astyp...]
  transfers between devices with their start and end apart: 14 -> 14, of which waited for: 9 -> 8; matrix products, arithmetic and copies ran while one was open for 19% -> 20% of each run, Pallas kernels for 0% -> 0%
where the time goes in v4:
time: 135 us; the launch traced here: 134 us
  starting transfers between devices  61.5 us (46%)
  waiting for transfers between devices  28.6 us (21%)
  other arithmetic  22.6 us (17%)
  matrix products  14.4 us (11%)
  local copies, waits for them, and re-layouts  4.3 us (3%)
  between operations  2.9 us (2%)
    ppermute x1, starting transfers between devices, local(): offset_next = lax.ppermute(replica_offset, 'expert', behind)[0]  10.7 us
    all_to_all x2, waiting for transfers between devices, exchange_y(): lax.all_to_all(parts, 'dp', split_axis=0, concat_axis=0, axis_index_group...  9.5 us
    ppermute x1, starting transfers between devices, local(): ret_g = lax.ppermute(sum_g, 'expert', behind)  8.56 us
    all_to_all x2, starting transfers between devices, exchange_y(): lax.all_to_all(parts, 'dp', split_axis=0, concat_axis=0, axis_index_group...  8.1 us
    all_to_all x1, starting transfers between devices, local(): got = lax.all_to_all(sent, 'dp', split_axis=0, concat_axis=0, tiled=True)  5.81 us
    ppermute x1, starting transfers between devices, local(): dx_in = lax.ppermute(dx_oth, 'dp', swap)  5.2 us
    dot_general x1, matrix products, local(): jnp.dot(home_terms, all_rows, preferred_element_type=jnp.float32)  5.2 us
    ppermute x1, waiting for transfers between devices, local(): ret_g = lax.ppermute(sum_g, 'expert', behind)  5.16 us
  transfers between devices with their start and end apart: 14, of which 8 were waited for; matrix products, arithmetic and copies ran while one was open for 20% of the time, Pallas kernels for 0%

profile of v4, /device:TPU:1, one launch (start us, length us, event | category | flops | bytes accessed | tf_op | source)
XLA Modules:
  0.0 134.2 jit_solution(6387833903045977747)
XLA Ops:
  0.6 4.0 %collective-permute-start.1 = (bf16[192,2048]{1,0:T(8,128)(2,1)}, bf16[192,2048]{1,0:T(8,128)(2,1)S(1)}, u32[]{:S(2)}, u32[]{:S(2)}) collective-permute-start(bf16[192,2048]{1,0:T(8,128)(2,1)} %bitcast.45), channel_id=1, source_target_pairs={{0,1},{1,2},{2,3},{3,4},{4,5},{5,6},{6,7},{7,8},{8,9},{9,10},{10,1... | collective-permute-start | bytes 2359304 | tf_op jit(solution)/shard_map/ppermute | solution.py:53
  4.6 4.7 %collective-permute-start.2 = (bf16[192,2048]{1,0:T(8,128)(2,1)}, bf16[192,2048]{1,0:T(8,128)(2,1)}, u32[]{:S(2)}, u32[]{:S(2)}) collective-permute-start(bf16[192,2048]{1,0:T(8,128)(2,1)} %bitcast.39), channel_id=1, source_target_pairs={{0,3},{1,0},{2,1},{3,2},{4,7},{5,4},{6,5},{7,6},{8,11},{9,8},{10,9... | collective-permute-start | bytes 2359304 | tf_op jit(solution)/shard_map/ppermute | solution.py:54
  9.3 2.6 %broadcast_in_dim.76 = bf16[4,128,2048]{2,1,0:T(8,128)(2,1)} broadcast(bf16[128,2048]{1,0:T(8,128)(2,1)} %param.9), dimensions={1,2} | broadcast | bytes 2621440 | tf_op jit(solution)/shard_map/broadcast_in_dim | solution.py:47
  12.0 4.3 %all-to-all-start = ((bf16[4,128,2048]{2,1,0:T(8,128)(2,1)}), bf16[4,128,2048]{2,1,0:T(8,128)(2,1)S(1)}, u32[]{:S(2)}, u32[]{:S(2)}) async-start(bf16[4,128,2048]{2,1,0:T(8,128)(2,1)} %broadcast_in_dim.76), calls=%async_computation | async-start | bytes 4194304 | tf_op jit(solution)/shard_map/all_to_all | solution.py:42
  20.4 10.7 %collective-permute-start.3 = (s32[1]{0:T(128)}, s32[1]{0:T(128)}, u32[]{:S(2)}, u32[]{:S(2)}) collective-permute-start(s32[1]{0:T(128)} %param.13), channel_id=1, source_target_pairs={{0,63},{1,0},{2,1},{3,2},{4,3},{5,4},{6,5},{7,6},{8,7},{9,8},{10,9... | collective-permute-start | bytes 20 | tf_op jit(solution)/shard_map/ppermute | solution.py:56
  32.6 2.1 %broadcast_select_fusion.3 = bf16[192,2048]{1,0:T(8,128)(2,1)} fusion(bf16[192,2048]{1,0:T(8,128)(2,1)} %bitcast.40, bf16[192,2048]{1,0:T(8,128)(2,1)S(1)} %collective-permute-done.1, pred[]{:T(512)} %bitcast.5), kind=kLoop, calls=%fused_computation.26 | loop fusion | flops 393216 | bytes 2359297 | tf_op jit(solution)/shard_map/jit(_where)/select_n | solution.py:60
  34.7 1.9 %collective-permute-start.4 = (bf16[192,2048]{1,0:T(8,128)(2,1)}, bf16[192,2048]{1,0:T(8,128)(2,1)}, u32[]{:S(2)}, u32[]{:S(2)}) collective-permute-start(bf16[192,2048]{1,0:T(8,128)(2,1)} %broadcast_select_fusion.3), channel_id=1, source_target_pairs={{0,1},{1,2},{2,3},{3,4},{4,5},{5,6},{6,7},{7,8},{8,9},{9,10},{10,1... | collective-permute-start | bytes 2359304 | tf_op jit(solution)/shard_map/ppermute | solution.py:64
  37.3 1.9 %collective-permute-start.5 = (bf16[192,2048]{1,0:T(8,128)(2,1)}, bf16[192,2048]{1,0:T(8,128)(2,1)}, u32[]{:S(2)}, u32[]{:S(2)}) collective-permute-start(bf16[192,2048]{1,0:T(8,128)(2,1)} %collective-permute-done.2), channel_id=1, source_target_pairs={{3,2},{0,3},{1,4},{2,5},{7,6},{4,7},{5,8},{6,9},{11,10},{8,11},{9,... | collective-permute-start | bytes 2359304 | tf_op jit(solution)/shard_map/ppermute | solution.py:63
  41.1 5.8 %all-to-all-start.1 = ((bf16[8,208,128]{2,1,0:T(8,128)(2,1)}), bf16[8,208,128]{2,1,0:T(8,128)(2,1)S(1)}, u32[]{:S(2)}, u32[]{:S(2)}) async-start(bf16[8,208,128]{2,1,0:T(8,128)(2,1)} %pad_maximum_fusion.3), calls=%async_computation.1 | async-start | bytes 851968 | tf_op jit(solution)/shard_map/all_to_all | solution.py:69
  46.9 6.2 %conditional.1 = (bf16[512,2048]{1,0:T(8,128)(2,1)}) conditional(s32[]{:T(128)} %convert_element_type.63, () %tuple.33, bf16[512,2048]{1,0:T(8,128)(2,1)S(1)} %bitcast.34), branch_computations={%region_0.1_spmd, %region_1.2_spmd} | conditional | bytes 8388656 | solution.py:66
  46.9 2.0 %collective-permute-start = (bf16[512,2048]{1,0:T(8,128)(2,1)S(1)}, bf16[512,2048]{1,0:T(8,128)(2,1)}, u32[]{:S(2)}, u32[]{:S(2)}) collective-permute-start(bf16[512,2048]{1,0:T(8,128)(2,1)S(1)} %param.1), channel_id=1, source_target_pairs={{0,64},{64,0},{128,192},{192,128},{256,320},{320,256},{384,448},{4... | collective-permute-start | bytes 6291464 | tf_op jit(solution)/shard_map/cond/branch_1_fun/ppermute | solution.py:67
  49.0 4.1 %collective-permute-done = bf16[512,2048]{1,0:T(8,128)(2,1)} collective-permute-done((bf16[512,2048]{1,0:T(8,128)(2,1)S(1)}, bf16[512,2048]{1,0:T(8,128)(2,1)}, u32[]{:S(2)}, u32[]{:S(2)}) %collective-permute-start) | collective-permute-done | bytes 2097184 | tf_op jit(solution)/shard_map/cond/branch_1_fun/ppermute | solution.py:67
  53.1 3.8 %collective-permute-done.4 = bf16[192,2048]{1,0:T(8,128)(2,1)} collective-permute-done((bf16[192,2048]{1,0:T(8,128)(2,1)}, bf16[192,2048]{1,0:T(8,128)(2,1)}, u32[]{:S(2)}, u32[]{:S(2)}) %collective-permute-start.4) | collective-permute-done | bytes 786464 | tf_op jit(solution)/shard_map/ppermute | solution.py:64
  56.9 2.1 %broadcast_select_fusion.6 = bf16[192,2048]{1,0:T(8,128)(2,1)} fusion(bf16[192,2048]{1,0:T(8,128)(2,1)S(1)} %collective-permute-done.1, bf16[192,2048]{1,0:T(8,128)(2,1)} %collective-permute-done.4, pred[]{:T(512)} %bitcast), kind=kLoop, calls=%fused_computation.29 | loop fusion | flops 393216 | bytes 2359297 | tf_op jit(solution)/shard_map/jit(_where)/select_n | solution.py:76
  59.2 2.3 %pad_maximum_fusion = bf16[1024,2048]{1,0:T(8,128)(2,1)S(1)} fusion(bf16[512,2048]{1,0:T(8,128)(2,1)} %get-tuple-element.90, bf16[512,2048]{1,0:T(8,128)(2,1)S(1)} %bitcast.35), kind=kLoop, calls=%fused_computation | loop fusion | flops 8388608 | bytes 8388608 | tf_op jit(solution)/shard_map/concatenate | solution.py:87
  63.4 3.4 %fusion.9 = f32[768,1024]{1,0:T(8,128)S(1)} fusion(bf16[1024,2048]{1,0:T(8,128)(2,1)S(1)} %pad_maximum_fusion, bf16[192,2048]{1,0:T(8,128)(2,1)S(1)} %broadcast_select_fusion.5, bf16[192,2048]{1,0:T(8,128)(2,1)S(1)} %copy-done.3, bf16[192,2048]{1,0:T(8,128)(2,1)S(1)} %bitcast.41, bf16[192,2048]{1,0:T(8,128)(2,1)S(1)} %bitcast.46), kind=kOutput, calls=%fused_computation.41 | convolution fusion | flops 3233808384 | bytes 10485760 | tf_op jit(solution)/shard_map/dot_general | solution.py:74
  71.2 2.0 %convolution_convert_fusion = bf16[512,2048]{1,0:T(8,128)(2,1)S(1)} fusion(bf16[768,1024]{1,0:T(8,128)(2,1)S(1)} %constant_dynamic-update-slice_fusion, bf16[192,2048]{1,0:T(8,128)(2,1)S(1)} %broadcast_select_fusion.5, bf16[192,2048]{1,0:T(8,128)(2,1)S(1)} %copy-done.3, bf16[192,2048]{1,0:T(8,128)(2,1)S(1)} %bitcast.42, bf16[192,2048]{1,0:T(8,128)(2,1)S(1)} %bitcast.47), kind=kOutput, calls=%fused_computation.3 | convolution fusion | flops 1624244224 | bytes 6029312 | tf_op jit(solution)/shard_map/dot_general | solution.py:116
  73.3 5.2 %collective-permute-start.7 = (bf16[512,2048]{1,0:T(8,128)(2,1)S(1)}, bf16[512,2048]{1,0:T(8,128)(2,1)S(1)}, u32[]{:S(2)}, u32[]{:S(2)}) collective-permute-start(bf16[512,2048]{1,0:T(8,128)(2,1)S(1)} %convolution_convert_fusion), channel_id=1, source_target_pairs={{0,64},{64,0},{128,192},{192,128},{256,320},{320,256},{384,448},{4... | collective-permute-start | bytes 6291464 | tf_op jit(solution)/shard_map/ppermute | solution.py:119
  79.1 4.7 %collective-permute-start.6 = (bf16[192,2048]{1,0:T(8,128)(2,1)}, bf16[192,2048]{1,0:T(8,128)(2,1)}, u32[]{:S(2)}, u32[]{:S(2)}) collective-permute-start(bf16[192,2048]{1,0:T(8,128)(2,1)} %get-tuple-element.61), channel_id=1, source_target_pairs={{0,63},{1,0},{2,1},{3,2},{4,3},{5,4},{6,5},{7,6},{8,7},{9,8},{10,9... | collective-permute-start | bytes 2359304 | tf_op jit(solution)/shard_map/ppermute | solution.py:110
  83.8 1.9 %collective-permute-start.9 = (bf16[192,2048]{1,0:T(8,128)(2,1)}, bf16[192,2048]{1,0:T(8,128)(2,1)}, u32[]{:S(2)}, u32[]{:S(2)}) collective-permute-start(bf16[192,2048]{1,0:T(8,128)(2,1)} %get-tuple-element.75), channel_id=1, source_target_pairs={{0,1},{1,2},{2,3},{3,0},{4,5},{5,6},{6,7},{7,4},{8,9},{9,10},{10,1... | collective-permute-start | bytes 2359304 | tf_op jit(solution)/shard_map/ppermute | solution.py:111
  85.7 1.9 %fusion.7 = f32[512,2048]{1,0:T(8,128)S(1)} fusion(bf16[768,1024]{1,0:T(8,128)(2,1)S(1)} %constant_dynamic-update-slice_fusion, bf16[192,2048]{1,0:T(8,128)(2,1)S(1)} %broadcast_select_fusion.5, bf16[192,2048]{1,0:T(8,128)(2,1)S(1)} %copy-done.3, bf16[192,2048]{1,0:T(8,128)(2,1)S(1)} %bitcast.43, bf16[192,2048]{1,0:T(8,128)(2,1)S(1)} %bitcast.48), kind=kOutput, calls=%fused_computation.19 | convolution fusion | flops 1623195648 | bytes 8126464 | tf_op jit(solution)/shard_map/dot_general | solution.py:116
  87.6 2.1 %add_convert_fusion = bf16[512,2048]{1,0:T(8,128)(2,1)} fusion(f32[512,2048]{1,0:T(8,128)S(1)} %fusion.7, bf16[512,2048]{1,0:T(8,128)(2,1)S(1)} %collective-permute-done.7), kind=kLoop, calls=%fused_computation.1 | loop fusion | flops 3145728 | bytes 8388608 | tf_op jit(solution)/shard_map/convert_element_type | solution.py:121
  89.8 3.8 %all-to-all-start.2 = ((bf16[4,128,2048]{2,1,0:T(8,128)(2,1)}), bf16[4,128,2048]{2,1,0:T(8,128)(2,1)S(1)}, u32[]{:S(2)}, u32[]{:S(2)}) async-start(bf16[4,128,2048]{2,1,0:T(8,128)(2,1)} %bitcast.36), calls=%async_computation.2 | async-start | bytes 4194304 | tf_op jit(solution)/shard_map/all_to_all | solution.py:42
  93.6 5.2 %convolution_convert_fusion.1 = bf16[384,2048]{1,0:T(8,128)(2,1)} fusion(bf16[384,1024]{1,0:T(8,128)(2,1)S(1)} %get-tuple-element.66, bf16[1024,2048]{1,0:T(8,128)(2,1)} %copy-done), kind=kOutput, calls=%fused_computation.4 | convolution fusion | flops 1611399168 | bytes 6553600 | tf_op jit(solution)/shard_map/dot_general | solution.py:125
  98.8 2.3 %collective-permute-done.6 = bf16[192,2048]{1,0:T(8,128)(2,1)} collective-permute-done((bf16[192,2048]{1,0:T(8,128)(2,1)}, bf16[192,2048]{1,0:T(8,128)(2,1)}, u32[]{:S(2)}, u32[]{:S(2)}) %collective-permute-start.6) | collective-permute-done | bytes 786464 | tf_op jit(solution)/shard_map/ppermute | solution.py:110
  101.4 8.6 %collective-permute-start.8 = (bf16[192,2048]{1,0:T(8,128)(2,1)S(1)}, bf16[192,2048]{1,0:T(8,128)(2,1)}, u32[]{:S(2)}, u32[]{:S(2)}) collective-permute-start(bf16[192,2048]{1,0:T(8,128)(2,1)S(1)} %add_convert_fusion.3), channel_id=1, source_target_pairs={{0,63},{1,0},{2,1},{3,2},{4,3},{5,4},{6,5},{7,6},{8,7},{9,8},{10,9... | collective-permute-start | bytes 2359304 | tf_op jit(solution)/shard_map/ppermute | solution.py:129
  109.9 1.9 %collective-permute-start.10 = (bf16[192,2048]{1,0:T(8,128)(2,1)}, bf16[192,2048]{1,0:T(8,128)(2,1)}, u32[]{:S(2)}, u32[]{:S(2)}) collective-permute-start(bf16[192,2048]{1,0:T(8,128)(2,1)} %collective-permute-done.9), channel_id=1, source_target_pairs={{1,62},{2,63},{3,0},{0,1},{5,2},{6,3},{7,4},{4,5},{9,6},{10,7},{11... | collective-permute-start | bytes 2359304 | tf_op jit(solution)/shard_map/ppermute | solution.py:131
  111.9 7.6 %all-to-all-done.2 = bf16[4,128,2048]{2,1,0:T(8,128)(2,1)S(1)} async-done(((bf16[4,128,2048]{2,1,0:T(8,128)(2,1)}), bf16[4,128,2048]{2,1,0:T(8,128)(2,1)S(1)}, u32[]{:S(2)}, u32[]{:S(2)}) %all-to-all-start.2) | async-done | bytes 2097184 | tf_op jit(solution)/shard_map/all_to_all | solution.py:42
  120.8 5.2 %collective-permute-done.8 = bf16[192,2048]{1,0:T(8,128)(2,1)} collective-permute-done((bf16[192,2048]{1,0:T(8,128)(2,1)S(1)}, bf16[192,2048]{1,0:T(8,128)(2,1)}, u32[]{:S(2)}, u32[]{:S(2)}) %collective-permute-start.8) | collective-permute-done | bytes 786464 | tf_op jit(solution)/shard_map/ppermute | solution.py:129
  126.0 2.5 %add_convert_fusion.2 = bf16[192,2048]{1,0:T(8,128)(2,1)} fusion(bf16[192,2048]{1,0:T(8,128)(2,1)} %collective-permute-done.8, bf16[384,2048]{1,0:T(8,128)(2,1)} %convolution_convert_fusion.1), kind=kLoop, calls=%fused_computation.8 | loop fusion | flops 1572864 | bytes 2359296 | tf_op jit(solution)/shard_map/convert_element_type | solution.py:134
  128.5 2.8 %collective-permute-done.10 = bf16[192,2048]{1,0:T(8,128)(2,1)} collective-permute-done((bf16[192,2048]{1,0:T(8,128)(2,1)}, bf16[192,2048]{1,0:T(8,128)(2,1)}, u32[]{:S(2)}, u32[]{:S(2)}) %collective-permute-start.10) | collective-permute-done | bytes 786464 | tf_op jit(solution)/shard_map/ppermute | solution.py:131
  131.3 2.9 %fusion.5 = bf16[1,192,2048]{2,1,0:T(8,128)(2,1)} fusion(bf16[192,2048]{1,0:T(8,128)(2,1)} %collective-permute-done.10, bf16[192,2048]{1,0:T(8,128)(2,1)} %collective-permute-done.6, bf16[384,2048]{1,0:T(8,128)(2,1)} %convolution_convert_fusion.1, pred[]{:T(512)} %bitcast.5), kind=kLoop, calls=%fused_computation.17 | loop fusion | flops 2752512 | bytes 3145729 | tf_op jit(solution)/shard_map/broadcast_in_dim | solution.py:141
  (45 shorter events, 14.7 us)
Async XLA Ops:
  0.6 32.0 %collective-permute-start.1 = (bf16[192,2048]{1,0:T(8,128)(2,1)}, bf16[192,2048]{1,0:T(8,128)(2,1)S(1)}, u32[]{:S(2)}, u32[]{:S(2)}) collective-permute-start(bf16[192,2048]{1,0:T(8,128)(2,1)} %bitcast.45), channel_id=1, source_target_pairs={{0,1},{1,2},{2,3},{3,4},{4,5},{5,6},{6,7},{7,8},{8,9},{9,10},{10,1... | collective-permute-start | bytes 2359304 | tf_op jit(solution)/shard_map/ppermute | solution.py:53
  4.6 11.7 %copy-start.5 = (s32[2]{0:T(128)S(1)}, s32[2]{0:T(128)}, u32[]{:S(2)}) copy-start(s32[2]{0:T(128)} %param.15) | copy-start | bytes 28
  4.6 28.0 %collective-permute-start.2 = (bf16[192,2048]{1,0:T(8,128)(2,1)}, bf16[192,2048]{1,0:T(8,128)(2,1)}, u32[]{:S(2)}, u32[]{:S(2)}) collective-permute-start(bf16[192,2048]{1,0:T(8,128)(2,1)} %bitcast.39), channel_id=1, source_target_pairs={{0,3},{1,0},{2,1},{3,2},{4,7},{5,4},{6,5},{7,6},{8,11},{9,8},{10,9... | collective-permute-start | bytes 2359304 | tf_op jit(solution)/shard_map/ppermute | solution.py:54
  12.0 6.5 %copy-start.6 = (s32[2]{0:T(128)S(1)}, s32[2]{0:T(128)}, u32[]{:S(2)}) copy-start(s32[2]{0:T(128)} %param.14) | copy-start | bytes 28
  12.0 29.2 %all-to-all-start = ((bf16[4,128,2048]{2,1,0:T(8,128)(2,1)}), bf16[4,128,2048]{2,1,0:T(8,128)(2,1)S(1)}, u32[]{:S(2)}, u32[]{:S(2)}) async-start(bf16[4,128,2048]{2,1,0:T(8,128)(2,1)} %broadcast_in_dim.76), calls=%async_computation | async-start | bytes 4194304 | tf_op jit(solution)/shard_map/all_to_all | solution.py:42
  20.4 11.6 %collective-permute-start.3 = (s32[1]{0:T(128)}, s32[1]{0:T(128)}, u32[]{:S(2)}, u32[]{:S(2)}) collective-permute-start(s32[1]{0:T(128)} %param.13), channel_id=1, source_target_pairs={{0,63},{1,0},{2,1},{3,2},{4,3},{5,4},{6,5},{7,6},{8,7},{9,8},{10,9... | collective-permute-start | bytes 20 | tf_op jit(solution)/shard_map/ppermute | solution.py:56
  34.7 22.2 %collective-permute-start.4 = (bf16[192,2048]{1,0:T(8,128)(2,1)}, bf16[192,2048]{1,0:T(8,128)(2,1)}, u32[]{:S(2)}, u32[]{:S(2)}) collective-permute-start(bf16[192,2048]{1,0:T(8,128)(2,1)} %broadcast_select_fusion.3), channel_id=1, source_target_pairs={{0,1},{1,2},{2,3},{3,4},{4,5},{5,6},{6,7},{7,8},{8,9},{9,10},{10,1... | collective-permute-start | bytes 2359304 | tf_op jit(solution)/shard_map/ppermute | solution.py:64
  37.3 24.2 %collective-permute-start.5 = (bf16[192,2048]{1,0:T(8,128)(2,1)}, bf16[192,2048]{1,0:T(8,128)(2,1)}, u32[]{:S(2)}, u32[]{:S(2)}) collective-permute-start(bf16[192,2048]{1,0:T(8,128)(2,1)} %collective-permute-done.2), channel_id=1, source_target_pairs={{3,2},{0,3},{1,4},{2,5},{7,6},{4,7},{5,8},{6,9},{11,10},{8,11},{9,... | collective-permute-start | bytes 2359304 | tf_op jit(solution)/shard_map/ppermute | solution.py:63
  41.1 17.9 %all-to-all-start.1 = ((bf16[8,208,128]{2,1,0:T(8,128)(2,1)}), bf16[8,208,128]{2,1,0:T(8,128)(2,1)S(1)}, u32[]{:S(2)}, u32[]{:S(2)}) async-start(bf16[8,208,128]{2,1,0:T(8,128)(2,1)} %pad_maximum_fusion.3), calls=%async_computation.1 | async-start | bytes 851968 | tf_op jit(solution)/shard_map/all_to_all | solution.py:69
  46.9 6.2 %collective-permute-start = (bf16[512,2048]{1,0:T(8,128)(2,1)S(1)}, bf16[512,2048]{1,0:T(8,128)(2,1)}, u32[]{:S(2)}, u32[]{:S(2)}) collective-permute-start(bf16[512,2048]{1,0:T(8,128)(2,1)S(1)} %param.1), channel_id=1, source_target_pairs={{0,64},{64,0},{128,192},{192,128},{256,320},{320,256},{384,448},{4... | collective-permute-start | bytes 6291464 | tf_op jit(solution)/shard_map/cond/branch_1_fun/ppermute | solution.py:67
  59.1 4.2 %copy-start.2 = (bf16[1,192,2048]{2,1,0:T(8,128)(2,1)S(1)}, bf16[1,192,2048]{2,1,0:T(8,128)(2,1)}, u32[]{:S(2)}) copy-start(bf16[1,192,2048]{2,1,0:T(8,128)(2,1)} %param.12) | copy-start | bytes 2359300
  59.2 4.2 %copy-start.3 = (bf16[192,2048]{1,0:T(8,128)(2,1)S(1)}, bf16[192,2048]{1,0:T(8,128)(2,1)}, u32[]{:S(2)}) copy-start(bf16[192,2048]{1,0:T(8,128)(2,1)} %broadcast_select_fusion.6) | copy-start | bytes 2359300
  59.2 4.2 %copy-start.4 = (bf16[1,192,2048]{2,1,0:T(8,128)(2,1)S(1)}, bf16[1,192,2048]{2,1,0:T(8,128)(2,1)}, u32[]{:S(2)}) copy-start(bf16[1,192,2048]{2,1,0:T(8,128)(2,1)} %param.11) | copy-start | bytes 2359300
  61.5 6.3 %copy-start = (bf16[1024,2048]{1,0:T(8,128)(2,1)}, bf16[1024,2048]{1,0:T(8,128)(2,1)S(1)}, u32[]{:S(2)}) copy-start(bf16[1024,2048]{1,0:T(8,128)(2,1)S(1)} %pad_maximum_fusion) | copy-start | bytes 12582916
  73.3 14.4 %collective-permute-start.7 = (bf16[512,2048]{1,0:T(8,128)(2,1)S(1)}, bf16[512,2048]{1,0:T(8,128)(2,1)S(1)}, u32[]{:S(2)}, u32[]{:S(2)}) collective-permute-start(bf16[512,2048]{1,0:T(8,128)(2,1)S(1)} %convolution_convert_fusion), channel_id=1, source_target_pairs={{0,64},{64,0},{128,192},{192,128},{256,320},{320,256},{384,448},{4... | collective-permute-start | bytes 6291464 | tf_op jit(solution)/shard_map/ppermute | solution.py:119
  79.1 21.9 %collective-permute-start.6 = (bf16[192,2048]{1,0:T(8,128)(2,1)}, bf16[192,2048]{1,0:T(8,128)(2,1)}, u32[]{:S(2)}, u32[]{:S(2)}) collective-permute-start(bf16[192,2048]{1,0:T(8,128)(2,1)} %get-tuple-element.61), channel_id=1, source_target_pairs={{0,63},{1,0},{2,1},{3,2},{4,3},{5,4},{6,5},{7,6},{8,7},{9,8},{10,9... | collective-permute-start | bytes 2359304 | tf_op jit(solution)/shard_map/ppermute | solution.py:110
  83.8 26.1 %collective-permute-start.9 = (bf16[192,2048]{1,0:T(8,128)(2,1)}, bf16[192,2048]{1,0:T(8,128)(2,1)}, u32[]{:S(2)}, u32[]{:S(2)}) collective-permute-start(bf16[192,2048]{1,0:T(8,128)(2,1)} %get-tuple-element.75), channel_id=1, source_target_pairs={{0,1},{1,2},{2,3},{3,0},{4,5},{5,6},{6,7},{7,4},{8,9},{9,10},{10,1... | collective-permute-start | bytes 2359304 | tf_op jit(solution)/shard_map/ppermute | solution.py:111
  89.8 29.8 %all-to-all-start.2 = ((bf16[4,128,2048]{2,1,0:T(8,128)(2,1)}), bf16[4,128,2048]{2,1,0:T(8,128)(2,1)S(1)}, u32[]{:S(2)}, u32[]{:S(2)}) async-start(bf16[4,128,2048]{2,1,0:T(8,128)(2,1)} %bitcast.36), calls=%async_computation.2 | async-start | bytes 4194304 | tf_op jit(solution)/shard_map/all_to_all | solution.py:42
  93.6 7.5 %copy-start.1 = (bf16[192,2048]{1,0:T(8,128)(2,1)S(1)}, bf16[192,2048]{1,0:T(8,128)(2,1)}, u32[]{:S(2)}) copy-start(bf16[192,2048]{1,0:T(8,128)(2,1)} %get-tuple-element.60) | copy-start | bytes 2359300
  101.4 24.6 %collective-permute-start.8 = (bf16[192,2048]{1,0:T(8,128)(2,1)S(1)}, bf16[192,2048]{1,0:T(8,128)(2,1)}, u32[]{:S(2)}, u32[]{:S(2)}) collective-permute-start(bf16[192,2048]{1,0:T(8,128)(2,1)S(1)} %add_convert_fusion.3), channel_id=1, source_target_pairs={{0,63},{1,0},{2,1},{3,2},{4,3},{5,4},{6,5},{7,6},{8,7},{9,8},{10,9... | collective-permute-start | bytes 2359304 | tf_op jit(solution)/shard_map/ppermute | solution.py:129
  109.9 21.4 %collective-permute-start.10 = (bf16[192,2048]{1,0:T(8,128)(2,1)}, bf16[192,2048]{1,0:T(8,128)(2,1)}, u32[]{:S(2)}, u32[]{:S(2)}) collective-permute-start(bf16[192,2048]{1,0:T(8,128)(2,1)} %collective-permute-done.9), channel_id=1, source_target_pairs={{1,62},{2,63},{3,0},{0,1},{5,2},{6,3},{7,4},{4,5},{9,6},{10,7},{11... | collective-permute-start | bytes 2359304 | tf_op jit(solution)/shard_map/ppermute | solution.py:131

commit v5 on v4

--- a/solution.py
+++ b/solution.py
@@ -130,14 +130,14 @@
     ret_h, _ = barrier((ret_h, sum_g))
     ret_u = lax.ppermute(ret_h, "expert", onward(n_exp, 1, -2))
     input_grad = jnp.sum(dx_parts.astype(jnp.float32), axis=0).astype(jnp.bfloat16)
-    home_part, input_grad, ret_g = barrier((home_part, input_grad, ret_g))
-    gate_grad = (home_part[:shard].astype(jnp.float32) + ret_g.astype(jnp.float32)).astype(jnp.bfloat16)
-    gate_grad, home_part, ret_1, ret_u = barrier((gate_grad, home_part, ret_1, ret_u))
-    up_grad = (
+    up_part = (
         home_part[shard:].astype(jnp.float32)
         + jnp.where(offset_next == 1, ret_1, zero).astype(jnp.float32)
-        + ret_u.astype(jnp.float32)
     ).astype(jnp.bfloat16)
+    home_part, up_part, input_grad, ret_g = barrier((home_part, up_part, input_grad, ret_g))
+    gate_grad = (home_part[:shard].astype(jnp.float32) + ret_g.astype(jnp.float32)).astype(jnp.bfloat16)
+    gate_grad, up_part, ret_u = barrier((gate_grad, up_part, ret_u))
+    up_grad = (up_part.astype(jnp.float32) + ret_u.astype(jnp.float32)).astype(jnp.bfloat16)
     return input_grad, gate_grad[None], up_grad[None]
 
 

time: 135 us -> 134 us (level)
  no operation moved by 1% of the time
where the time goes in v5:
time: 134 us; the launch traced here: 133 us
  starting transfers between devices  60.9 us (45%)
  waiting for transfers between devices  28.7 us (21%)
  other arithmetic  22.9 us (17%)
  matrix products  13.4 us (10%)
  local copies, waits for them, and re-layouts  4.32 us (3%)
  between operations  2.91 us (2%)
    ppermute x1, starting transfers between devices, local(): offset_next = lax.ppermute(replica_offset, 'expert', behind)[0]  10.7 us
    all_to_all x2, waiting for transfers between devices, exchange_y(): lax.all_to_all(parts, 'dp', split_axis=0, concat_axis=0, axis_index_group...  8.32 us
    all_to_all x2, starting transfers between devices, exchange_y(): lax.all_to_all(parts, 'dp', split_axis=0, concat_axis=0, axis_index_group...  8.1 us
    ppermute x1, starting transfers between devices, local(): ret_g = lax.ppermute(sum_g, 'expert', behind)  7.31 us
    all_to_all x1, starting transfers between devices, local(): got = lax.all_to_all(sent, 'dp', split_axis=0, concat_axis=0, tiled=True)  5.81 us
    ppermute x1, starting transfers between devices, local(): ret_1 = lax.ppermute(first, 'expert', behind)  5.48 us
    ppermute x1, waiting for transfers between devices, local(): ret_g = lax.ppermute(sum_g, 'expert', behind)  5.48 us
    ppermute x1, starting transfers between devices, local(): dx_in = lax.ppermute(dx_oth, 'dp', swap)  5.07 us
  transfers between devices with their start and end apart: 14, of which 8 were waited for; matrix products, arithmetic and copies ran while one was open for 20% of the time, Pallas kernels for 0%

profile of v5, /device:TPU:1, one launch (start us, length us, event | category | flops | bytes accessed | tf_op | source)
XLA Modules:
  0.0 133.2 jit_solution(16063500983088763603)
XLA Ops:
  0.6 4.0 %collective-permute-start.1 = (bf16[192,2048]{1,0:T(8,128)(2,1)}, bf16[192,2048]{1,0:T(8,128)(2,1)S(1)}, u32[]{:S(2)}, u32[]{:S(2)}) collective-permute-start(bf16[192,2048]{1,0:T(8,128)(2,1)} %bitcast.45), channel_id=1, source_target_pairs={{0,1},{1,2},{2,3},{3,4},{4,5},{5,6},{6,7},{7,8},{8,9},{9,10},{10,1... | collective-permute-start | bytes 2359304 | tf_op jit(solution)/shard_map/ppermute | solution.py:53
  4.6 4.7 %collective-permute-start.2 = (bf16[192,2048]{1,0:T(8,128)(2,1)}, bf16[192,2048]{1,0:T(8,128)(2,1)}, u32[]{:S(2)}, u32[]{:S(2)}) collective-permute-start(bf16[192,2048]{1,0:T(8,128)(2,1)} %bitcast.39), channel_id=1, source_target_pairs={{0,3},{1,0},{2,1},{3,2},{4,7},{5,4},{6,5},{7,6},{8,11},{9,8},{10,9... | collective-permute-start | bytes 2359304 | tf_op jit(solution)/shard_map/ppermute | solution.py:54
  9.3 2.6 %broadcast_in_dim.76 = bf16[4,128,2048]{2,1,0:T(8,128)(2,1)} broadcast(bf16[128,2048]{1,0:T(8,128)(2,1)} %param.9), dimensions={1,2} | broadcast | bytes 2621440 | tf_op jit(solution)/shard_map/broadcast_in_dim | solution.py:47
  12.0 4.3 %all-to-all-start = ((bf16[4,128,2048]{2,1,0:T(8,128)(2,1)}), bf16[4,128,2048]{2,1,0:T(8,128)(2,1)S(1)}, u32[]{:S(2)}, u32[]{:S(2)}) async-start(bf16[4,128,2048]{2,1,0:T(8,128)(2,1)} %broadcast_in_dim.76), calls=%async_computation | async-start | bytes 4194304 | tf_op jit(solution)/shard_map/all_to_all | solution.py:42
  20.4 10.7 %collective-permute-start.3 = (s32[1]{0:T(128)}, s32[1]{0:T(128)}, u32[]{:S(2)}, u32[]{:S(2)}) collective-permute-start(s32[1]{0:T(128)} %param.13), channel_id=1, source_target_pairs={{0,63},{1,0},{2,1},{3,2},{4,3},{5,4},{6,5},{7,6},{8,7},{9,8},{10,9... | collective-permute-start | bytes 20 | tf_op jit(solution)/shard_map/ppermute | solution.py:56
  32.6 2.1 %broadcast_select_fusion.3 = bf16[192,2048]{1,0:T(8,128)(2,1)} fusion(bf16[192,2048]{1,0:T(8,128)(2,1)} %bitcast.40, bf16[192,2048]{1,0:T(8,128)(2,1)S(1)} %collective-permute-done.1, pred[]{:T(512)} %bitcast.5), kind=kLoop, calls=%fused_computation.27 | loop fusion | flops 393216 | bytes 2359297 | tf_op jit(solution)/shard_map/jit(_where)/select_n | solution.py:60
  34.7 1.9 %collective-permute-start.4 = (bf16[192,2048]{1,0:T(8,128)(2,1)}, bf16[192,2048]{1,0:T(8,128)(2,1)}, u32[]{:S(2)}, u32[]{:S(2)}) collective-permute-start(bf16[192,2048]{1,0:T(8,128)(2,1)} %broadcast_select_fusion.3), channel_id=1, source_target_pairs={{0,1},{1,2},{2,3},{3,4},{4,5},{5,6},{6,7},{7,8},{8,9},{9,10},{10,1... | collective-permute-start | bytes 2359304 | tf_op jit(solution)/shard_map/ppermute | solution.py:64
  37.3 1.9 %collective-permute-start.5 = (bf16[192,2048]{1,0:T(8,128)(2,1)}, bf16[192,2048]{1,0:T(8,128)(2,1)}, u32[]{:S(2)}, u32[]{:S(2)}) collective-permute-start(bf16[192,2048]{1,0:T(8,128)(2,1)} %collective-permute-done.2), channel_id=1, source_target_pairs={{3,2},{0,3},{1,4},{2,5},{7,6},{4,7},{5,8},{6,9},{11,10},{8,11},{9,... | collective-permute-start | bytes 2359304 | tf_op jit(solution)/shard_map/ppermute | solution.py:63
  39.3 1.9 %all-to-all-done = bf16[4,128,2048]{2,1,0:T(8,128)(2,1)S(1)} async-done(((bf16[4,128,2048]{2,1,0:T(8,128)(2,1)}), bf16[4,128,2048]{2,1,0:T(8,128)(2,1)S(1)}, u32[]{:S(2)}, u32[]{:S(2)}) %all-to-all-start) | async-done | bytes 2097184 | tf_op jit(solution)/shard_map/all_to_all | solution.py:42
  41.1 5.8 %all-to-all-start.1 = ((bf16[8,208,128]{2,1,0:T(8,128)(2,1)}), bf16[8,208,128]{2,1,0:T(8,128)(2,1)S(1)}, u32[]{:S(2)}, u32[]{:S(2)}) async-start(bf16[8,208,128]{2,1,0:T(8,128)(2,1)} %pad_maximum_fusion.3), calls=%async_computation.1 | async-start | bytes 851968 | tf_op jit(solution)/shard_map/all_to_all | solution.py:69
  46.9 6.2 %conditional.1 = (bf16[512,2048]{1,0:T(8,128)(2,1)}) conditional(s32[]{:T(128)} %convert_element_type.69, () %tuple.33, bf16[512,2048]{1,0:T(8,128)(2,1)S(1)} %bitcast.34), branch_computations={%region_0.1_spmd, %region_1.2_spmd} | conditional | bytes 8388656 | solution.py:66
  46.9 2.0 %collective-permute-start = (bf16[512,2048]{1,0:T(8,128)(2,1)S(1)}, bf16[512,2048]{1,0:T(8,128)(2,1)}, u32[]{:S(2)}, u32[]{:S(2)}) collective-permute-start(bf16[512,2048]{1,0:T(8,128)(2,1)S(1)} %param.1), channel_id=1, source_target_pairs={{0,64},{64,0},{128,192},{192,128},{256,320},{320,256},{384,448},{4... | collective-permute-start | bytes 6291464 | tf_op jit(solution)/shard_map/cond/branch_1_fun/ppermute | solution.py:67
  49.0 4.1 %collective-permute-done = bf16[512,2048]{1,0:T(8,128)(2,1)} collective-permute-done((bf16[512,2048]{1,0:T(8,128)(2,1)S(1)}, bf16[512,2048]{1,0:T(8,128)(2,1)}, u32[]{:S(2)}, u32[]{:S(2)}) %collective-permute-start) | collective-permute-done | bytes 2097184 | tf_op jit(solution)/shard_map/cond/branch_1_fun/ppermute | solution.py:67
  53.1 4.3 %collective-permute-done.4 = bf16[192,2048]{1,0:T(8,128)(2,1)} collective-permute-done((bf16[192,2048]{1,0:T(8,128)(2,1)}, bf16[192,2048]{1,0:T(8,128)(2,1)}, u32[]{:S(2)}, u32[]{:S(2)}) %collective-permute-start.4) | collective-permute-done | bytes 786464 | tf_op jit(solution)/shard_map/ppermute | solution.py:64
  58.5 2.3 %pad_maximum_fusion = bf16[1024,2048]{1,0:T(8,128)(2,1)S(1)} fusion(bf16[512,2048]{1,0:T(8,128)(2,1)} %get-tuple-element.90, bf16[512,2048]{1,0:T(8,128)(2,1)S(1)} %bitcast.35), kind=kLoop, calls=%fused_computation | loop fusion | flops 8388608 | bytes 8388608 | tf_op jit(solution)/shard_map/concatenate | solution.py:87
  62.7 3.4 %fusion.9 = f32[768,1024]{1,0:T(8,128)S(1)} fusion(bf16[1024,2048]{1,0:T(8,128)(2,1)S(1)} %pad_maximum_fusion, bf16[192,2048]{1,0:T(8,128)(2,1)S(1)} %broadcast_select_fusion.5, bf16[192,2048]{1,0:T(8,128)(2,1)S(1)} %copy-done.6, bf16[192,2048]{1,0:T(8,128)(2,1)S(1)} %bitcast.41, bf16[192,2048]{1,0:T(8,128)(2,1)S(1)} %bitcast.46), kind=kOutput, calls=%fused_computation.42 | convolution fusion | flops 3233808384 | bytes 10485760 | tf_op jit(solution)/shard_map/dot_general | solution.py:74
  70.6 2.0 %convolution_convert_fusion = bf16[512,2048]{1,0:T(8,128)(2,1)S(1)} fusion(bf16[768,1024]{1,0:T(8,128)(2,1)S(1)} %constant_dynamic-update-slice_fusion, bf16[192,2048]{1,0:T(8,128)(2,1)S(1)} %broadcast_select_fusion.5, bf16[192,2048]{1,0:T(8,128)(2,1)S(1)} %copy-done.6, bf16[192,2048]{1,0:T(8,128)(2,1)S(1)} %bitcast.42, bf16[192,2048]{1,0:T(8,128)(2,1)S(1)} %bitcast.47), kind=kOutput, calls=%fused_computation.3 | convolution fusion | flops 1624244224 | bytes 6029312 | tf_op jit(solution)/shard_map/dot_general | solution.py:116
  72.6 5.1 %collective-permute-start.7 = (bf16[512,2048]{1,0:T(8,128)(2,1)S(1)}, bf16[512,2048]{1,0:T(8,128)(2,1)S(1)}, u32[]{:S(2)}, u32[]{:S(2)}) collective-permute-start(bf16[512,2048]{1,0:T(8,128)(2,1)S(1)} %convolution_convert_fusion), channel_id=1, source_target_pairs={{0,64},{64,0},{128,192},{192,128},{256,320},{320,256},{384,448},{4... | collective-permute-start | bytes 6291464 | tf_op jit(solution)/shard_map/ppermute | solution.py:119
  78.3 5.5 %collective-permute-start.6 = (bf16[192,2048]{1,0:T(8,128)(2,1)}, bf16[192,2048]{1,0:T(8,128)(2,1)S(1)}, u32[]{:S(2)}, u32[]{:S(2)}) collective-permute-start(bf16[192,2048]{1,0:T(8,128)(2,1)} %get-tuple-element.61), channel_id=1, source_target_pairs={{0,63},{1,0},{2,1},{3,2},{4,3},{5,4},{6,5},{7,6},{8,7},{9,8},{10,9... | collective-permute-start | bytes 2359304 | tf_op jit(solution)/shard_map/ppermute | solution.py:110
  83.8 1.9 %collective-permute-start.9 = (bf16[192,2048]{1,0:T(8,128)(2,1)}, bf16[192,2048]{1,0:T(8,128)(2,1)}, u32[]{:S(2)}, u32[]{:S(2)}) collective-permute-start(bf16[192,2048]{1,0:T(8,128)(2,1)} %get-tuple-element.76), channel_id=1, source_target_pairs={{0,1},{1,2},{2,3},{3,0},{4,5},{5,6},{6,7},{7,4},{8,9},{9,10},{10,1... | collective-permute-start | bytes 2359304 | tf_op jit(solution)/shard_map/ppermute | solution.py:111
  85.7 1.9 %fusion.7 = f32[512,2048]{1,0:T(8,128)S(1)} fusion(bf16[768,1024]{1,0:T(8,128)(2,1)S(1)} %constant_dynamic-update-slice_fusion, bf16[192,2048]{1,0:T(8,128)(2,1)S(1)} %broadcast_select_fusion.5, bf16[192,2048]{1,0:T(8,128)(2,1)S(1)} %copy-done.6, bf16[192,2048]{1,0:T(8,128)(2,1)S(1)} %bitcast.43, bf16[192,2048]{1,0:T(8,128)(2,1)S(1)} %bitcast.48), kind=kOutput, calls=%fused_computation.20 | convolution fusion | flops 1623195648 | bytes 8126464 | tf_op jit(solution)/shard_map/dot_general | solution.py:116
  87.7 2.1 %add_convert_fusion = bf16[512,2048]{1,0:T(8,128)(2,1)} fusion(f32[512,2048]{1,0:T(8,128)S(1)} %fusion.7, bf16[512,2048]{1,0:T(8,128)(2,1)S(1)} %collective-permute-done.7), kind=kLoop, calls=%fused_computation.1 | loop fusion | flops 3145728 | bytes 8388608 | tf_op jit(solution)/shard_map/convert_element_type | solution.py:121
  89.8 3.8 %all-to-all-start.2 = ((bf16[4,128,2048]{2,1,0:T(8,128)(2,1)}), bf16[4,128,2048]{2,1,0:T(8,128)(2,1)S(1)}, u32[]{:S(2)}, u32[]{:S(2)}) async-start(bf16[4,128,2048]{2,1,0:T(8,128)(2,1)} %bitcast.36), calls=%async_computation.2 | async-start | bytes 4194304 | tf_op jit(solution)/shard_map/all_to_all | solution.py:42
  93.6 4.3 %convolution_convert_fusion.1 = bf16[384,2048]{1,0:T(8,128)(2,1)S(1)} fusion(bf16[384,1024]{1,0:T(8,128)(2,1)} %copy-done.2, bf16[1024,2048]{1,0:T(8,128)(2,1)} %copy-done), kind=kOutput, calls=%fused_computation.4 | convolution fusion | flops 1611399168 | bytes 6553600 | tf_op jit(solution)/shard_map/dot_general | solution.py:125
  97.9 3.2 %collective-permute-done.6 = bf16[192,2048]{1,0:T(8,128)(2,1)S(1)} collective-permute-done((bf16[192,2048]{1,0:T(8,128)(2,1)}, bf16[192,2048]{1,0:T(8,128)(2,1)S(1)}, u32[]{:S(2)}, u32[]{:S(2)}) %collective-permute-start.6) | collective-permute-done | bytes 786464 | tf_op jit(solution)/shard_map/ppermute | solution.py:110
  102.2 7.3 %collective-permute-start.8 = (bf16[192,2048]{1,0:T(8,128)(2,1)}, bf16[192,2048]{1,0:T(8,128)(2,1)}, u32[]{:S(2)}, u32[]{:S(2)}) collective-permute-start(bf16[192,2048]{1,0:T(8,128)(2,1)} %add_convert_fusion.4), channel_id=1, source_target_pairs={{0,63},{1,0},{2,1},{3,2},{4,3},{5,4},{6,5},{7,6},{8,7},{9,8},{10,9... | collective-permute-start | bytes 2359304 | tf_op jit(solution)/shard_map/ppermute | solution.py:129
  109.6 1.9 %collective-permute-start.10 = (bf16[192,2048]{1,0:T(8,128)(2,1)}, bf16[192,2048]{1,0:T(8,128)(2,1)}, u32[]{:S(2)}, u32[]{:S(2)}) collective-permute-start(bf16[192,2048]{1,0:T(8,128)(2,1)} %collective-permute-done.9), channel_id=1, source_target_pairs={{1,62},{2,63},{3,0},{0,1},{5,2},{6,3},{7,4},{4,5},{9,6},{10,7},{11... | collective-permute-start | bytes 2359304 | tf_op jit(solution)/shard_map/ppermute | solution.py:131
  112.7 6.5 %all-to-all-done.2 = bf16[4,128,2048]{2,1,0:T(8,128)(2,1)S(1)} async-done(((bf16[4,128,2048]{2,1,0:T(8,128)(2,1)}), bf16[4,128,2048]{2,1,0:T(8,128)(2,1)S(1)}, u32[]{:S(2)}, u32[]{:S(2)}) %all-to-all-start.2) | async-done | bytes 2097184 | tf_op jit(solution)/shard_map/all_to_all | solution.py:42
  120.5 5.5 %collective-permute-done.8 = bf16[192,2048]{1,0:T(8,128)(2,1)} collective-permute-done((bf16[192,2048]{1,0:T(8,128)(2,1)}, bf16[192,2048]{1,0:T(8,128)(2,1)}, u32[]{:S(2)}, u32[]{:S(2)}) %collective-permute-start.8) | collective-permute-done | bytes 786464 | tf_op jit(solution)/shard_map/ppermute | solution.py:129
  125.9 2.5 %add_convert_fusion.2 = bf16[192,2048]{1,0:T(8,128)(2,1)} fusion(bf16[192,2048]{1,0:T(8,128)(2,1)} %collective-permute-done.8, bf16[384,2048]{1,0:T(8,128)(2,1)} %copy-done.4), kind=kLoop, calls=%fused_computation.8 | loop fusion | flops 1572864 | bytes 2359296 | tf_op jit(solution)/shard_map/convert_element_type | solution.py:138
  128.5 2.5 %collective-permute-done.10 = bf16[192,2048]{1,0:T(8,128)(2,1)} collective-permute-done((bf16[192,2048]{1,0:T(8,128)(2,1)}, bf16[192,2048]{1,0:T(8,128)(2,1)}, u32[]{:S(2)}, u32[]{:S(2)}) %collective-permute-start.10) | collective-permute-done | bytes 786464 | tf_op jit(solution)/shard_map/ppermute | solution.py:131
  131.0 2.3 %fusion.5 = bf16[1,192,2048]{2,1,0:T(8,128)(2,1)} fusion(bf16[192,2048]{1,0:T(8,128)(2,1)} %collective-permute-done.10, bf16[192,2048]{1,0:T(8,128)(2,1)S(1)} %copy-done.1), kind=kLoop, calls=%fused_computation.18 | loop fusion | flops 1572864 | bytes 2359296 | tf_op jit(solution)/shard_map/broadcast_in_dim | solution.py:141
  (52 shorter events, 15.9 us)
Async XLA Ops:
  0.6 32.0 %collective-permute-start.1 = (bf16[192,2048]{1,0:T(8,128)(2,1)}, bf16[192,2048]{1,0:T(8,128)(2,1)S(1)}, u32[]{:S(2)}, u32[]{:S(2)}) collective-permute-start(bf16[192,2048]{1,0:T(8,128)(2,1)} %bitcast.45), channel_id=1, source_target_pairs={{0,1},{1,2},{2,3},{3,4},{4,5},{5,6},{6,7},{7,8},{8,9},{9,10},{10,1... | collective-permute-start | bytes 2359304 | tf_op jit(solution)/shard_map/ppermute | solution.py:53
  4.6 11.7 %copy-start.8 = (s32[2]{0:T(128)S(1)}, s32[2]{0:T(128)}, u32[]{:S(2)}) copy-start(s32[2]{0:T(128)} %param.15) | copy-start | bytes 28
  4.6 28.0 %collective-permute-start.2 = (bf16[192,2048]{1,0:T(8,128)(2,1)}, bf16[192,2048]{1,0:T(8,128)(2,1)}, u32[]{:S(2)}, u32[]{:S(2)}) collective-permute-start(bf16[192,2048]{1,0:T(8,128)(2,1)} %bitcast.39), channel_id=1, source_target_pairs={{0,3},{1,0},{2,1},{3,2},{4,7},{5,4},{6,5},{7,6},{8,11},{9,8},{10,9... | collective-permute-start | bytes 2359304 | tf_op jit(solution)/shard_map/ppermute | solution.py:54
  12.0 6.5 %copy-start.9 = (s32[2]{0:T(128)S(1)}, s32[2]{0:T(128)}, u32[]{:S(2)}) copy-start(s32[2]{0:T(128)} %param.14) | copy-start | bytes 28
  12.0 29.2 %all-to-all-start = ((bf16[4,128,2048]{2,1,0:T(8,128)(2,1)}), bf16[4,128,2048]{2,1,0:T(8,128)(2,1)S(1)}, u32[]{:S(2)}, u32[]{:S(2)}) async-start(bf16[4,128,2048]{2,1,0:T(8,128)(2,1)} %broadcast_in_dim.76), calls=%async_computation | async-start | bytes 4194304 | tf_op jit(solution)/shard_map/all_to_all | solution.py:42
  20.4 11.6 %collective-permute-start.3 = (s32[1]{0:T(128)}, s32[1]{0:T(128)}, u32[]{:S(2)}, u32[]{:S(2)}) collective-permute-start(s32[1]{0:T(128)} %param.13), channel_id=1, source_target_pairs={{0,63},{1,0},{2,1},{3,2},{4,3},{5,4},{6,5},{7,6},{8,7},{9,8},{10,9... | collective-permute-start | bytes 20 | tf_op jit(solution)/shard_map/ppermute | solution.py:56
  34.7 22.6 %collective-permute-start.4 = (bf16[192,2048]{1,0:T(8,128)(2,1)}, bf16[192,2048]{1,0:T(8,128)(2,1)}, u32[]{:S(2)}, u32[]{:S(2)}) collective-permute-start(bf16[192,2048]{1,0:T(8,128)(2,1)} %broadcast_select_fusion.3), channel_id=1, source_target_pairs={{0,1},{1,2},{2,3},{3,4},{4,5},{5,6},{6,7},{7,8},{8,9},{9,10},{10,1... | collective-permute-start | bytes 2359304 | tf_op jit(solution)/shard_map/ppermute | solution.py:64
  37.3 23.5 %collective-permute-start.5 = (bf16[192,2048]{1,0:T(8,128)(2,1)}, bf16[192,2048]{1,0:T(8,128)(2,1)}, u32[]{:S(2)}, u32[]{:S(2)}) collective-permute-start(bf16[192,2048]{1,0:T(8,128)(2,1)} %collective-permute-done.2), channel_id=1, source_target_pairs={{3,2},{0,3},{1,4},{2,5},{7,6},{4,7},{5,8},{6,9},{11,10},{8,11},{9,... | collective-permute-start | bytes 2359304 | tf_op jit(solution)/shard_map/ppermute | solution.py:63
  41.1 17.2 %all-to-all-start.1 = ((bf16[8,208,128]{2,1,0:T(8,128)(2,1)}), bf16[8,208,128]{2,1,0:T(8,128)(2,1)S(1)}, u32[]{:S(2)}, u32[]{:S(2)}) async-start(bf16[8,208,128]{2,1,0:T(8,128)(2,1)} %pad_maximum_fusion.3), calls=%async_computation.1 | async-start | bytes 851968 | tf_op jit(solution)/shard_map/all_to_all | solution.py:69
  46.9 6.2 %collective-permute-start = (bf16[512,2048]{1,0:T(8,128)(2,1)S(1)}, bf16[512,2048]{1,0:T(8,128)(2,1)}, u32[]{:S(2)}, u32[]{:S(2)}) collective-permute-start(bf16[512,2048]{1,0:T(8,128)(2,1)S(1)} %param.1), channel_id=1, source_target_pairs={{0,64},{64,0},{128,192},{192,128},{256,320},{320,256},{384,448},{4... | collective-permute-start | bytes 6291464 | tf_op jit(solution)/shard_map/cond/branch_1_fun/ppermute | solution.py:67
  58.5 4.2 %copy-start.5 = (bf16[1,192,2048]{2,1,0:T(8,128)(2,1)S(1)}, bf16[1,192,2048]{2,1,0:T(8,128)(2,1)}, u32[]{:S(2)}) copy-start(bf16[1,192,2048]{2,1,0:T(8,128)(2,1)} %param.12) | copy-start | bytes 2359300
  58.5 4.2 %copy-start.6 = (bf16[192,2048]{1,0:T(8,128)(2,1)S(1)}, bf16[192,2048]{1,0:T(8,128)(2,1)}, u32[]{:S(2)}) copy-start(bf16[192,2048]{1,0:T(8,128)(2,1)} %broadcast_select_fusion.6) | copy-start | bytes 2359300
  58.5 4.2 %copy-start.7 = (bf16[1,192,2048]{2,1,0:T(8,128)(2,1)S(1)}, bf16[1,192,2048]{2,1,0:T(8,128)(2,1)}, u32[]{:S(2)}) copy-start(bf16[1,192,2048]{2,1,0:T(8,128)(2,1)} %param.11) | copy-start | bytes 2359300
  60.8 6.4 %copy-start = (bf16[1024,2048]{1,0:T(8,128)(2,1)}, bf16[1024,2048]{1,0:T(8,128)(2,1)S(1)}, u32[]{:S(2)}) copy-start(bf16[1024,2048]{1,0:T(8,128)(2,1)S(1)} %pad_maximum_fusion) | copy-start | bytes 12582916
  67.2 3.3 %copy-start.2 = (bf16[384,1024]{1,0:T(8,128)(2,1)}, bf16[384,1024]{1,0:T(8,128)(2,1)S(1)}, u32[]{:S(2)}) copy-start(bf16[384,1024]{1,0:T(8,128)(2,1)S(1)} %get-tuple-element.66) | copy-start | bytes 2359300
  72.6 15.0 %collective-permute-start.7 = (bf16[512,2048]{1,0:T(8,128)(2,1)S(1)}, bf16[512,2048]{1,0:T(8,128)(2,1)S(1)}, u32[]{:S(2)}, u32[]{:S(2)}) collective-permute-start(bf16[512,2048]{1,0:T(8,128)(2,1)S(1)} %convolution_convert_fusion), channel_id=1, source_target_pairs={{0,64},{64,0},{128,192},{192,128},{256,320},{320,256},{384,448},{4... | collective-permute-start | bytes 6291464 | tf_op jit(solution)/shard_map/ppermute | solution.py:119
  78.3 22.7 %collective-permute-start.6 = (bf16[192,2048]{1,0:T(8,128)(2,1)}, bf16[192,2048]{1,0:T(8,128)(2,1)S(1)}, u32[]{:S(2)}, u32[]{:S(2)}) collective-permute-start(bf16[192,2048]{1,0:T(8,128)(2,1)} %get-tuple-element.61), channel_id=1, source_target_pairs={{0,63},{1,0},{2,1},{3,2},{4,3},{5,4},{6,5},{7,6},{8,7},{9,8},{10,9... | collective-permute-start | bytes 2359304 | tf_op jit(solution)/shard_map/ppermute | solution.py:110
  83.8 25.8 %collective-permute-start.9 = (bf16[192,2048]{1,0:T(8,128)(2,1)}, bf16[192,2048]{1,0:T(8,128)(2,1)}, u32[]{:S(2)}, u32[]{:S(2)}) collective-permute-start(bf16[192,2048]{1,0:T(8,128)(2,1)} %get-tuple-element.76), channel_id=1, source_target_pairs={{0,1},{1,2},{2,3},{3,0},{4,5},{5,6},{6,7},{7,4},{8,9},{9,10},{10,1... | collective-permute-start | bytes 2359304 | tf_op jit(solution)/shard_map/ppermute | solution.py:111
  89.8 29.3 %all-to-all-start.2 = ((bf16[4,128,2048]{2,1,0:T(8,128)(2,1)}), bf16[4,128,2048]{2,1,0:T(8,128)(2,1)S(1)}, u32[]{:S(2)}, u32[]{:S(2)}) async-start(bf16[4,128,2048]{2,1,0:T(8,128)(2,1)} %bitcast.36), calls=%async_computation.2 | async-start | bytes 4194304 | tf_op jit(solution)/shard_map/all_to_all | solution.py:42
  93.6 7.5 %copy-start.3 = (bf16[192,2048]{1,0:T(8,128)(2,1)S(1)}, bf16[192,2048]{1,0:T(8,128)(2,1)}, u32[]{:S(2)}) copy-start(bf16[192,2048]{1,0:T(8,128)(2,1)} %get-tuple-element.60) | copy-start | bytes 2359300
  97.9 13.6 %copy-start.4 = (bf16[384,2048]{1,0:T(8,128)(2,1)}, bf16[384,2048]{1,0:T(8,128)(2,1)S(1)}, u32[]{:S(2)}) copy-start(bf16[384,2048]{1,0:T(8,128)(2,1)S(1)} %convolution_convert_fusion.1) | copy-start | bytes 4718596
  102.2 23.7 %collective-permute-start.8 = (bf16[192,2048]{1,0:T(8,128)(2,1)}, bf16[192,2048]{1,0:T(8,128)(2,1)}, u32[]{:S(2)}, u32[]{:S(2)}) collective-permute-start(bf16[192,2048]{1,0:T(8,128)(2,1)} %add_convert_fusion.4), channel_id=1, source_target_pairs={{0,63},{1,0},{2,1},{3,2},{4,3},{5,4},{6,5},{7,6},{8,7},{9,8},{10,9... | collective-permute-start | bytes 2359304 | tf_op jit(solution)/shard_map/ppermute | solution.py:129
  109.6 21.4 %collective-permute-start.10 = (bf16[192,2048]{1,0:T(8,128)(2,1)}, bf16[192,2048]{1,0:T(8,128)(2,1)}, u32[]{:S(2)}, u32[]{:S(2)}) collective-permute-start(bf16[192,2048]{1,0:T(8,128)(2,1)} %collective-permute-done.9), channel_id=1, source_target_pairs={{1,62},{2,63},{3,0},{0,1},{5,2},{6,3},{7,4},{4,5},{9,6},{10,7},{11... | collective-permute-start | bytes 2359304 | tf_op jit(solution)/shard_map/ppermute | solution.py:131
  112.7 18.3 %copy-start.1 = (bf16[192,2048]{1,0:T(8,128)(2,1)S(1)}, bf16[192,2048]{1,0:T(8,128)(2,1)}, u32[]{:S(2)}) copy-start(bf16[192,2048]{1,0:T(8,128)(2,1)} %add_convert_fusion.3) | copy-start | bytes 2359300
